TPU v7x, 512 devices: a whole 4x8x8 slice. The times are simulated.
512 devices in a mesh: sec: 4 (over x_hi, core), gx: 16 (over x_lo, z), gy: 8 (over y).
Axes of the slice: x: 4 (x_hi: 2, x_lo: 2; x = x_hi * 2 + x_lo), y: 8, z: 8, core: 2. Of those that a mesh axis runs over, the one named last changes fastest.
Arguments:
- profile: bfloat16 [4, 128, 512, 1024], P('sec', None, 'gx', 'gy'), may hold values from -6 to 6
- surface: float32 [4, 512, 1024], P('sec', 'gx', 'gy'), may hold values from -6 to 6
- diffusion: float32 [4, 512, 1024], P('sec', 'gx', 'gy'), may hold values from 0.05 to 0.24
- sea_mask: int32 [4, 512, 1024], P('sec', 'gx', 'gy'), may hold values 0 or 1
- convective: int32 [4, 512, 1024], P('sec', 'gx', 'gy'), may hold values from 0 to 1, as said below
- mixing: bfloat16 [4, 2, 128, 128], P('sec'), may hold values from -0.5 to 0.5
- remap_weights: bfloat16 [4, 16, 8, 32, 2, 128, 128], P('sec', 'gx', 'gy'), may hold values from -0.375 to 0.375
- sources: int32 [4, 16, 8, 32, 2], P('sec', 'gx', 'gy'), may hold values from 0 to 127, as said below
- send_lists: int32 [4, 16, 8, 64, 2], P('sec', 'gx', 'gy'), may hold values from 0 to 31
Outputs:
- column_state: bfloat16 [4, 128, 512, 1024], P('sec', None, 'gx', 'gy')
- surface_state: float32 [4, 512, 1024], P('sec', 'gx', 'gy')
Inputs may be any that keep to these rules, and one draw needn't show every extreme that they name: sources[s, i, j, a, k] = e * 2 + c names slot c from sender e = s2 * 16 + i2 at the same j; for s below 3 the sender has s2 = 3, for s = 3 it has s2 below 3. `convective`: each device holds 64 to 1024 columns with 1, and some device exactly 1024.
All inputs are finite; a program needn't handle non-finite values. No bound on the sum of `sea_mask` on one device may be relied on, other than what follows from the above.
Results may differ from a plain program's by a relative error of at most 0.0074.
Values may be sent and summed in bfloat16 or wider, within the bound.
No kernel may reach another device: no remote copies, remote signals or barrier semaphores. Data moves between devices by JAX's collectives and lax.ppermute only.
A program may use at most 64 MiB of HBM per device.

v0:
```python
import jax
import jax.numpy as jnp
from jax import lax
from jax.sharding import PartitionSpec as P

STEPS = 2
PHYS = 4
PASSES = 4


def padded_2(cells, sides, width):
    for axis, dim in sides:
        count = lax.axis_size(axis)
        ends = count - 1
        head = lax.slice_in_dim(cells, 0, width, axis=dim)
        tail = lax.slice_in_dim(cells, cells.shape[dim] - width, cells.shape[dim], axis=dim)
        cells = jnp.concatenate(
            [
                lax.ppermute(tail, axis, [(i, (i + 1) % count) for i in range(ends)]),
                cells,
                lax.ppermute(head, axis, [((i + 1) % count, i) for i in range(ends)]),
            ],
            axis=dim,
        )
    return cells


def body(
    profile, surface, diffusion, sea_mask, convective, mixing, remap_weights, sources, send_lists
):
    levels = profile.shape[1]
    grid_rows = profile.shape[2]
    grid_cols = profile.shape[3]
    cell_count = grid_rows * grid_cols
    tile_size = remap_weights.shape[-1]
    column_state = profile.reshape(levels, cell_count)
    start_surface = surface.reshape(grid_rows, grid_cols)
    surface_state = start_surface
    coefficient = diffusion.reshape(grid_rows, grid_cols)
    sea_float = sea_mask.reshape(grid_rows, grid_cols).astype(jnp.float32)
    deep_flags = convective.reshape(cell_count) == 1
    matrices = mixing.reshape(2, levels, levels)
    weights = remap_weights.reshape(remap_weights.shape[3:])
    wanted = sources.reshape(sources.shape[3:])
    lists = send_lists.reshape(send_lists.shape[3:])
    senders = lists.shape[0]
    slot_count = lists.shape[1]
    own_index = lax.axis_index(("sec", "gx"))
    sec_count = lax.axis_size("sec")
    sec_index = lax.axis_index("sec")
    ocean_side = sec_index == sec_count - 1

    def advance(state):
        for substep in range(PHYS):
            plain_mix = jnp.dot(matrices[0], state, preferred_element_type=jnp.float32)
            deep_mix = jnp.dot(matrices[1], state, preferred_element_type=jnp.float32)
            mixed = jnp.where(deep_flags, deep_mix, plain_mix)
            state = (0.5 * state.astype(jnp.float32) + jnp.tanh(mixed)).astype(jnp.bfloat16)
        return state

    def unchanged(state):
        return state

    for coupled in range(STEPS):
        lowest = column_state[0]
        tiles = lowest.reshape(cell_count // tile_size, tile_size)
        piece_tiles = lax.all_gather(tiles[None], ("sec", "gx"), axis=0, tiled=True)
        piece_lists = lax.all_gather(lists[None], ("sec", "gx"), axis=0, tiled=True)
        rows_sel = piece_lists[:, own_index, :]
        values = jnp.take_along_axis(piece_tiles, rows_sel[:, :, None], axis=1)
        picked = values.reshape(senders * slot_count, tile_size)[wanted]
        imported = jnp.einsum("akij,akj->ai", weights, picked, preferred_element_type=jnp.float32)
        flux = sea_float * (imported - lowest.reshape(grid_rows, grid_cols).astype(jnp.float32))
        forcing = flux / PASSES
        for sweep in range(PASSES):
            padded = padded_2(surface_state, (("gx", 0), ("gy", 1)), 1)
            beside_all = padded[2:, 1:-1] + padded[:-2, 1:-1]
            beside_all = beside_all + padded[1:-1, 2:] + padded[1:-1, :-2]
            surface_state = sea_float * (
                surface_state + coefficient * (beside_all - 4.0 * surface_state) + forcing
            )
        bottom = (lowest.astype(jnp.float32) + flux.reshape(cell_count)).astype(jnp.bfloat16)
        forced = column_state.at[0].set(bottom)
        column_state = lax.cond(ocean_side, unchanged, advance, forced)
        column_state = jnp.where(ocean_side, column_state.at[0].set(lowest), column_state)
    surface_out = jnp.where(ocean_side, surface_state, start_surface)
    return (column_state.reshape(profile.shape), surface_out.reshape(surface.shape))


def solution(mesh):
    return jax.shard_map(
        body,
        mesh=mesh,
        in_specs=(
            P("sec", None, "gx", "gy"),
            P("sec", "gx", "gy"),
            P("sec", "gx", "gy"),
            P("sec", "gx", "gy"),
            P("sec", "gx", "gy"),
            P("sec", None, None, None),
            P("sec", "gx", "gy", None, None, None, None),
            P("sec", "gx", "gy", None, None),
            P("sec", "gx", "gy", None, None),
        ),
        out_specs=(P("sec", None, "gx", "gy"), P("sec", "gx", "gy")),
        check_vma=False,
    )
```

profile of v0, /device:TPU:2, one launch (start us, length us, event | category | flops | bytes accessed | tf_op | source)
XLA Modules:
  0.0 537.8 jit_solution(15609668887644981467)
XLA Ops:
  1.5 10.9 %collective-permute-start = (f32[1,128]{1,0:T(1,128)S(1)}, f32[1,128]{1,0:T(1,128)S(1)}, u32[]{:S(2)}, u32[]{:S(2)}) collective-permute-start(f32[1,128]{1,0:T(1,128)S(1)} %get-tuple-element.124), channel_id=1, source_target_pairs={{8,0},{16,8},{24,16},{32,24},{40,32},{48,40},{56,48},{64,56},{72,6... | collective-permute-start | bytes 1544 | tf_op jit(solution)/shard_map/ppermute | solution.py:21
  14.4 120.6 %all-gather.1 = s32[64,1,1,64,2]{3,4,2,1,0:T(2,128)S(1)} all-gather(s32[1,1,1,64,2]{3,4,2,1,0:T(2,128)} %param.31), channel_id=3, replica_groups=mesh['sec'=4,'gx'=16,'gy'=8] {'sec','gx'}, dimensions={0}, use_global_device_ids=true | all-gather | bytes 33280 | tf_op jit(solution)/shard_map/all_gather | solution.py:68
  135.9 118.8 %all-gather = bf16[64,1,32,128]{3,2,1,0:T(8,128)(2,1)S(1)} all-gather(bf16[1,1,32,128]{3,2,1,0:T(8,128)(2,1)S(1)} %get-tuple-element.92), channel_id=2, replica_groups=mesh['sec'=4,'gx'=16,'gy'=8] {'sec','gx'}, dimensions={0}, use_global_device_ids=true | all-gather | bytes 532480 | tf_op jit(solution)/shard_map/all_gather | solution.py:67
  258.7 3.5 collective-permute-start.3
  265.0 2.9 collective-permute-done.2
  268.0 6.2 %collective-permute-start.4 = (f32[1,128]{1,0:T(1,128)S(1)}, f32[1,128]{1,0:T(1,128)S(1)}, u32[]{:S(2)}, u32[]{:S(2)}) collective-permute-start(f32[1,128]{1,0:T(1,128)S(1)} %get-tuple-element.122), channel_id=1, source_target_pairs={{8,0},{16,8},{24,16},{32,24},{40,32},{48,40},{56,48},{64,56},{72,6... | collective-permute-start | bytes 1544 | tf_op jit(solution)/shard_map/ppermute | solution.py:21
  277.7 4.1 collective-permute-done.5
  281.8 3.5 collective-permute-start.7
  286.6 9.0 %conditional.2 = (bf16[128,4096]{1,0:T(8,128)(2,1)}, bf16[1,4096]{1,0:T(2,128)(2,1)S(1)}) conditional(s32[]{:T(128)} %convert_element_type.94, (bf16[128,4096]{1,0:T(8,128)(2,1)}, pred[4096]{0:T(1024)(128)(4,1)S(1)}, bf16[2,128,128]{2,1,0:T(8,128)(2,1)S(1)}) %tuple.72, bf16[128,4096]{1,0:T(8,128)(2,1)} %scatter.13), branch_computations={%region_0.2_spmd, %region_1.0_spmd} | conditional | flops 1084227584 | bytes 33849360 | solution.py:84
  298.0 3.6 collective-permute-start.9
  301.6 3.9 collective-permute-done.9
  305.6 4.9 collective-permute-start.11
  312.0 5.4 %collective-permute-done.10 = f32[34,1]{1,0:T(8,128)S(1)} collective-permute-done((f32[34,1]{1,0:T(8,128)S(1)}, f32[34,1]{1,0:T(8,128)S(1)}, u32[]{:S(2)}, u32[]{:S(2)}) %collective-permute-start.10) | collective-permute-done | bytes 168 | tf_op jit(solution)/shard_map/ppermute | solution.py:21
  319.8 3.6 collective-permute-start.13
  323.4 121.3 %all_gather.12 = bf16[64,32,128]{2,1,0:T(8,128)(2,1)S(1)} all-gather(bf16[1,32,128]{2,1,0:T(8,128)(2,1)S(1)} %bitcast.203), channel_id=1, replica_groups=mesh['sec'=4,'gx'=16,'gy'=8] {'sec','gx'}, dimensions={0}, use_global_device_ids=true | all-gather | bytes 532480 | tf_op jit(solution)/shard_map/all_gather | solution.py:67
  444.8 3.9 collective-permute-start.15
  451.1 3.2 collective-permute-done.14
  456.4 3.9 collective-permute-start.17
  461.1 2.8 collective-permute-done.17
  464.0 4.3 collective-permute-start.19
  470.3 3.7 collective-permute-done.18
  476.1 3.9 collective-permute-start.21
  480.0 3.6 collective-permute-done.21
  483.7 3.9 collective-permute-start.23
  490.4 2.8 collective-permute-done.22
  495.3 3.9 collective-permute-start.25
  502.9 3.1 collective-permute-start.27
  507.4 9.1 %conditional.3 = (bf16[128,4096]{1,0:T(8,128)(2,1)}, bf16[1,4096]{1,0:T(2,128)(2,1)S(1)}) conditional(s32[]{:T(128)} %convert_element_type.94, (bf16[128,4096]{1,0:T(8,128)(2,1)}, pred[4096]{0:T(1024)(128)(4,1)S(1)}, bf16[2,128,128]{2,1,0:T(8,128)(2,1)S(1)}) %tuple.73, bf16[128,4096]{1,0:T(8,128)(2,1)} %scatter.16), branch_computations={%region_2.4_spmd, %region_3.5_spmd} | conditional | flops 1084227584 | bytes 33849360 | solution.py:84
  516.7 2.6 collective-permute-start.28
  519.2 3.3 collective-permute-start.29
  524.1 2.7 collective-permute-done.29
  526.9 4.5 collective-permute-start.31
  (133 shorter events, 66.8 us)
Async XLA Ops:
  1.5 257.1 %collective-permute-start = (f32[1,128]{1,0:T(1,128)S(1)}, f32[1,128]{1,0:T(1,128)S(1)}, u32[]{:S(2)}, u32[]{:S(2)}) collective-permute-start(f32[1,128]{1,0:T(1,128)S(1)} %get-tuple-element.124), channel_id=1, source_target_pairs={{8,0},{16,8},{24,16},{32,24},{40,32},{48,40},{56,48},{64,56},{72,6... | collective-permute-start | bytes 1544 | tf_op jit(solution)/shard_map/ppermute | solution.py:21
  12.4 246.2 %collective-permute-start.1 = (f32[1,128]{1,0:T(1,128)S(1)}, f32[1,128]{1,0:T(1,128)S(1)}, u32[]{:S(2)}, u32[]{:S(2)}) collective-permute-start(f32[1,128]{1,0:T(1,128)S(1)} %get-tuple-element.123), channel_id=1, source_target_pairs={{0,8},{8,16},{16,24},{24,32},{32,40},{40,48},{48,56},{56,64},{64,7... | collective-permute-start | bytes 1544 | tf_op jit(solution)/shard_map/ppermute | solution.py:19
  258.7 6.2 %collective-permute-start.3 = (f32[34,1]{1,0:T(8,128)S(1)}, f32[34,1]{1,0:T(8,128)S(1)}, u32[]{:S(2)}, u32[]{:S(2)}) collective-permute-start(f32[34,1]{1,0:T(8,128)S(1)} %get-tuple-element.108), channel_id=1, source_target_pairs={{0,1},{1,2},{2,3},{3,4},{4,5},{5,6},{6,7},{8,9},{9,10},{10,11},{11... | collective-permute-start | bytes 416 | tf_op jit(solution)/shard_map/ppermute | solution.py:19
  262.2 5.7 %collective-permute-start.2 = (f32[34,1]{1,0:T(8,128)S(1)}, f32[34,1]{1,0:T(8,128)S(1)}, u32[]{:S(2)}, u32[]{:S(2)}) collective-permute-start(f32[34,1]{1,0:T(8,128)S(1)} %get-tuple-element.107), channel_id=1, source_target_pairs={{1,0},{2,1},{3,2},{4,3},{5,4},{6,5},{7,6},{9,8},{10,9},{11,10},{12... | collective-permute-start | bytes 416 | tf_op jit(solution)/shard_map/ppermute | solution.py:21
  268.0 9.7 %collective-permute-start.4 = (f32[1,128]{1,0:T(1,128)S(1)}, f32[1,128]{1,0:T(1,128)S(1)}, u32[]{:S(2)}, u32[]{:S(2)}) collective-permute-start(f32[1,128]{1,0:T(1,128)S(1)} %get-tuple-element.122), channel_id=1, source_target_pairs={{8,0},{16,8},{24,16},{32,24},{40,32},{48,40},{56,48},{64,56},{72,6... | collective-permute-start | bytes 1544 | tf_op jit(solution)/shard_map/ppermute | solution.py:21
  274.2 7.5 %collective-permute-start.5 = (f32[1,128]{1,0:T(1,128)S(1)}, f32[1,128]{1,0:T(1,128)S(1)}, u32[]{:S(2)}, u32[]{:S(2)}) collective-permute-start(f32[1,128]{1,0:T(1,128)S(1)} %get-tuple-element.121), channel_id=1, source_target_pairs={{0,8},{8,16},{16,24},{24,32},{32,40},{40,48},{48,56},{56,64},{64,7... | collective-permute-start | bytes 1544 | tf_op jit(solution)/shard_map/ppermute | solution.py:19
  281.8 13.8 %collective-permute-start.7 = (f32[34,1]{1,0:T(8,128)S(1)}, f32[34,1]{1,0:T(8,128)S(1)}, u32[]{:S(2)}, u32[]{:S(2)}) collective-permute-start(f32[34,1]{1,0:T(8,128)S(1)} %get-tuple-element.106), channel_id=1, source_target_pairs={{0,1},{1,2},{2,3},{3,4},{4,5},{5,6},{6,7},{8,9},{9,10},{10,11},{11... | collective-permute-start | bytes 416 | tf_op jit(solution)/shard_map/ppermute | solution.py:19
  285.3 10.3 %collective-permute-start.6 = (f32[34,1]{1,0:T(8,128)S(1)}, f32[34,1]{1,0:T(8,128)S(1)}, u32[]{:S(2)}, u32[]{:S(2)}) collective-permute-start(f32[34,1]{1,0:T(8,128)S(1)} %get-tuple-element.105), channel_id=1, source_target_pairs={{1,0},{2,1},{3,2},{4,3},{5,4},{6,5},{7,6},{9,8},{10,9},{11,10},{12... | collective-permute-start | bytes 416 | tf_op jit(solution)/shard_map/ppermute | solution.py:21
  295.7 5.9 %collective-permute-start.8 = (f32[1,128]{1,0:T(1,128)S(1)}, f32[1,128]{1,0:T(1,128)S(1)}, u32[]{:S(2)}, u32[]{:S(2)}) collective-permute-start(f32[1,128]{1,0:T(1,128)S(1)} %get-tuple-element.120), channel_id=1, source_target_pairs={{8,0},{16,8},{24,16},{32,24},{40,32},{48,40},{56,48},{64,56},{72,6... | collective-permute-start | bytes 1544 | tf_op jit(solution)/shard_map/ppermute | solution.py:21
  298.0 7.5 %collective-permute-start.9 = (f32[1,128]{1,0:T(1,128)S(1)}, f32[1,128]{1,0:T(1,128)S(1)}, u32[]{:S(2)}, u32[]{:S(2)}) collective-permute-start(f32[1,128]{1,0:T(1,128)S(1)} %get-tuple-element.119), channel_id=1, source_target_pairs={{0,8},{8,16},{16,24},{24,32},{32,40},{40,48},{48,56},{56,64},{64,7... | collective-permute-start | bytes 1544 | tf_op jit(solution)/shard_map/ppermute | solution.py:19
  305.6 6.3 %collective-permute-start.11 = (f32[34,1]{1,0:T(8,128)S(1)}, f32[34,1]{1,0:T(8,128)S(1)}, u32[]{:S(2)}, u32[]{:S(2)}) collective-permute-start(f32[34,1]{1,0:T(8,128)S(1)} %get-tuple-element.104), channel_id=1, source_target_pairs={{0,1},{1,2},{2,3},{3,4},{4,5},{5,6},{6,7},{8,9},{9,10},{10,11},{11... | collective-permute-start | bytes 416 | tf_op jit(solution)/shard_map/ppermute | solution.py:19
  310.5 6.9 %collective-permute-start.10 = (f32[34,1]{1,0:T(8,128)S(1)}, f32[34,1]{1,0:T(8,128)S(1)}, u32[]{:S(2)}, u32[]{:S(2)}) collective-permute-start(f32[34,1]{1,0:T(8,128)S(1)} %get-tuple-element.103), channel_id=1, source_target_pairs={{1,0},{2,1},{3,2},{4,3},{5,4},{6,5},{7,6},{9,8},{10,9},{11,10},{12... | collective-permute-start | bytes 416 | tf_op jit(solution)/shard_map/ppermute | solution.py:21
  317.5 127.1 %collective-permute-start.12 = (f32[1,128]{1,0:T(1,128)S(1)}, f32[1,128]{1,0:T(1,128)S(1)}, u32[]{:S(2)}, u32[]{:S(2)}) collective-permute-start(f32[1,128]{1,0:T(1,128)S(1)} %get-tuple-element.118), channel_id=1, source_target_pairs={{8,0},{16,8},{24,16},{32,24},{40,32},{48,40},{56,48},{64,56},{72,6... | collective-permute-start | bytes 1544 | tf_op jit(solution)/shard_map/ppermute | solution.py:21
  319.8 124.9 %collective-permute-start.13 = (f32[1,128]{1,0:T(1,128)S(1)}, f32[1,128]{1,0:T(1,128)S(1)}, u32[]{:S(2)}, u32[]{:S(2)}) collective-permute-start(f32[1,128]{1,0:T(1,128)S(1)} %get-tuple-element.117), channel_id=1, source_target_pairs={{0,8},{8,16},{16,24},{24,32},{32,40},{40,48},{48,56},{56,64},{64,7... | collective-permute-start | bytes 1544 | tf_op jit(solution)/shard_map/ppermute | solution.py:19
  444.8 6.3 %collective-permute-start.15 = (f32[34,1]{1,0:T(8,128)S(1)}, f32[34,1]{1,0:T(8,128)S(1)}, u32[]{:S(2)}, u32[]{:S(2)}) collective-permute-start(f32[34,1]{1,0:T(8,128)S(1)} %get-tuple-element.102), channel_id=1, source_target_pairs={{0,1},{1,2},{2,3},{3,4},{4,5},{5,6},{6,7},{8,9},{9,10},{10,11},{11... | collective-permute-start | bytes 416 | tf_op jit(solution)/shard_map/ppermute | solution.py:19
  448.7 5.7 %collective-permute-start.14 = (f32[34,1]{1,0:T(8,128)S(1)}, f32[34,1]{1,0:T(8,128)S(1)}, u32[]{:S(2)}, u32[]{:S(2)}) collective-permute-start(f32[34,1]{1,0:T(8,128)S(1)} %get-tuple-element.101), channel_id=1, source_target_pairs={{1,0},{2,1},{3,2},{4,3},{5,4},{6,5},{7,6},{9,8},{10,9},{11,10},{12... | collective-permute-start | bytes 416 | tf_op jit(solution)/shard_map/ppermute | solution.py:21
  454.5 6.6 %collective-permute-start.16 = (f32[1,128]{1,0:T(1,128)S(1)}, f32[1,128]{1,0:T(1,128)S(1)}, u32[]{:S(2)}, u32[]{:S(2)}) collective-permute-start(f32[1,128]{1,0:T(1,128)S(1)} %get-tuple-element.116), channel_id=1, source_target_pairs={{8,0},{16,8},{24,16},{32,24},{40,32},{48,40},{56,48},{64,56},{72,6... | collective-permute-start | bytes 1544 | tf_op jit(solution)/shard_map/ppermute | solution.py:21
  456.4 7.5 %collective-permute-start.17 = (f32[1,128]{1,0:T(1,128)S(1)}, f32[1,128]{1,0:T(1,128)S(1)}, u32[]{:S(2)}, u32[]{:S(2)}) collective-permute-start(f32[1,128]{1,0:T(1,128)S(1)} %get-tuple-element.115), channel_id=1, source_target_pairs={{0,8},{8,16},{16,24},{24,32},{32,40},{40,48},{48,56},{56,64},{64,7... | collective-permute-start | bytes 1544 | tf_op jit(solution)/shard_map/ppermute | solution.py:19
  464.0 6.3 %collective-permute-start.19 = (f32[34,1]{1,0:T(8,128)S(1)}, f32[34,1]{1,0:T(8,128)S(1)}, u32[]{:S(2)}, u32[]{:S(2)}) collective-permute-start(f32[34,1]{1,0:T(8,128)S(1)} %get-tuple-element.100), channel_id=1, source_target_pairs={{0,1},{1,2},{2,3},{3,4},{4,5},{5,6},{6,7},{8,9},{9,10},{10,11},{11... | collective-permute-start | bytes 416 | tf_op jit(solution)/shard_map/ppermute | solution.py:19
  468.4 5.7 %collective-permute-start.18 = (f32[34,1]{1,0:T(8,128)S(1)}, f32[34,1]{1,0:T(8,128)S(1)}, u32[]{:S(2)}, u32[]{:S(2)}) collective-permute-start(f32[34,1]{1,0:T(8,128)S(1)} %get-tuple-element.99), channel_id=1, source_target_pairs={{1,0},{2,1},{3,2},{4,3},{5,4},{6,5},{7,6},{9,8},{10,9},{11,10},{12... | collective-permute-start | bytes 416 | tf_op jit(solution)/shard_map/ppermute | solution.py:21
  474.1 5.9 %collective-permute-start.20 = (f32[1,128]{1,0:T(1,128)S(1)}, f32[1,128]{1,0:T(1,128)S(1)}, u32[]{:S(2)}, u32[]{:S(2)}) collective-permute-start(f32[1,128]{1,0:T(1,128)S(1)} %get-tuple-element.114), channel_id=1, source_target_pairs={{8,0},{16,8},{24,16},{32,24},{40,32},{48,40},{56,48},{64,56},{72,6... | collective-permute-start | bytes 1544 | tf_op jit(solution)/shard_map/ppermute | solution.py:21
  476.1 7.5 %collective-permute-start.21 = (f32[1,128]{1,0:T(1,128)S(1)}, f32[1,128]{1,0:T(1,128)S(1)}, u32[]{:S(2)}, u32[]{:S(2)}) collective-permute-start(f32[1,128]{1,0:T(1,128)S(1)} %get-tuple-element.113), channel_id=1, source_target_pairs={{0,8},{8,16},{16,24},{24,32},{32,40},{40,48},{48,56},{56,64},{64,7... | collective-permute-start | bytes 1544 | tf_op jit(solution)/shard_map/ppermute | solution.py:19
  483.7 6.8 %collective-permute-start.23 = (f32[34,1]{1,0:T(8,128)S(1)}, f32[34,1]{1,0:T(8,128)S(1)}, u32[]{:S(2)}, u32[]{:S(2)}) collective-permute-start(f32[34,1]{1,0:T(8,128)S(1)} %get-tuple-element.98), channel_id=1, source_target_pairs={{0,1},{1,2},{2,3},{3,4},{4,5},{5,6},{6,7},{8,9},{9,10},{10,11},{11... | collective-permute-start | bytes 416 | tf_op jit(solution)/shard_map/ppermute | solution.py:19
  487.6 5.7 %collective-permute-start.22 = (f32[34,1]{1,0:T(8,128)S(1)}, f32[34,1]{1,0:T(8,128)S(1)}, u32[]{:S(2)}, u32[]{:S(2)}) collective-permute-start(f32[34,1]{1,0:T(8,128)S(1)} %get-tuple-element.97), channel_id=1, source_target_pairs={{1,0},{2,1},{3,2},{4,3},{5,4},{6,5},{7,6},{9,8},{10,9},{11,10},{12... | collective-permute-start | bytes 416 | tf_op jit(solution)/shard_map/ppermute | solution.py:21
  493.4 7.4 %collective-permute-start.24 = (f32[1,128]{1,0:T(1,128)S(1)}, f32[1,128]{1,0:T(1,128)S(1)}, u32[]{:S(2)}, u32[]{:S(2)}) collective-permute-start(f32[1,128]{1,0:T(1,128)S(1)} %get-tuple-element.112), channel_id=1, source_target_pairs={{8,0},{16,8},{24,16},{32,24},{40,32},{48,40},{56,48},{64,56},{72,6... | collective-permute-start | bytes 1544 | tf_op jit(solution)/shard_map/ppermute | solution.py:21
  495.3 7.5 %collective-permute-start.25 = (f32[1,128]{1,0:T(1,128)S(1)}, f32[1,128]{1,0:T(1,128)S(1)}, u32[]{:S(2)}, u32[]{:S(2)}) collective-permute-start(f32[1,128]{1,0:T(1,128)S(1)} %get-tuple-element.111), channel_id=1, source_target_pairs={{0,8},{8,16},{16,24},{24,32},{32,40},{40,48},{48,56},{56,64},{64,7... | collective-permute-start | bytes 1544 | tf_op jit(solution)/shard_map/ppermute | solution.py:19
  502.9 13.6 %collective-permute-start.27 = (f32[34,1]{1,0:T(8,128)S(1)}, f32[34,1]{1,0:T(8,128)S(1)}, u32[]{:S(2)}, u32[]{:S(2)}) collective-permute-start(f32[34,1]{1,0:T(8,128)S(1)} %get-tuple-element.96), channel_id=1, source_target_pairs={{0,1},{1,2},{2,3},{3,4},{4,5},{5,6},{6,7},{8,9},{9,10},{10,11},{11... | collective-permute-start | bytes 416 | tf_op jit(solution)/shard_map/ppermute | solution.py:19
  506.1 10.5 %collective-permute-start.26 = (f32[34,1]{1,0:T(8,128)S(1)}, f32[34,1]{1,0:T(8,128)S(1)}, u32[]{:S(2)}, u32[]{:S(2)}) collective-permute-start(f32[34,1]{1,0:T(8,128)S(1)} %get-tuple-element.95), channel_id=1, source_target_pairs={{1,0},{2,1},{3,2},{4,3},{5,4},{6,5},{7,6},{9,8},{10,9},{11,10},{12... | collective-permute-start | bytes 416 | tf_op jit(solution)/shard_map/ppermute | solution.py:21
  516.7 7.4 %collective-permute-start.28 = (f32[1,128]{1,0:T(1,128)S(1)}, f32[1,128]{1,0:T(1,128)S(1)}, u32[]{:S(2)}, u32[]{:S(2)}) collective-permute-start(f32[1,128]{1,0:T(1,128)S(1)} %get-tuple-element.110), channel_id=1, source_target_pairs={{8,0},{16,8},{24,16},{32,24},{40,32},{48,40},{56,48},{64,56},{72,6... | collective-permute-start | bytes 1544 | tf_op jit(solution)/shard_map/ppermute | solution.py:21
  519.2 7.5 %collective-permute-start.29 = (f32[1,128]{1,0:T(1,128)S(1)}, f32[1,128]{1,0:T(1,128)S(1)}, u32[]{:S(2)}, u32[]{:S(2)}) collective-permute-start(f32[1,128]{1,0:T(1,128)S(1)} %get-tuple-element.109), channel_id=1, source_target_pairs={{0,8},{8,16},{16,24},{24,32},{32,40},{40,48},{48,56},{56,64},{64,7... | collective-permute-start | bytes 1544 | tf_op jit(solution)/shard_map/ppermute | solution.py:19
  526.9 8.3 %collective-permute-start.31 = (f32[34,1]{1,0:T(8,128)S(1)}, f32[34,1]{1,0:T(8,128)S(1)}, u32[]{:S(2)}, u32[]{:S(2)}) collective-permute-start(f32[34,1]{1,0:T(8,128)S(1)} %get-tuple-element.94), channel_id=1, source_target_pairs={{0,1},{1,2},{2,3},{3,4},{4,5},{5,6},{6,7},{8,9},{9,10},{10,11},{11... | collective-permute-start | bytes 416 | tf_op jit(solution)/shard_map/ppermute | solution.py:19
  531.4 5.7 %collective-permute-start.30 = (f32[34,1]{1,0:T(8,128)S(1)}, f32[34,1]{1,0:T(8,128)S(1)}, u32[]{:S(2)}, u32[]{:S(2)}) collective-permute-start(f32[34,1]{1,0:T(8,128)S(1)} %get-tuple-element.93), channel_id=1, source_target_pairs={{1,0},{2,1},{3,2},{4,3},{5,4},{6,5},{7,6},{9,8},{10,9},{11,10},{12... | collective-permute-start | bytes 416 | tf_op jit(solution)/shard_map/ppermute | solution.py:21
  (7 other events, 827.0 us)
where the time goes:
time: 539 us; the launch traced here: 538 us
  blocking collectives  361 us (67%)
  starting transfers between devices  98 us (18%)
  waiting for transfers between devices  39.4 us (7%)
  local copies, waits for them, and re-layouts  18.2 us (3%)
  matrix products  17.4 us (3%)
    all_gather x2, blocking collectives, body(): piece_tiles = lax.all_gather(tiles[None], ('sec', 'gx'), axis=0, tiled=True)  240 us
    all_gather x1, blocking collectives, body(): piece_lists = lax.all_gather(lists[None], ('sec', 'gx'), axis=0, tiled=True)  121 us
    ppermute x16, starting transfers between devices, padded_2(): lax.ppermute(tail, axis, [(i, (i + 1) % count) for i in range(ends)])  57.7 us
    ppermute x16, starting transfers between devices, padded_2(): lax.ppermute(head, axis, [((i + 1) % count, i) for i in range(ends)])  40.3 us
    ppermute x16, waiting for transfers between devices, padded_2(): lax.ppermute(head, axis, [((i + 1) % count, i) for i in range(ends)])  20.1 us
    ppermute x16, waiting for transfers between devices, padded_2(): lax.ppermute(tail, axis, [(i, (i + 1) % count) for i in range(ends)])  19.3 us
  transfers between devices with their start and end apart: 32, of which 13 were waited for; matrix products, arithmetic and copies ran while one was open for 7% of the time, Pallas kernels for 0%

commit v1 on v0

v1 whole, which is shorter than its diff:
```python
import jax
import jax.numpy as jnp
from jax import lax
from jax.sharding import PartitionSpec as P

STEPS = 2
PHYS = 4
PASSES = 4
HALO = 4


def body(
    profile, surface, diffusion, sea_mask, convective, mixing, remap_weights, sources, send_lists
):
    levels = profile.shape[1]
    grid_rows = profile.shape[2]
    grid_cols = profile.shape[3]
    cell_count = grid_rows * grid_cols
    tile_size = remap_weights.shape[-1]
    column_state = profile.reshape(levels, cell_count)
    start_surface = surface.reshape(grid_rows, grid_cols)
    coefficient = diffusion.reshape(grid_rows, grid_cols)
    sea_float = sea_mask.reshape(grid_rows, grid_cols).astype(jnp.float32)
    deep_flags = convective.reshape(cell_count) == 1
    matrices = mixing.reshape(2, levels, levels)
    weights = remap_weights.reshape(remap_weights.shape[3:])
    wanted = sources.reshape(sources.shape[3:])
    lists = send_lists.reshape(send_lists.shape[3:])
    senders, slot_count = lists.shape
    sec_count = lax.axis_size("sec")
    gx_count = lax.axis_size("gx")
    gy_count = lax.axis_size("gy")
    ocean_side = lax.axis_index("sec") == sec_count - 1
    base_x = (sec_count - 1) * gx_count
    base_y = (sec_count - 1) * gy_count

    def advance(state):
        for substep in range(PHYS):
            plain_mix = jnp.dot(matrices[0], state, preferred_element_type=jnp.float32)
            deep_mix = jnp.dot(matrices[1], state, preferred_element_type=jnp.float32)
            mixed = jnp.where(deep_flags, deep_mix, plain_mix)
            state = (0.5 * state.astype(jnp.float32) + jnp.tanh(mixed)).astype(jnp.bfloat16)
        return state

    def exchange(lowest):
        tiles = lowest.reshape(cell_count // tile_size, tile_size)
        chosen = tiles[lists]
        return lax.all_to_all(chosen, ("sec", "gx"), 0, 0, tiled=True)

    def remap(received):
        picked = received.reshape(senders * slot_count, tile_size)[wanted]
        return jnp.einsum("akij,akj->ai", weights, picked, preferred_element_type=jnp.float32)

    def widen(fields):
        up = [(base_x + i, base_x + i + 1) for i in range(gx_count - 1)]
        down = [(t, s) for s, t in up]
        before = lax.ppermute(fields[:, -HALO:, :], ("sec", "gx"), up)
        after = lax.ppermute(fields[:, :HALO, :], ("sec", "gx"), down)
        fields = jnp.concatenate([before, fields, after], axis=1)
        up = [(base_y + i, base_y + i + 1) for i in range(gy_count - 1)]
        down = [(t, s) for s, t in up]
        before = lax.ppermute(fields[:, :, -HALO:], ("sec", "gy"), up)
        after = lax.ppermute(fields[:, :, :HALO], ("sec", "gy"), down)
        return jnp.concatenate([before, fields, after], axis=2)

    def passes(height, forcing, coef, sea):
        for sweep in range(PASSES):
            around = height[2:, 1:-1] + height[:-2, 1:-1]
            around = around + height[1:-1, 2:] + height[1:-1, :-2]
            inner = height[1:-1, 1:-1]
            cut = sweep + 1
            rows = slice(cut, coef.shape[0] - cut)
            cols = slice(cut, coef.shape[1] - cut)
            height = sea[rows, cols] * (
                inner + coef[rows, cols] * (around - 4.0 * inner) + forcing[rows, cols]
            )
        return height

    still = widen(jnp.stack([start_surface, coefficient, sea_float]))
    lowest = column_state[0]
    imported = remap(exchange(lowest))
    flux = sea_float * (imported - lowest.reshape(grid_rows, grid_cols).astype(jnp.float32))

    def bottom_of(lowest, flux):
        return (lowest.astype(jnp.float32) + flux.reshape(cell_count)).astype(jnp.bfloat16)

    def unchanged(state, bottom):
        return state

    def forced_advance(state, bottom):
        return advance(state.at[0].set(bottom))

    first = lax.cond(ocean_side, unchanged, forced_advance, column_state, bottom_of(lowest, flux))
    lowest_1 = first[0]
    received_1 = exchange(lowest_1)

    forcing = widen((flux / PASSES)[None])[0]
    height = passes(still[0], forcing, still[1], still[2])

    flux_air = sea_float * (imported - lowest_1.reshape(grid_rows, grid_cols).astype(jnp.float32))
    column_state = lax.cond(ocean_side, unchanged, forced_advance, first, bottom_of(lowest_1, flux_air))

    imported_1 = remap(received_1)
    flux_1 = sea_float * (imported_1 - lowest_1.reshape(grid_rows, grid_cols).astype(jnp.float32))
    both = widen(jnp.stack([height, flux_1 / PASSES]))
    height = passes(both[0], both[1], still[1], still[2])
    surface_out = jnp.where(ocean_side, height, start_surface)
    return (column_state.reshape(profile.shape), surface_out.reshape(surface.shape))


def solution(mesh):
    return jax.shard_map(
        body,
        mesh=mesh,
        in_specs=(
            P("sec", None, "gx", "gy"),
            P("sec", "gx", "gy"),
            P("sec", "gx", "gy"),
            P("sec", "gx", "gy"),
            P("sec", "gx", "gy"),
            P("sec", None, None, None),
            P("sec", "gx", "gy", None, None, None, None),
            P("sec", "gx", "gy", None, None),
            P("sec", "gx", "gy", None, None),
        ),
        out_specs=(P("sec", None, "gx", "gy"), P("sec", "gx", "gy")),
        check_vma=False,
    )
```

time: 539 us -> 106 us (0.20)
  the two profiles are of different devices: /device:TPU:2 before, /device:TPU:23 now
where the time goes in v1:
time: 106 us; the launch traced here: 105 us
  starting transfers between devices  75.2 us (71%)
  local copies, waits for them, and re-layouts  11.9 us (11%)
  other arithmetic  9.04 us (9%)
  waiting for transfers between devices  6.27 us (6%)
  matrix products  1.28 us (1%)
    all_to_all x2, starting transfers between devices, exchange(): return lax.all_to_all(chosen, ('sec', 'gx'), 0, 0, tiled=True)  35.9 us
    ppermute x3, starting transfers between devices, widen(): after = lax.ppermute(fields[:, :HALO, :], ('sec', 'gx'), down)  14.9 us
    ppermute x3, starting transfers between devices, widen(): before = lax.ppermute(fields[:, :, -HALO:], ('sec', 'gy'), up)  11 us
    ppermute x3, starting transfers between devices, widen(): before = lax.ppermute(fields[:, -HALO:, :], ('sec', 'gx'), up)  7.38 us
    ppermute x3, starting transfers between devices, widen(): after = lax.ppermute(fields[:, :, :HALO], ('sec', 'gy'), down)  6.08 us
    ppermute x3, waiting for transfers between devices, widen(): after = lax.ppermute(fields[:, :, :HALO], ('sec', 'gy'), down)  4.49 us
    cond x2, local copies, waits for them, and re-layouts  2.9 us
    unnamed x13, local copies, waits for them, and re-layouts  2.73 us
  transfers between devices with their start and end apart: 14, of which 4 were waited for; matrix products, arithmetic and copies ran while one was open for 11% of the time, Pallas kernels for 0%

profile of v1, /device:TPU:23, one launch (start us, length us, event | category | flops | bytes accessed | tf_op | source)
XLA Modules:
  0.0 104.9 jit_solution(7366933367550570942)
XLA Ops:
  0.7 0.8 compare_select_fusion.1
  2.4 1.3 %gather_fusion = bf16[128,128]{1,0:T(8,128)(2,1)} fusion(bf16[32,128]{1,0:T(8,128)(2,1)S(1)} %slice_bitcast_fusion.5, s32[1024]{0:T(1024)S(1)} %pad_clamp_fusion.1), kind=kCustom, calls=%fused_computation | custom fusion | bytes 66048 | tf_op jit(solution)/shard_map/gather | solution.py:47
  3.7 14.4 %all-to-all-start = ((bf16[64,2,128]{2,1,0:T(2,128)(2,1)}), bf16[64,2,128]{2,1,0:T(2,128)(2,1)S(1)}, u32[]{:S(2)}, u32[]{:S(2)}) async-start(bf16[64,2,128]{2,1,0:T(2,128)(2,1)} %bitcast.18), calls=%async_computation | async-start | bytes 65536 | tf_op jit(solution)/shard_map/all_to_all | solution.py:48
  18.1 0.7 convert_element_type.87
  18.8 0.7 pad_maximum_fusion.7
  19.6 3.1 %collective-permute-start = (f32[3,4,128]{2,1,0:T(4,128)S(1)}, f32[3,4,128]{2,1,0:T(4,128)S(1)}, u32[]{:S(2)}, u32[]{:S(2)}) collective-permute-start(f32[3,4,128]{2,1,0:T(4,128)S(1)} %get-tuple-element.72), channel_id=1, source_target_pairs={{384,392},{392,400},{400,408},{408,416},{416,424},{424,432},{432,4... | collective-permute-start | bytes 18440 | tf_op jit(solution)/shard_map/ppermute | solution.py:57
  22.7 4.3 %collective-permute-start.1 = (f32[3,4,128]{2,1,0:T(4,128)S(1)}, f32[3,4,128]{2,1,0:T(4,128)S(1)}, u32[]{:S(2)}, u32[]{:S(2)}) collective-permute-start(f32[3,4,128]{2,1,0:T(4,128)S(1)} %get-tuple-element.73), channel_id=1, source_target_pairs={{392,384},{400,392},{408,400},{416,408},{424,416},{432,424},{440,4... | collective-permute-start | bytes 18440 | tf_op jit(solution)/shard_map/ppermute | solution.py:58
  27.8 0.7 compare_bitcast_fusion
  28.6 2.7 %copy.19 = bf16[1,128,32,128]{1,3,2,0:T(8,128)(2,1)} copy(bf16[1,128,32,128]{3,2,1,0:T(8,128)(2,1)} %param.17) | data formatting | bytes 2097152 | tf_op args[0]
  32.6 0.7 fusion.120
  33.4 1.2 %conditional.2 = (bf16[128,4096]{0,1:T(8,128)(2,1)S(1)}) conditional(s32[]{:T(128)} %convert_element_type.84, (bf16[4096]{0:T(1024)(128)(2,1)S(1)}, bf16[128,4096]{0,1:T(8,128)(2,1)}, pred[4096]{0:T(1024)(128)(4,1)S(1)}, bf16[2,128,128]{2,1,0:T(8,128)(2,1)S(1)}) %tuple.51, bf16[128,4096]{0,1:T(8,128)(2,1)} %bitcast.27), branch_computations={%region_0.1_spmd, %region_1.2_spmd} | conditional | flops 1084227584 | bytes 33865740 | solution.py:93
  33.4 1.2 %copy.34 = bf16[128,4096]{0,1:T(8,128)(2,1)S(1)} copy(bf16[128,4096]{0,1:T(8,128)(2,1)} %param.5) | data formatting | bytes 2097152 | tf_op jit(solution)/shard_map/cond
  35.0 1.3 %gather_fusion.2 = bf16[128,128]{1,0:T(8,128)(2,1)} fusion(bf16[32,128]{1,0:T(8,128)(2,1)S(1)} %bitcast.186, s32[1024]{0:T(1024)S(1)} %pad_clamp_fusion.1), kind=kCustom, calls=%fused_computation.2 | custom fusion | bytes 66048 | tf_op jit(solution)/shard_map/gather | solution.py:47
  36.3 21.6 %all-to-all-start.1 = ((bf16[64,2,128]{2,1,0:T(2,128)(2,1)}), bf16[64,2,128]{2,1,0:T(2,128)(2,1)S(1)}, u32[]{:S(2)}, u32[]{:S(2)}) async-start(bf16[64,2,128]{2,1,0:T(2,128)(2,1)} %bitcast.38), calls=%async_computation.1 | async-start | bytes 65536 | tf_op jit(solution)/shard_map/all_to_all | solution.py:48
  58.6 3.2 %collective-permute-start.2 = (f32[3,40,4]{2,1,0:T(8,128)}, f32[3,40,4]{2,1,0:T(8,128)S(1)}, u32[]{:S(2)}, u32[]{:S(2)}) collective-permute-start(f32[3,40,4]{2,1,0:T(8,128)} %get-tuple-element.70), channel_id=1, source_target_pairs={{384,385},{385,386},{386,387},{387,388},{388,389},{389,390},{390,3... | collective-permute-start | bytes 5768 | tf_op jit(solution)/shard_map/ppermute | solution.py:62
  61.8 2.1 %collective-permute-start.3 = (f32[3,40,4]{2,1,0:T(8,128)S(1)}, f32[3,40,4]{2,1,0:T(8,128)S(1)}, u32[]{:S(2)}, u32[]{:S(2)}) collective-permute-start(f32[3,40,4]{2,1,0:T(8,128)S(1)} %get-tuple-element.71), channel_id=1, source_target_pairs={{385,384},{386,385},{387,386},{388,387},{389,388},{390,389},{391,3... | collective-permute-start | bytes 5768 | tf_op jit(solution)/shard_map/ppermute | solution.py:63
  63.9 1.4 %all-to-all-done.1 = bf16[64,2,128]{2,1,0:T(2,128)(2,1)S(1)} async-done(((bf16[64,2,128]{2,1,0:T(2,128)(2,1)}), bf16[64,2,128]{2,1,0:T(2,128)(2,1)S(1)}, u32[]{:S(2)}, u32[]{:S(2)}) %all-to-all-start.1) | async-done | bytes 32800 | tf_op jit(solution)/shard_map/all_to_all | solution.py:48
  66.5 0.7 multiply_bitcast_fusion
  67.3 2.2 %collective-permute-start.4 = (f32[1,4,128]{2,1,0:T(4,128)S(1)}, f32[1,4,128]{2,1,0:T(4,128)S(1)}, u32[]{:S(2)}, u32[]{:S(2)}) collective-permute-start(f32[1,4,128]{2,1,0:T(4,128)S(1)} %get-tuple-element.80), channel_id=1, source_target_pairs={{384,392},{392,400},{400,408},{408,416},{416,424},{424,432},{432,4... | collective-permute-start | bytes 6152 | tf_op jit(solution)/shard_map/ppermute | solution.py:57
  69.5 5.2 %collective-permute-start.5 = (f32[1,4,128]{2,1,0:T(4,128)S(1)}, f32[1,4,128]{2,1,0:T(4,128)S(1)}, u32[]{:S(2)}, u32[]{:S(2)}) collective-permute-start(f32[1,4,128]{2,1,0:T(4,128)S(1)} %get-tuple-element.81), channel_id=1, source_target_pairs={{392,384},{400,392},{408,400},{416,408},{424,416},{432,424},{440,4... | collective-permute-start | bytes 6152 | tf_op jit(solution)/shard_map/ppermute | solution.py:58
  74.7 0.8 pad_maximum_fusion
  75.6 3.2 %collective-permute-start.6 = (f32[1,40,4]{2,1,0:T(8,128)S(1)}, f32[1,40,4]{2,1,0:T(8,128)S(1)}, u32[]{:S(2)}, u32[]{:S(2)}) collective-permute-start(f32[1,40,4]{2,1,0:T(8,128)S(1)} %get-tuple-element.78), channel_id=1, source_target_pairs={{384,385},{385,386},{386,387},{387,388},{388,389},{389,390},{390,3... | collective-permute-start | bytes 1928 | tf_op jit(solution)/shard_map/ppermute | solution.py:62
  78.8 2.1 %collective-permute-start.7 = (f32[1,40,4]{2,1,0:T(8,128)S(1)}, f32[1,40,4]{2,1,0:T(8,128)S(1)}, u32[]{:S(2)}, u32[]{:S(2)}) collective-permute-start(f32[1,40,4]{2,1,0:T(8,128)S(1)} %get-tuple-element.79), channel_id=1, source_target_pairs={{385,384},{386,385},{387,386},{388,387},{389,388},{390,389},{391,3... | collective-permute-start | bytes 1928 | tf_op jit(solution)/shard_map/ppermute | solution.py:63
  81.0 3.5 %collective-permute-done.7 = f32[1,40,4]{2,1,0:T(8,128)S(1)} collective-permute-done((f32[1,40,4]{2,1,0:T(8,128)S(1)}, f32[1,40,4]{2,1,0:T(8,128)S(1)}, u32[]{:S(2)}, u32[]{:S(2)}) %collective-permute-start.7) | collective-permute-done | bytes 672 | tf_op jit(solution)/shard_map/ppermute | solution.py:63
  85.1 2.1 %collective-permute-start.8 = (f32[2,4,128]{2,1,0:T(4,128)S(1)}, f32[2,4,128]{2,1,0:T(4,128)S(1)}, u32[]{:S(2)}, u32[]{:S(2)}) collective-permute-start(f32[2,4,128]{2,1,0:T(4,128)S(1)} %get-tuple-element.76), channel_id=1, source_target_pairs={{384,392},{392,400},{400,408},{408,416},{416,424},{424,432},{432,4... | collective-permute-start | bytes 12296 | tf_op jit(solution)/shard_map/ppermute | solution.py:57
  87.2 5.4 %collective-permute-start.9 = (f32[2,4,128]{2,1,0:T(4,128)S(1)}, f32[2,4,128]{2,1,0:T(4,128)S(1)}, u32[]{:S(2)}, u32[]{:S(2)}) collective-permute-start(f32[2,4,128]{2,1,0:T(4,128)S(1)} %get-tuple-element.77), channel_id=1, source_target_pairs={{392,384},{400,392},{408,400},{416,408},{424,416},{432,424},{440,4... | collective-permute-start | bytes 12296 | tf_op jit(solution)/shard_map/ppermute | solution.py:58
  93.4 4.6 %collective-permute-start.10 = (f32[2,40,4]{2,1,0:T(8,128)S(1)}, f32[2,40,4]{2,1,0:T(8,128)S(1)}, u32[]{:S(2)}, u32[]{:S(2)}) collective-permute-start(f32[2,40,4]{2,1,0:T(8,128)S(1)} %get-tuple-element.74), channel_id=1, source_target_pairs={{384,385},{385,386},{386,387},{387,388},{388,389},{389,390},{390,3... | collective-permute-start | bytes 3848 | tf_op jit(solution)/shard_map/ppermute | solution.py:62
  98.0 1.9 %collective-permute-start.11 = (f32[2,40,4]{2,1,0:T(8,128)S(1)}, f32[2,40,4]{2,1,0:T(8,128)}, u32[]{:S(2)}, u32[]{:S(2)}) collective-permute-start(f32[2,40,4]{2,1,0:T(8,128)S(1)} %get-tuple-element.75), channel_id=1, source_target_pairs={{385,384},{386,385},{387,386},{388,387},{389,388},{390,389},{391,3... | collective-permute-start | bytes 3848 | tf_op jit(solution)/shard_map/ppermute | solution.py:63
  99.9 1.9 %conditional.3 = (bf16[1,128,32,128]{3,2,1,0:T(8,128)(2,1)}) conditional(s32[]{:T(128)} %convert_element_type.84, (bf16[4096]{0:T(1024)(128)(2,1)S(1)}, bf16[128,4096]{0,1:T(8,128)(2,1)S(1)}, pred[4096]{0:T(1024)(128)(4,1)S(1)}, bf16[2,128,128]{2,1,0:T(8,128)(2,1)S(1)}) %tuple.52, bf16[128,4096]{0,1:T(8,128)(2,1)S(1)} %get-tuple-element.86), branch_computations={%region_2.3_spmd, %region_3.4_spmd} | conditional | flops 1084227584 | bytes 35962892 | solution.py:101
  100.1 1.7 %copy.26 = bf16[1,128,32,128]{3,2,1,0:T(8,128)(2,1)} copy(bf16[1,128,32,128]{1,3,2,0:T(8,128)(2,1)S(1)} %bitcast.185) | data formatting | bytes 2097152 | tf_op jit(solution)/shard_map/cond
  101.8 1.0 collective-permute-done.11
  102.8 0.9 pad_maximum_fusion.1
  (57 shorter events, 8.2 us)
Async XLA Ops:
  0.6 31.4 %copy-start = (bf16[1,1,1,32,2,128,128]{6,5,4,3,2,1,0:T(8,128)(2,1)S(1)}, bf16[1,1,1,32,2,128,128]{6,5,4,3,2,1,0:T(8,128)(2,1)}, u32[]{:S(2)}) copy-start(bf16[1,1,1,32,2,128,128]{6,5,4,3,2,1,0:T(8,128)(2,1)} %param.23) | copy-start | bytes 6291460
  0.6 30.7 %copy-start.2 = (f32[1,32,128]{2,1,0:T(8,128)S(1)}, f32[1,32,128]{2,1,0:T(8,128)}, u32[]{:S(2)}) copy-start(f32[1,32,128]{2,1,0:T(8,128)} %param.18) | copy-start | bytes 49156
  0.7 30.7 %copy-start.4 = (f32[1,32,128]{2,1,0:T(8,128)S(1)}, f32[1,32,128]{2,1,0:T(8,128)}, u32[]{:S(2)}) copy-start(f32[1,32,128]{2,1,0:T(8,128)} %param.19) | copy-start | bytes 49156
  3.7 27.6 %all-to-all-start = ((bf16[64,2,128]{2,1,0:T(2,128)(2,1)}), bf16[64,2,128]{2,1,0:T(2,128)(2,1)S(1)}, u32[]{:S(2)}, u32[]{:S(2)}) async-start(bf16[64,2,128]{2,1,0:T(2,128)(2,1)} %bitcast.18), calls=%async_computation | async-start | bytes 65536 | tf_op jit(solution)/shard_map/all_to_all | solution.py:48
  19.6 11.7 %collective-permute-start = (f32[3,4,128]{2,1,0:T(4,128)S(1)}, f32[3,4,128]{2,1,0:T(4,128)S(1)}, u32[]{:S(2)}, u32[]{:S(2)}) collective-permute-start(f32[3,4,128]{2,1,0:T(4,128)S(1)} %get-tuple-element.72), channel_id=1, source_target_pairs={{384,392},{392,400},{400,408},{408,416},{416,424},{424,432},{432,4... | collective-permute-start | bytes 18440 | tf_op jit(solution)/shard_map/ppermute | solution.py:57
  22.7 8.6 %collective-permute-start.1 = (f32[3,4,128]{2,1,0:T(4,128)S(1)}, f32[3,4,128]{2,1,0:T(4,128)S(1)}, u32[]{:S(2)}, u32[]{:S(2)}) collective-permute-start(f32[3,4,128]{2,1,0:T(4,128)S(1)} %get-tuple-element.73), channel_id=1, source_target_pairs={{392,384},{400,392},{408,400},{416,408},{424,416},{432,424},{440,4... | collective-permute-start | bytes 18440 | tf_op jit(solution)/shard_map/ppermute | solution.py:58
  28.6 4.1 %copy-start.3 = (s32[1,32,128]{2,1,0:T(8,128)S(1)}, s32[1,32,128]{2,1,0:T(8,128)}, u32[]{:S(2)}) copy-start(s32[1,32,128]{2,1,0:T(8,128)} %param.20) | copy-start | bytes 49156
  28.6 4.8 %copy-start.1 = (bf16[1,2,128,128]{3,2,1,0:T(8,128)(2,1)S(1)}, bf16[1,2,128,128]{3,2,1,0:T(8,128)(2,1)}, u32[]{:S(2)}) copy-start(bf16[1,2,128,128]{3,2,1,0:T(8,128)(2,1)} %param.22) | copy-start | bytes 196612
  31.3 1.3 %copy-start.5 = (f32[3,4,128]{2,1,0:T(4,128)}, f32[3,4,128]{2,1,0:T(4,128)S(1)}, u32[]{:S(2)}) copy-start(f32[3,4,128]{2,1,0:T(4,128)S(1)} %collective-permute-done.1) | copy-start | bytes 18436
  36.3 29.0 %all-to-all-start.1 = ((bf16[64,2,128]{2,1,0:T(2,128)(2,1)}), bf16[64,2,128]{2,1,0:T(2,128)(2,1)S(1)}, u32[]{:S(2)}, u32[]{:S(2)}) async-start(bf16[64,2,128]{2,1,0:T(2,128)(2,1)} %bitcast.38), calls=%async_computation.1 | async-start | bytes 65536 | tf_op jit(solution)/shard_map/all_to_all | solution.py:48
  58.6 16.1 %collective-permute-start.2 = (f32[3,40,4]{2,1,0:T(8,128)}, f32[3,40,4]{2,1,0:T(8,128)S(1)}, u32[]{:S(2)}, u32[]{:S(2)}) collective-permute-start(f32[3,40,4]{2,1,0:T(8,128)} %get-tuple-element.70), channel_id=1, source_target_pairs={{384,385},{385,386},{386,387},{387,388},{388,389},{389,390},{390,3... | collective-permute-start | bytes 5768 | tf_op jit(solution)/shard_map/ppermute | solution.py:62
  61.8 12.9 %collective-permute-start.3 = (f32[3,40,4]{2,1,0:T(8,128)S(1)}, f32[3,40,4]{2,1,0:T(8,128)S(1)}, u32[]{:S(2)}, u32[]{:S(2)}) collective-permute-start(f32[3,40,4]{2,1,0:T(8,128)S(1)} %get-tuple-element.71), channel_id=1, source_target_pairs={{385,384},{386,385},{387,386},{388,387},{389,388},{390,389},{391,3... | collective-permute-start | bytes 5768 | tf_op jit(solution)/shard_map/ppermute | solution.py:63
  67.3 8.3 %collective-permute-start.4 = (f32[1,4,128]{2,1,0:T(4,128)S(1)}, f32[1,4,128]{2,1,0:T(4,128)S(1)}, u32[]{:S(2)}, u32[]{:S(2)}) collective-permute-start(f32[1,4,128]{2,1,0:T(4,128)S(1)} %get-tuple-element.80), channel_id=1, source_target_pairs={{384,392},{392,400},{400,408},{408,416},{416,424},{424,432},{432,4... | collective-permute-start | bytes 6152 | tf_op jit(solution)/shard_map/ppermute | solution.py:57
  69.5 6.0 %collective-permute-start.5 = (f32[1,4,128]{2,1,0:T(4,128)S(1)}, f32[1,4,128]{2,1,0:T(4,128)S(1)}, u32[]{:S(2)}, u32[]{:S(2)}) collective-permute-start(f32[1,4,128]{2,1,0:T(4,128)S(1)} %get-tuple-element.81), channel_id=1, source_target_pairs={{392,384},{400,392},{408,400},{416,408},{424,416},{432,424},{440,4... | collective-permute-start | bytes 6152 | tf_op jit(solution)/shard_map/ppermute | solution.py:58
  75.6 5.3 %collective-permute-start.6 = (f32[1,40,4]{2,1,0:T(8,128)S(1)}, f32[1,40,4]{2,1,0:T(8,128)S(1)}, u32[]{:S(2)}, u32[]{:S(2)}) collective-permute-start(f32[1,40,4]{2,1,0:T(8,128)S(1)} %get-tuple-element.78), channel_id=1, source_target_pairs={{384,385},{385,386},{386,387},{387,388},{388,389},{389,390},{390,3... | collective-permute-start | bytes 1928 | tf_op jit(solution)/shard_map/ppermute | solution.py:62
  78.8 5.6 %collective-permute-start.7 = (f32[1,40,4]{2,1,0:T(8,128)S(1)}, f32[1,40,4]{2,1,0:T(8,128)S(1)}, u32[]{:S(2)}, u32[]{:S(2)}) collective-permute-start(f32[1,40,4]{2,1,0:T(8,128)S(1)} %get-tuple-element.79), channel_id=1, source_target_pairs={{385,384},{386,385},{387,386},{388,387},{389,388},{390,389},{391,3... | collective-permute-start | bytes 1928 | tf_op jit(solution)/shard_map/ppermute | solution.py:63
  85.1 7.9 %collective-permute-start.8 = (f32[2,4,128]{2,1,0:T(4,128)S(1)}, f32[2,4,128]{2,1,0:T(4,128)S(1)}, u32[]{:S(2)}, u32[]{:S(2)}) collective-permute-start(f32[2,4,128]{2,1,0:T(4,128)S(1)} %get-tuple-element.76), channel_id=1, source_target_pairs={{384,392},{392,400},{400,408},{408,416},{416,424},{424,432},{432,4... | collective-permute-start | bytes 12296 | tf_op jit(solution)/shard_map/ppermute | solution.py:57
  87.2 6.1 %collective-permute-start.9 = (f32[2,4,128]{2,1,0:T(4,128)S(1)}, f32[2,4,128]{2,1,0:T(4,128)S(1)}, u32[]{:S(2)}, u32[]{:S(2)}) collective-permute-start(f32[2,4,128]{2,1,0:T(4,128)S(1)} %get-tuple-element.77), channel_id=1, source_target_pairs={{392,384},{400,392},{408,400},{416,408},{424,416},{432,424},{440,4... | collective-permute-start | bytes 12296 | tf_op jit(solution)/shard_map/ppermute | solution.py:58
  93.4 8.4 %collective-permute-start.10 = (f32[2,40,4]{2,1,0:T(8,128)S(1)}, f32[2,40,4]{2,1,0:T(8,128)S(1)}, u32[]{:S(2)}, u32[]{:S(2)}) collective-permute-start(f32[2,40,4]{2,1,0:T(8,128)S(1)} %get-tuple-element.74), channel_id=1, source_target_pairs={{384,385},{385,386},{386,387},{387,388},{388,389},{389,390},{390,3... | collective-permute-start | bytes 3848 | tf_op jit(solution)/shard_map/ppermute | solution.py:62
  98.0 4.9 %collective-permute-start.11 = (f32[2,40,4]{2,1,0:T(8,128)S(1)}, f32[2,40,4]{2,1,0:T(8,128)}, u32[]{:S(2)}, u32[]{:S(2)}) collective-permute-start(f32[2,40,4]{2,1,0:T(8,128)S(1)} %get-tuple-element.75), channel_id=1, source_target_pairs={{385,384},{386,385},{387,386},{388,387},{389,388},{390,389},{391,3... | collective-permute-start | bytes 3848 | tf_op jit(solution)/shard_map/ppermute | solution.py:63

commit v2 on v0

v2 whole, which is shorter than its diff:
```python
import functools

import jax
import jax.numpy as jnp
from jax import lax
from jax.experimental import pallas as pl
from jax.experimental.pallas import tpu as pltpu
from jax.sharding import PartitionSpec as P

PHYS = 4
PASSES = 4
HALO = 8
NEAR = 3
PLANES = 5
WIDTH = 2048
MESSAGE = 6
bf16 = jnp.bfloat16
f32 = jnp.float32
VMEM_LIMIT = 24 * 1024 * 1024


def call(kernel, outs, name, in_specs=None, scratch=(), flops=0):
    more = {} if in_specs is None else {"in_specs": in_specs, "grid": (1,)}
    return pl.pallas_call(
        kernel,
        out_shape=[jax.ShapeDtypeStruct(shape, kind) for shape, kind in outs],
        scratch_shapes=list(scratch),
        name=name,
        cost_estimate=pl.CostEstimate(flops=flops, bytes_accessed=1 << 20, transcendentals=0),
        compiler_params=pltpu.CompilerParams(vmem_limit_bytes=VMEM_LIMIT),
        **more,
    )


def whole():
    return pl.BlockSpec(memory_space=pltpu.VMEM)


def is_ocean():
    return lax.axis_index("sec") == lax.axis_size("sec") - 1


def iota(shape, dim):
    return lax.broadcasted_iota(jnp.int32, shape, dim)


def one_hot(flags):
    return jnp.where(flags, 1.0, 0.0).astype(bf16)


def take(hot, rows):
    return jnp.dot(hot, rows, preferred_element_type=f32).astype(bf16)


def listed(tiles, lists):
    place = iota((lists.shape[0], tiles.shape[0]), 1)
    return jnp.concatenate(
        [take(one_hot(lists[:, c : c + 1] == place), tiles) for c in range(lists.shape[1])], axis=0
    )


def select_kernel(level_ref, lists_ref, out_ref, lowest_ref):
    lists = lists_ref[...]
    senders = lists.shape[0]
    tiles = level_ref[0, 0]
    lowest_ref[...] = tiles.astype(f32)
    chosen = listed(tiles, lists)
    row = iota((out_ref.shape[0], chosen.shape[0]), 0)
    col = iota((out_ref.shape[0], chosen.shape[0]), 1)
    out_ref[...] = take(one_hot(col == (row & 1) * senders + (row >> 1)), chosen)


def edges_kernel(*refs):
    surface, diffusion, sea, lowest, sources = refs[:5]
    weights = refs[5 : 5 + 2 * NEAR]
    to_next, to_prev = refs[-2:]
    rows = surface.shape[0]
    for out, first, blocks in ((to_prev, 0, weights[:NEAR]), (to_next, rows - HALO, weights[NEAR:])):
        part = slice(first, first + HALO)
        out[0:HALO] = surface[part]
        out[HALO : 2 * HALO] = diffusion[part]
        out[2 * HALO : 3 * HALO] = sea[part].astype(f32)
        out[3 * HALO : 4 * HALO] = lowest[part]
        out[4 * HALO : 5 * HALO] = jnp.zeros((HALO, out.shape[1]), f32)
        out[4 * HALO : 5 * HALO, 0:2] = sources[part].astype(f32)
        base = PLANES * HALO
        for block in blocks:
            for k in range(2):
                size = block.shape[2]
                out[base : base + size] = block[0, k].astype(f32)
                base += size


def import_row(pick_ref, a, first, second):
    row = pick_ref[a : a + 1, :].astype(bf16)
    block = jnp.concatenate([first, second], axis=1)
    return lax.dot_general(row, block, (((1,), (1,)), ((), ())), preferred_element_type=f32)


def substep(x, flag, mix):
    deep = x * flag
    both = jnp.concatenate([x - deep, deep], axis=0)
    mixed = jnp.dot(mix, both, preferred_element_type=f32)
    return (0.5 * x.astype(f32) + jnp.tanh(mixed)).astype(bf16)


def with_bottom(x, bottom):
    top = x[0:16].astype(f32)
    top = jnp.where(iota(top.shape, 0) == 0, bottom, top).astype(bf16)
    return jnp.concatenate([top, x[16:]], axis=0)


def flat_rows(grid, first, count):
    return jnp.concatenate([grid[first + r : first + r + 1] for r in range(count)], axis=1)


def first_kernel(
    received, sources, weights, lowest_ref, sea, x_ref, flag_ref, mixing, lists_ref,
    state, message, low, carry, pick, low_f,
):
    src = sources[...]
    rows = src.shape[0]
    place = iota((rows, received.shape[0]), 1)
    tile = received.shape[1]
    for k in range(2):
        hot = one_hot(src[:, k : k + 1] == place)
        pick[:, k * tile : (k + 1) * tile] = jnp.dot(hot, received[...], preferred_element_type=f32)
    for a in range(rows):
        carry[a : a + 1, :] = import_row(pick, a, weights[a, 0], weights[a, 1])
    lowest = lowest_ref[...]
    flux = sea[...].astype(f32) * (carry[...] - lowest)

    @pl.when(is_ocean())
    def _():
        carry[...] = flux * (1.0 / PASSES)
        message[...] = jnp.zeros(message.shape, bf16)

    @pl.when(jnp.logical_not(is_ocean()))
    def _():
        mix = jnp.concatenate([mixing[0], mixing[1]], axis=1)
        bottom = (lowest + flux).astype(bf16).astype(f32)
        per = WIDTH // tile
        for c in range(x_ref.shape[1] // WIDTH):
            cols = slice(c * WIDTH, (c + 1) * WIDTH)
            flag = flag_ref[:, cols]
            x = with_bottom(x_ref[:, cols], flat_rows(bottom, c * per, per))
            for _ in range(PHYS - 1):
                x = substep(x, flag, mix)
            state[:, cols] = x
            deep = x * flag
            both = jnp.concatenate([x - deep, deep], axis=0)
            mixed = jnp.dot(mix[0:16], both, preferred_element_type=f32)
            last = 0.5 * x[0:16].astype(f32) + jnp.tanh(mixed)
            for r in range(per):
                low_f[c * per + r : c * per + r + 1, :] = last[0:1, r * tile : (r + 1) * tile]
        tiles = low_f[...].astype(bf16)
        low[...] = tiles
        lists = lists_ref[...]
        senders = lists.shape[0]
        chosen = listed(tiles, lists)
        row = iota((message.shape[0], chosen.shape[0]), 0)
        col = iota((message.shape[0], chosen.shape[0]), 1)
        target = (row * 10923) >> 16
        m = row - MESSAGE * target
        message[...] = take(one_hot(col == (m & 1) * senders + target - 1 + (m >> 1)), chosen)


def second_kernel(state, low, carry, sea, x_ref, flag_ref, mixing, out, to_next, to_prev):
    @pl.when(is_ocean())
    def _():
        rows = carry.shape[0]
        to_prev[...] = carry[0:HALO]
        to_next[...] = carry[rows - HALO : rows]
        out[...] = x_ref[...]

    @pl.when(jnp.logical_not(is_ocean()))
    def _():
        mix = jnp.concatenate([mixing[0], mixing[1]], axis=1)
        lowest = low[...].astype(f32)
        flux = sea[...].astype(f32) * (carry[...] - lowest)
        bottom = (lowest + flux).astype(bf16).astype(f32)
        per = WIDTH // low.shape[1]
        for c in range(x_ref.shape[1] // WIDTH):
            cols = slice(c * WIDTH, (c + 1) * WIDTH)
            flag = flag_ref[:, cols]
            x = substep(state[:, cols], flag, mix)
            x = with_bottom(x, flat_rows(bottom, c * per, per))
            for _ in range(PHYS):
                x = substep(x, flag, mix)
            out[:, cols] = x


def third_kernel(
    received, sources, weights, lowest_ref, sea, surface, diffusion, forcing, still_above, still_below,
    forcing_above, forcing_below, wide, to_right, to_left, pick, imported,
):
    @pl.when(is_ocean())
    def _():
        rows, tile = surface.shape

        def plane(own, p):
            part = slice(p * HALO, (p + 1) * HALO)
            return jnp.concatenate([own, still_below[part], still_above[part]], axis=0)

        part = slice(4 * HALO, 5 * HALO)
        src = jnp.concatenate(
            [sources[...], still_below[part, 0:2].astype(jnp.int32), still_above[part, 0:2].astype(jnp.int32)],
            axis=0,
        )
        total = src.shape[0]
        row = iota((total, 1), 0)
        offset = jnp.where(row < rows, 2, jnp.where(row < rows + HALO, 4, 0))
        place = iota((total, received.shape[0]), 1)
        for k in range(2):
            q = src[:, k : k + 1]
            hot = one_hot((q >> 1) * MESSAGE + (q & 1) + offset == place)
            pick[:, k * tile : (k + 1) * tile] = jnp.dot(hot, received[...], preferred_element_type=f32)
        imported[...] = jnp.zeros(imported.shape, f32)
        for a in range(rows):
            imported[a : a + 1, :] = import_row(pick, a, weights[a, 0], weights[a, 1])
        for still, first in ((still_below, rows), (still_above, total - NEAR)):
            for n in range(NEAR):
                base = PLANES * HALO + 2 * n * tile
                blocks = [still[base + k * tile : base + (k + 1) * tile, :].astype(bf16) for k in range(2)]
                a = first + n
                imported[a : a + 1, :] = import_row(pick, a, blocks[0], blocks[1])
        sea_all = plane(sea[...].astype(f32), 2)
        lowest = plane(lowest_ref[...], 3)
        planes = [
            jnp.concatenate([forcing[...], forcing_below[...], forcing_above[...]], axis=0),
            sea_all * (imported[...] - lowest) * (1.0 / PASSES),
            plane(surface[...], 0),
            plane(diffusion[...], 1),
            sea_all,
        ]
        group = iota((total, tile), 1) >> 3
        right = planes[0]
        left = planes[0]
        for p, values in enumerate(planes):
            wide[p] = values
            if p:
                right = jnp.where(group == tile // HALO - 1 - p, pltpu.roll(values, tile - HALO * p, 1), right)
                left = jnp.where(group == p, pltpu.roll(values, HALO * p, 1), left)
        to_right[...] = right
        to_left[...] = left


def fourth_kernel(wide, from_left, from_right, surface, out):
    @pl.when(jnp.logical_not(is_ocean()))
    def _():
        out[...] = surface[...]

    @pl.when(is_ocean())
    def _():
        rows, tile = surface.shape
        total = wide.shape[1]
        group = iota((total, tile), 1) >> 3
        fields = []
        for p in range(PLANES):
            right, left = from_right[...], from_left[...]
            if p:
                right = pltpu.roll(right, tile - HALO * p, 1)
                left = pltpu.roll(left, HALO * p, 1)
            beside = jnp.where(group == 0, right, jnp.where(group == tile // HALO - 1, left, 0.0))
            fields.append(jnp.concatenate([wide[p], beside], axis=1))
        first, second, height, coefficient, sea = fields
        for forcing in (first, second):
            for sweep in range(PASSES):
                around = pltpu.roll(height, total - 1, 0) + pltpu.roll(height, 1, 0)
                around = around + pltpu.roll(height, 2 * tile - 1, 1) + pltpu.roll(height, 1, 1)
                height = sea * (height + coefficient * (around - 4.0 * height) + forcing)
        out[...] = height[0:rows, 0:tile]


def body(
    profile, surface, diffusion, sea_mask, convective, mixing, remap_weights, sources, send_lists
):
    levels, rows, tile = profile.shape[1:]
    cells = rows * tile
    surface_2d = surface.reshape(rows, tile)
    coefficient = diffusion.reshape(rows, tile)
    sea = sea_mask.reshape(rows, tile)
    matrices = mixing.reshape(2, levels, levels)
    weights = remap_weights.reshape(remap_weights.shape[3:])
    wanted = sources.reshape(sources.shape[3:])
    lists = send_lists.reshape(send_lists.shape[3:])
    senders, slots = lists.shape
    secs = lax.axis_size("sec")
    gx = lax.axis_size("gx")
    gy = lax.axis_size("gy")
    total = rows + 2 * HALO
    level = pl.BlockSpec((1, 1, rows, tile), lambda i: (0, 0, 0, 0))

    def along(axis, count, to_next, to_prev):
        base = (secs - 1) * count
        up = [(base + i, base + i + 1) for i in range(count - 1)]
        down = [(t, s) for s, t in up]
        return lax.ppermute(to_next, ("sec", axis), up), lax.ppermute(to_prev, ("sec", axis), down)

    chosen, lowest = call(
        select_kernel,
        [((senders * slots, tile), bf16), ((rows, tile), f32)],
        "select_tiles",
        [level, whole()],
    )(profile, lists)
    received = lax.all_to_all(chosen.reshape(senders, slots, tile), ("sec", "gx"), 0, 0, tiled=True)

    def near(a):
        return pl.BlockSpec((1, 2, tile, tile), lambda i: (a, 0, 0, 0))

    nears = [near(a) for a in (*range(NEAR), *range(rows - NEAR, rows))]
    height = PLANES * HALO + NEAR * 2 * tile
    still_next, still_prev = call(
        edges_kernel,
        [((height, tile), f32)] * 2,
        "edge_rows",
        [whole()] * 5 + nears,
    )(surface_2d, coefficient, sea, lowest, wanted, *[weights] * (2 * NEAR))
    still_above, still_below = along("gx", gx, still_next, still_prev)

    columns = profile.reshape(levels, cells)
    flag = convective.reshape(1, cells).astype(bf16)
    state, message, low, carry = call(
        first_kernel,
        [
            ((levels, cells), bf16),
            ((senders * MESSAGE, tile), bf16),
            ((rows, tile), bf16),
            ((rows, tile), f32),
        ],
        "first_step",
        scratch=[pltpu.VMEM((rows, 2 * tile), f32), pltpu.VMEM((rows, tile), f32)],
        flops=1 << 30,
    )(
        received.reshape(senders * slots, tile), wanted, weights, lowest, sea, columns, flag,
        matrices, lists,
    )
    again = lax.all_to_all(
        message.reshape(senders * MESSAGE // 2, 2, tile), ("sec", "gx"), 0, 0, tiled=True
    )
    final, forcing_next, forcing_prev = call(
        second_kernel,
        [((levels, cells), bf16), ((HALO, tile), f32), ((HALO, tile), f32)],
        "second_step",
        flops=1 << 31,
    )(state, low, carry, sea, columns, flag, matrices)
    forcing_above, forcing_below = along("gx", gx, forcing_next, forcing_prev)

    wide, to_right, to_left = call(
        third_kernel,
        [((PLANES, total, tile), f32), ((total, tile), f32), ((total, tile), f32)],
        "second_import",
        scratch=[pltpu.VMEM((total, 2 * tile), f32), pltpu.VMEM((total, tile), f32)],
    )(
        again.reshape(senders * MESSAGE, tile), wanted, weights, lowest, sea, surface_2d,
        coefficient, carry, still_above, still_below, forcing_above, forcing_below,
    )
    from_left, from_right = along("gy", gy, to_right, to_left)
    (surface_out,) = call(fourth_kernel, [((rows, tile), f32)], "passes")(
        wide, from_left, from_right, surface_2d
    )
    return (final.reshape(profile.shape), surface_out.reshape(surface.shape))


def solution(mesh):
    return jax.shard_map(
        body,
        mesh=mesh,
        in_specs=(
            P("sec", None, "gx", "gy"),
            P("sec", "gx", "gy"),
            P("sec", "gx", "gy"),
            P("sec", "gx", "gy"),
            P("sec", "gx", "gy"),
            P("sec", None, None, None),
            P("sec", "gx", "gy", None, None, None, None),
            P("sec", "gx", "gy", None, None),
            P("sec", "gx", "gy", None, None),
        ),
        out_specs=(P("sec", None, "gx", "gy"), P("sec", "gx", "gy")),
        check_vma=False,
    )
```

time: 539 us -> 68.3 us (0.13)
  the two profiles are of different devices: /device:TPU:2 before, /device:TPU:31 now
where the time goes in v2:
time: 68.3 us; the launch traced here: 67.6 us
  starting transfers between devices  44.8 us (66%)
  local copies, waits for them, and re-layouts  11.6 us (17%)
  Pallas kernels  6.95 us (10%)
  waiting for transfers between devices  3.4 us (5%)
  between operations  0.83 us (1%)
    all_to_all x1, starting transfers between devices, body(): lax.all_to_all(chosen.reshape(senders, slots, tile), ('sec', 'gx'), 0, 0,...  14.4 us
    ppermute x3, starting transfers between devices, along(): lax.ppermute(to_next, ('sec', axis), up)  10.7 us
    ppermute x3, starting transfers between devices, along(): lax.ppermute(to_prev, ('sec', axis), down)  10.5 us
    unnamed x35, local copies, waits for them, and re-layouts  10.1 us
    all_to_all x1, starting transfers between devices, body(): lax.all_to_all(message.reshape(senders * MESSAGE // 2, 2, tile), ('sec',...  9.23 us
    ppermute x3, waiting for transfers between devices, along(): lax.ppermute(to_prev, ('sec', axis), down)  3.38 us
    pallas_call x1, Pallas kernels, body(): call(third_kernel, [((PLANES, total, tile), f32), ((total, tile), f32), (...  2.16 us
    pallas_call x1, Pallas kernels, body(): call(first_kernel, [((levels, cells), bf16), ((senders * MESSAGE, tile),...  1.48 us
  transfers between devices with their start and end apart: 8, of which 2 were waited for; matrix products, arithmetic and copies ran while one was open for 4% of the time, Pallas kernels for 4%

profile of v2, /device:TPU:31, one launch (start us, length us, event | category | flops | bytes accessed | tf_op | source)
XLA Modules:
  0.0 67.6 jit_solution(16066658546281428663)
XLA Ops:
  0.6 0.8 %copy.11.lists_ref = s32[64,2]{1,0:T(8,128)S(1)} copy(s32[64,2]{0,1:T(2,128)} %bitcast.54) | data formatting | bytes 1024 | tf_op jit(solution)/shard_map/reshape | solution.py:286
  1.4 1.2 %copy-done.2 = bf16[1,128,32,128]{3,2,1,0:T(8,128)(2,1)S(1)} copy-done((bf16[1,128,32,128]{3,2,1,0:T(8,128)(2,1)S(1)}, bf16[1,128,32,128]{3,2,1,0:T(8,128)(2,1)}, u32[]{:S(2)}) %copy-start.2) | copy-done | bytes 1048600
  2.6 0.9 %select_tiles.1 = (bf16[128,128]{1,0:T(8,128)(2,1)}, f32[32,128]{1,0:T(8,128)S(1)}) custom-call(bf16[1,128,32,128]{3,2,1,0:T(8,128)(2,1)S(1)} %copy-done.2, s32[64,2]{1,0:T(8,128)S(1)} %copy.11.lists_ref), custom_call_target="tpu_custom_call" | custom-call | bytes 1048576 | tf_op jit(solution)/shard_map/select_tiles/pallas_call | solution.py:300
  3.6 14.4 %all-to-all-start = ((bf16[64,2,128]{2,1,0:T(2,128)(2,1)}), bf16[64,2,128]{2,1,0:T(2,128)(2,1)S(1)}, u32[]{:S(2)}, u32[]{:S(2)}) async-start(bf16[64,2,128]{2,1,0:T(2,128)(2,1)} %bitcast.1), calls=%async_computation | async-start | bytes 65536 | tf_op jit(solution)/shard_map/all_to_all | solution.py:306
  17.9 0.8 %copy.12.sources.refs_4_ = s32[32,2]{1,0:T(8,128)S(1)} copy(s32[32,2]{0,1:T(2,128)} %bitcast.55) | data formatting | bytes 512 | tf_op jit(solution)/shard_map/reshape | solution.py:285
  18.7 1.6 %copy-done = bf16[1,1,1,32,2,128,128]{6,5,4,3,2,1,0:T(8,128)(2,1)S(1)} copy-done((bf16[1,1,1,32,2,128,128]{6,5,4,3,2,1,0:T(8,128)(2,1)S(1)}, bf16[1,1,1,32,2,128,128]{6,5,4,3,2,1,0:T(8,128)(2,1)}, u32[]{:S(2)}) %copy-start) | copy-done | bytes 2097176
  20.3 0.7 %copy-done.6 = f32[1,32,128]{2,1,0:T(8,128)S(1)} copy-done((f32[1,32,128]{2,1,0:T(8,128)S(1)}, f32[1,32,128]{2,1,0:T(8,128)}, u32[]{:S(2)}) %copy-start.6) | copy-done | bytes 16408
  21.0 0.7 %copy-done.8 = s32[1,32,128]{2,1,0:T(8,128)S(1)} copy-done((s32[1,32,128]{2,1,0:T(8,128)S(1)}, s32[1,32,128]{2,1,0:T(8,128)}, u32[]{:S(2)}) %copy-start.8) | copy-done | bytes 16408
  21.7 0.7 %copy-done.10 = f32[1,32,128]{2,1,0:T(8,128)S(1)} copy-done((f32[1,32,128]{2,1,0:T(8,128)S(1)}, f32[1,32,128]{2,1,0:T(8,128)}, u32[]{:S(2)}) %copy-start.10) | copy-done | bytes 16408
  22.4 0.9 %edge_rows.1 = (f32[808,128]{1,0:T(8,128)}, f32[808,128]{1,0:T(8,128)}) custom-call(f32[32,128]{1,0:T(8,128)S(1)} %bitcast.38, f32[32,128]{1,0:T(8,128)S(1)} %bitcast.45, s32[32,128]{1,0:T(8,128)S(1)} %bitcast.41, f32[32,128]{1,0:T(8,128)S(1)} %get-tuple-element.17.lowest_ref.refs_3_, s32[32,2]{1,0:T(8,128)S(1)} %copy.12.sources.refs_4_, ...), custom_call_target="tpu_custom_call" | custom-call | bytes 1048576 | tf_op jit(solution)/shard_map/edge_rows/pallas_call | solution.py:313
  23.4 3.2 %collective-permute-start = (f32[808,128]{1,0:T(8,128)}, f32[808,128]{1,0:T(8,128)}, u32[]{:S(2)}, u32[]{:S(2)}) collective-permute-start(f32[808,128]{1,0:T(8,128)} %get-tuple-element.23), channel_id=1, source_target_pairs={{384,392},{392,400},{400,408},{408,416},{416,424},{424,432},{432,4... | collective-permute-start | bytes 1241096 | tf_op jit(solution)/shard_map/ppermute | solution.py:298
  26.6 4.3 %collective-permute-start.1 = (f32[808,128]{1,0:T(8,128)}, f32[808,128]{1,0:T(8,128)}, u32[]{:S(2)}, u32[]{:S(2)}) collective-permute-start(f32[808,128]{1,0:T(8,128)} %get-tuple-element.24), channel_id=1, source_target_pairs={{392,384},{400,392},{408,400},{416,408},{424,416},{432,424},{440,4... | collective-permute-start | bytes 1241096 | tf_op jit(solution)/shard_map/ppermute | solution.py:298
  30.9 0.5 copy.21
  31.4 0.0 all-to-all-done
  31.5 1.5 %first_step.1 = (bf16[128,4096]{1,0:T(8,128)(2,1)S(1)}, bf16[384,128]{1,0:T(8,128)(2,1)}, bf16[32,128]{1,0:T(8,128)(2,1)S(1)}, f32[32,128]{1,0:T(8,128)S(1)}) custom-call(bf16[128,128]{1,0:T(8,128)(2,1)S(1)} %bitcast.47, s32[32,2]{1,0:T(8,128)S(1)} %copy.12.sources.refs_4_, bf16[32,2,128,128]{3,2,1,0:T(8,128)(2,1)S(1)} %bitcast.31, ...), custom_call_target="tpu_custom_call" | custom-call | flops 1073741824 | bytes 1048576 | tf_op jit(solution)/shard_map/first_step/pallas_call | solution.py:323
  33.0 1.0 %copy-done.13 = bf16[128,4096]{1,0:T(8,128)(2,1)} copy-done((bf16[128,4096]{1,0:T(8,128)(2,1)}, bf16[128,4096]{1,0:T(8,128)(2,1)S(1)}, u32[]{:S(2)}) %copy-start.13) | copy-done | bytes 1048600
  33.9 9.2 %all-to-all-start.1 = ((bf16[192,2,128]{2,1,0:T(2,128)(2,1)}), bf16[192,2,128]{2,1,0:T(2,128)(2,1)S(1)}, u32[]{:S(2)}, u32[]{:S(2)}) async-start(bf16[192,2,128]{2,1,0:T(2,128)(2,1)} %bitcast.7), calls=%async_computation.1 | async-start | bytes 196608 | tf_op jit(solution)/shard_map/all_to_all | solution.py:338
  43.2 1.2 %copy-done.5 = bf16[16,8,32,128]{3,1,2,0:T(8,128)(2,1)S(1)} copy-done((bf16[16,8,32,128]{3,1,2,0:T(8,128)(2,1)S(1)}, bf16[16,8,32,128]{3,1,2,0:T(8,128)(2,1)}, u32[]{:S(2)}) %copy-start.5) | copy-done | bytes 1048600
  44.4 1.2 %copy-done.14 = bf16[128,4096]{1,0:T(8,128)(2,1)S(1)} copy-done((bf16[128,4096]{1,0:T(8,128)(2,1)S(1)}, bf16[128,4096]{1,0:T(8,128)(2,1)}, u32[]{:S(2)}) %copy-start.14) | copy-done | bytes 1048600
  45.6 0.1 second_step.1
  45.7 3.1 %collective-permute-start.2 = (f32[8,128]{1,0:T(8,128)S(1)}, f32[8,128]{1,0:T(8,128)S(1)}, u32[]{:S(2)}, u32[]{:S(2)}) collective-permute-start(f32[8,128]{1,0:T(8,128)S(1)} %get-tuple-element.25), channel_id=1, source_target_pairs={{384,392},{392,400},{400,408},{408,416},{416,424},{424,432},{432,4... | collective-permute-start | bytes 12296 | tf_op jit(solution)/shard_map/ppermute | solution.py:298
  48.8 4.3 %collective-permute-start.3 = (f32[8,128]{1,0:T(8,128)S(1)}, f32[8,128]{1,0:T(8,128)S(1)}, u32[]{:S(2)}, u32[]{:S(2)}) collective-permute-start(f32[8,128]{1,0:T(8,128)S(1)} %get-tuple-element.26), channel_id=1, source_target_pairs={{392,384},{400,392},{408,400},{416,408},{424,416},{432,424},{440,4... | collective-permute-start | bytes 12296 | tf_op jit(solution)/shard_map/ppermute | solution.py:298
  53.1 0.0 collective-permute-done.2.forcing_above
  53.1 0.7 %collective-permute-done.3.forcing_below = f32[8,128]{1,0:T(8,128)S(1)} collective-permute-done((f32[8,128]{1,0:T(8,128)S(1)}, f32[8,128]{1,0:T(8,128)S(1)}, u32[]{:S(2)}, u32[]{:S(2)}) %collective-permute-start.3) | collective-permute-done | bytes 4128 | tf_op jit(solution)/shard_map/ppermute | solution.py:298
  53.8 0.0 collective-permute-done.1.still_below
  53.9 2.2 %second_import.1 = (f32[5,48,128]{2,1,0:T(8,128)S(1)}, f32[48,128]{1,0:T(8,128)S(1)}, f32[48,128]{1,0:T(8,128)S(1)}) custom-call(bf16[384,128]{1,0:T(8,128)(2,1)S(1)} %bitcast.37, s32[32,2]{1,0:T(8,128)S(1)} %copy.12.sources.refs_4_, bf16[32,2,128,128]{3,2,1,0:T(8,128)(2,1)S(1)} %bitcast.32, f32[32,128]{1,0:T(8,128)S(1)} %get-tuple-element.17.lowest_ref.refs_3_, ...), custom_call_target="tpu_custom_call" | custom-call | bytes 1048576 | tf_op jit(solution)/shard_map/second_import/pallas_call | solution.py:349
  56.0 4.4 %collective-permute-start.4 = (f32[48,128]{1,0:T(8,128)S(1)}, f32[48,128]{1,0:T(8,128)S(1)}, u32[]{:S(2)}, u32[]{:S(2)}) collective-permute-start(f32[48,128]{1,0:T(8,128)S(1)} %get-tuple-element.28), channel_id=1, source_target_pairs={{384,385},{385,386},{386,387},{387,388},{388,389},{389,390},{390,3... | collective-permute-start | bytes 73736 | tf_op jit(solution)/shard_map/ppermute | solution.py:298
  60.5 1.9 %collective-permute-start.5 = (f32[48,128]{1,0:T(8,128)S(1)}, f32[48,128]{1,0:T(8,128)S(1)}, u32[]{:S(2)}, u32[]{:S(2)}) collective-permute-start(f32[48,128]{1,0:T(8,128)S(1)} %get-tuple-element.29), channel_id=1, source_target_pairs={{385,384},{386,385},{387,386},{388,387},{389,388},{390,389},{391,3... | collective-permute-start | bytes 73736 | tf_op jit(solution)/shard_map/ppermute | solution.py:298
  62.4 1.2 %copy.18 = bf16[16,8,32,128]{3,2,1,0:T(8,128)(2,1)} copy(bf16[16,8,32,128]{3,1,2,0:T(8,128)(2,1)S(1)} %bitcast.34) | data formatting | bytes 2097152
  63.6 0.0 collective-permute-done.4.from_left
  63.6 2.7 %collective-permute-done.5.from_right = f32[48,128]{1,0:T(8,128)S(1)} collective-permute-done((f32[48,128]{1,0:T(8,128)S(1)}, f32[48,128]{1,0:T(8,128)S(1)}, u32[]{:S(2)}, u32[]{:S(2)}) %collective-permute-start.5) | collective-permute-done | bytes 24608 | tf_op jit(solution)/shard_map/ppermute | solution.py:298
  66.2 1.4 %passes.1 = f32[32,128]{1,0:T(8,128)} custom-call(f32[5,48,128]{2,1,0:T(8,128)S(1)} %get-tuple-element.27.wide, f32[48,128]{1,0:T(8,128)S(1)} %collective-permute-done.4.from_left, f32[48,128]{1,0:T(8,128)S(1)} %collective-permute-done.5.from_right, f32[32,128]{1,0:T(8,128)S(1)} %bitcast.40), custom_call_target="tpu_custom_call" | custom-call | bytes 1048576 | tf_op jit(solution)/shard_map/passes/pallas_call | solution.py:359
  (28 shorter events, 0.1 us)
Async XLA Ops:
  1.4 1.2 %copy-start.2 = (bf16[1,128,32,128]{3,2,1,0:T(8,128)(2,1)S(1)}, bf16[1,128,32,128]{3,2,1,0:T(8,128)(2,1)}, u32[]{:S(2)}) copy-start(bf16[1,128,32,128]{3,2,1,0:T(8,128)(2,1)} %level_ref.1) | copy-start | bytes 3145732
  3.6 27.9 %all-to-all-start = ((bf16[64,2,128]{2,1,0:T(2,128)(2,1)}), bf16[64,2,128]{2,1,0:T(2,128)(2,1)S(1)}, u32[]{:S(2)}, u32[]{:S(2)}) async-start(bf16[64,2,128]{2,1,0:T(2,128)(2,1)} %bitcast.1), calls=%async_computation | async-start | bytes 65536 | tf_op jit(solution)/shard_map/all_to_all | solution.py:306
  18.7 1.6 %copy-start = (bf16[1,1,1,32,2,128,128]{6,5,4,3,2,1,0:T(8,128)(2,1)S(1)}, bf16[1,1,1,32,2,128,128]{6,5,4,3,2,1,0:T(8,128)(2,1)}, u32[]{:S(2)}) copy-start(bf16[1,1,1,32,2,128,128]{6,5,4,3,2,1,0:T(8,128)(2,1)} %param.15) | copy-start | bytes 6291460
  20.3 0.7 %copy-start.6 = (f32[1,32,128]{2,1,0:T(8,128)S(1)}, f32[1,32,128]{2,1,0:T(8,128)}, u32[]{:S(2)}) copy-start(f32[1,32,128]{2,1,0:T(8,128)} %param.10) | copy-start | bytes 49156
  21.0 0.7 %copy-start.8 = (s32[1,32,128]{2,1,0:T(8,128)S(1)}, s32[1,32,128]{2,1,0:T(8,128)}, u32[]{:S(2)}) copy-start(s32[1,32,128]{2,1,0:T(8,128)} %param.12) | copy-start | bytes 49156
  21.7 0.7 %copy-start.10 = (f32[1,32,128]{2,1,0:T(8,128)S(1)}, f32[1,32,128]{2,1,0:T(8,128)}, u32[]{:S(2)}) copy-start(f32[1,32,128]{2,1,0:T(8,128)} %param.11) | copy-start | bytes 49156
  22.4 8.5 %copy-start.15 = (s32[1,32,128]{2,1,0:T(8,128)S(1)}, s32[1,32,128]{2,1,0:T(8,128)}, u32[]{:S(2)}) copy-start(s32[1,32,128]{2,1,0:T(8,128)} %param.13) | copy-start | bytes 49156
  22.4 8.5 %copy-start.3 = (bf16[1,128,32,128]{3,2,1,0:T(8,128)(2,1)S(1)}, bf16[1,128,32,128]{3,2,1,0:T(8,128)(2,1)}, u32[]{:S(2)}) copy-start(bf16[1,128,32,128]{3,2,1,0:T(8,128)(2,1)} %level_ref.1) | copy-start | bytes 3145732
  22.4 9.0 %copy-start.12 = (bf16[1,2,128,128]{3,2,1,0:T(8,128)(2,1)S(1)}, bf16[1,2,128,128]{3,2,1,0:T(8,128)(2,1)}, u32[]{:S(2)}) copy-start(bf16[1,2,128,128]{3,2,1,0:T(8,128)(2,1)} %param.14) | copy-start | bytes 196612
  23.4 8.1 %copy-start.1 = (bf16[1,1,1,32,2,128,128]{6,5,4,3,2,1,0:T(8,128)(2,1)S(1)}, bf16[1,1,1,32,2,128,128]{6,5,4,3,2,1,0:T(8,128)(2,1)}, u32[]{:S(2)}) copy-start(bf16[1,1,1,32,2,128,128]{6,5,4,3,2,1,0:T(8,128)(2,1)} %param.15) | copy-start | bytes 6291460
  23.4 8.1 %copy-start.9 = (s32[1,32,128]{2,1,0:T(8,128)S(1)}, s32[1,32,128]{2,1,0:T(8,128)}, u32[]{:S(2)}) copy-start(s32[1,32,128]{2,1,0:T(8,128)} %param.12) | copy-start | bytes 49156
  23.4 30.5 %collective-permute-start = (f32[808,128]{1,0:T(8,128)}, f32[808,128]{1,0:T(8,128)}, u32[]{:S(2)}, u32[]{:S(2)}) collective-permute-start(f32[808,128]{1,0:T(8,128)} %get-tuple-element.23), channel_id=1, source_target_pairs={{384,392},{392,400},{400,408},{408,416},{416,424},{424,432},{432,4... | collective-permute-start | bytes 1241096 | tf_op jit(solution)/shard_map/ppermute | solution.py:298
  26.6 27.2 %collective-permute-start.1 = (f32[808,128]{1,0:T(8,128)}, f32[808,128]{1,0:T(8,128)}, u32[]{:S(2)}, u32[]{:S(2)}) collective-permute-start(f32[808,128]{1,0:T(8,128)} %get-tuple-element.24), channel_id=1, source_target_pairs={{392,384},{400,392},{408,400},{416,408},{424,416},{432,424},{440,4... | collective-permute-start | bytes 1241096 | tf_op jit(solution)/shard_map/ppermute | solution.py:298
  31.4 2.5 %copy-start.4 = (bf16[16,8,32,128]{3,1,2,0:T(8,128)(2,1)}, bf16[16,8,32,128]{3,1,2,0:T(8,128)(2,1)S(1)}, u32[]{:S(2)}) copy-start(bf16[16,8,32,128]{3,1,2,0:T(8,128)(2,1)S(1)} %copy.21) | copy-start | bytes 3145732
  33.0 1.0 %copy-start.13 = (bf16[128,4096]{1,0:T(8,128)(2,1)}, bf16[128,4096]{1,0:T(8,128)(2,1)S(1)}, u32[]{:S(2)}) copy-start(bf16[128,4096]{1,0:T(8,128)(2,1)S(1)} %get-tuple-element.18.state) | copy-start | bytes 3145732
  33.9 19.9 %all-to-all-start.1 = ((bf16[192,2,128]{2,1,0:T(2,128)(2,1)}), bf16[192,2,128]{2,1,0:T(2,128)(2,1)S(1)}, u32[]{:S(2)}, u32[]{:S(2)}) async-start(bf16[192,2,128]{2,1,0:T(2,128)(2,1)} %bitcast.7), calls=%async_computation.1 | async-start | bytes 196608 | tf_op jit(solution)/shard_map/all_to_all | solution.py:338
  43.2 1.2 %copy-start.5 = (bf16[16,8,32,128]{3,1,2,0:T(8,128)(2,1)S(1)}, bf16[16,8,32,128]{3,1,2,0:T(8,128)(2,1)}, u32[]{:S(2)}) copy-start(bf16[16,8,32,128]{3,1,2,0:T(8,128)(2,1)} %copy-done.4) | copy-start | bytes 3145732
  44.4 1.2 %copy-start.14 = (bf16[128,4096]{1,0:T(8,128)(2,1)S(1)}, bf16[128,4096]{1,0:T(8,128)(2,1)}, u32[]{:S(2)}) copy-start(bf16[128,4096]{1,0:T(8,128)(2,1)} %copy-done.13) | copy-start | bytes 3145732
  45.6 8.2 %copy-start.7 = (f32[1,32,128]{2,1,0:T(8,128)S(1)}, f32[1,32,128]{2,1,0:T(8,128)}, u32[]{:S(2)}) copy-start(f32[1,32,128]{2,1,0:T(8,128)} %param.10) | copy-start | bytes 49156
  45.6 8.2 %copy-start.11 = (f32[1,32,128]{2,1,0:T(8,128)S(1)}, f32[1,32,128]{2,1,0:T(8,128)}, u32[]{:S(2)}) copy-start(f32[1,32,128]{2,1,0:T(8,128)} %param.11) | copy-start | bytes 49156
  45.7 7.4 %collective-permute-start.2 = (f32[8,128]{1,0:T(8,128)S(1)}, f32[8,128]{1,0:T(8,128)S(1)}, u32[]{:S(2)}, u32[]{:S(2)}) collective-permute-start(f32[8,128]{1,0:T(8,128)S(1)} %get-tuple-element.25), channel_id=1, source_target_pairs={{384,392},{392,400},{400,408},{408,416},{416,424},{424,432},{432,4... | collective-permute-start | bytes 12296 | tf_op jit(solution)/shard_map/ppermute | solution.py:298
  48.8 5.0 %collective-permute-start.3 = (f32[8,128]{1,0:T(8,128)S(1)}, f32[8,128]{1,0:T(8,128)S(1)}, u32[]{:S(2)}, u32[]{:S(2)}) collective-permute-start(f32[8,128]{1,0:T(8,128)S(1)} %get-tuple-element.26), channel_id=1, source_target_pairs={{392,384},{400,392},{408,400},{416,408},{424,416},{432,424},{440,4... | collective-permute-start | bytes 12296 | tf_op jit(solution)/shard_map/ppermute | solution.py:298
  56.0 7.5 %collective-permute-start.4 = (f32[48,128]{1,0:T(8,128)S(1)}, f32[48,128]{1,0:T(8,128)S(1)}, u32[]{:S(2)}, u32[]{:S(2)}) collective-permute-start(f32[48,128]{1,0:T(8,128)S(1)} %get-tuple-element.28), channel_id=1, source_target_pairs={{384,385},{385,386},{386,387},{387,388},{388,389},{389,390},{390,3... | collective-permute-start | bytes 73736 | tf_op jit(solution)/shard_map/ppermute | solution.py:298
  60.5 5.8 %collective-permute-start.5 = (f32[48,128]{1,0:T(8,128)S(1)}, f32[48,128]{1,0:T(8,128)S(1)}, u32[]{:S(2)}, u32[]{:S(2)}) collective-permute-start(f32[48,128]{1,0:T(8,128)S(1)} %get-tuple-element.29), channel_id=1, source_target_pairs={{385,384},{386,385},{387,386},{388,387},{389,388},{390,389},{391,3... | collective-permute-start | bytes 73736 | tf_op jit(solution)/shard_map/ppermute | solution.py:298

commit v3 on v2

v3 whole, which is shorter than its diff:
```python
import functools

import jax
import jax.numpy as jnp
from jax import lax
from jax.experimental import pallas as pl
from jax.experimental.pallas import tpu as pltpu
from jax.sharding import PartitionSpec as P

PHYS = 4
PASSES = 4
HALO = 8
NEAR = 3
PLANES = 5
WIDTH = 2048
MESSAGE = 6
bf16 = jnp.bfloat16
f32 = jnp.float32
HBM = pltpu.HBM
VMEM = pltpu.VMEM
VMEM_LIMIT = 16 * 1024 * 1024


def call(kernel, name, operands, outs, scratch=(), flops=0):
    values, specs = [], []
    for operand in operands:
        value, place = operand if isinstance(operand, tuple) else (operand, None)
        if place is not None:
            value = pltpu.with_memory_space_constraint(value, place)
        values.append(value)
        specs.append(pl.BlockSpec(memory_space=HBM if place is HBM else VMEM))
    shapes = [
        out[2](out[0], out[1]) if len(out) > 2 else jax.ShapeDtypeStruct(out[0], out[1]) for out in outs
    ]
    return pl.pallas_call(
        kernel,
        out_shape=shapes,
        in_specs=specs,
        out_specs=[pl.BlockSpec(memory_space=out[2] if len(out) > 2 else VMEM) for out in outs],
        scratch_shapes=list(scratch),
        name=name,
        cost_estimate=pl.CostEstimate(flops=flops, bytes_accessed=1 << 20, transcendentals=0),
        compiler_params=pltpu.CompilerParams(vmem_limit_bytes=VMEM_LIMIT),
    )(*values)


def fetch(sems, *pairs):
    copies = [pltpu.make_async_copy(source, target, sems.at[n]) for n, (source, target) in enumerate(pairs)]
    for copy in copies:
        copy.start()
    return copies


def is_ocean():
    return lax.axis_index("sec") == lax.axis_size("sec") - 1


def is_even(axis):
    return lax.rem(lax.axis_index(axis), 2) == 0


def iota(shape, dim):
    return lax.broadcasted_iota(jnp.int32, shape, dim)


def one_hot(flags):
    return jnp.where(flags, 1.0, 0.0).astype(bf16)


def spread(rows, column, odd):
    hot = one_hot(iota((column.shape[0], rows.shape[1]), 1) == column)
    values = rows.astype(f32).astype(bf16)
    both = lax.dot_general(hot, values, (((1,), (1,)), ((), ())), preferred_element_type=f32)
    return jnp.where(odd == 1, both[:, 1:2], both[:, 0:1]).astype(jnp.int32)


def upright(rows, first=0, count=None):
    count = rows.shape[1] if count is None else count
    unit = one_hot(iota((count, rows.shape[1]), 0) + first == iota((count, rows.shape[1]), 1))
    values = rows.astype(f32).astype(bf16)
    turned = lax.dot_general(unit, values, (((1,), (1,)), ((), ())), preferred_element_type=f32)
    return turned.astype(jnp.int32)


def select_kernel(profile, lists_ref, out_ref, tiles_v, lists_v, sems):
    copies = fetch(sems, (lists_ref, lists_v), (profile.at[0, 0], tiles_v))
    row = iota((out_ref.shape[0], 1), 0)
    copies[0].wait()
    tile = spread(lists_v[...], row >> 1, row & 1)
    hot = one_hot(iota((out_ref.shape[0], tiles_v.shape[0]), 1) == tile)
    copies[1].wait()
    out_ref[...] = jnp.dot(hot, tiles_v[...], preferred_element_type=f32).astype(bf16)


def edges_kernel(
    surface, diffusion, sea, profile, sources, weights, to_a, to_b,
    surface_v, diffusion_v, sea_v, level_v, sources_v, weights_v, sems,
):
    @pl.when(is_ocean())
    def _():
        rows, size = surface_v.shape
        even = is_even("gx")
        near = jnp.where(even, rows - NEAR, 0)
        copies = fetch(
            sems,
            (surface, surface_v),
            (diffusion, diffusion_v),
            (sea, sea_v),
            (profile.at[0, 0], level_v),
            (sources, sources_v),
            (weights.at[pl.ds(near, NEAR)], weights_v.at[0]),
            (weights.at[pl.ds(rows - NEAR - near, NEAR)], weights_v.at[1]),
        )
        for copy in copies:
            copy.wait()
        first = jnp.where(even, rows - HALO, 0)
        lowest = level_v[...].astype(f32)
        for n, (out, start) in enumerate(((to_a, first), (to_b, rows - HALO - first))):
            part = pl.ds(pl.multiple_of(start, HALO), HALO)
            out[0:HALO] = surface_v[part]
            out[HALO : 2 * HALO] = diffusion_v[part]
            out[2 * HALO : 3 * HALO] = sea_v[part].astype(f32)
            out[3 * HALO : 4 * HALO] = jnp.where(start == 0, lowest[0:HALO], lowest[rows - HALO : rows])
            out[4 * HALO : 5 * HALO] = jnp.zeros((HALO, size), f32)
            out[4 * HALO : 4 * HALO + 2, 0:rows] = sources_v[...].astype(f32)
            for a in range(NEAR):
                for k in range(2):
                    base = PLANES * HALO + (2 * a + k) * size
                    out[base : base + size] = weights_v[n, a, k].astype(f32)


def import_row(pick_ref, a, first, second):
    row = pick_ref[a : a + 1, :].astype(bf16)
    block = jnp.concatenate([first, second], axis=1)
    return lax.dot_general(row, block, (((1,), (1,)), ((), ())), preferred_element_type=f32)


def chosen_rows(pick, received, index):
    tile = received.shape[1]
    place = iota((index.shape[0], received.shape[0]), 1)
    for k in range(index.shape[1]):
        hot = one_hot(index[:, k : k + 1] == place)
        pick[:, k * tile : (k + 1) * tile] = jnp.dot(hot, received[...], preferred_element_type=f32)


def substep(x, flag, mix):
    deep = x * flag
    both = jnp.concatenate([x - deep, deep], axis=0)
    mixed = jnp.dot(mix, both, preferred_element_type=f32)
    return (0.5 * x.astype(f32) + jnp.tanh(mixed)).astype(bf16)


def with_bottom(x, bottom):
    top = x[0:16].astype(f32)
    top = jnp.where(iota(top.shape, 0) == 0, bottom, top).astype(bf16)
    return jnp.concatenate([top, x[16:]], axis=0)


def flat_rows(grid, first, count):
    return jnp.concatenate([grid[first + r : first + r + 1] for r in range(count)], axis=1)


def first_kernel(
    received, sources, weights, sea, x_ref, flag_ref, mixing, lists_ref, profile,
    message, carry, pick, low_f, level_v, carry_v, sems,
):
    tile = received.shape[1]
    (level,) = fetch(sems, (profile.at[0, 0], level_v))
    chosen_rows(pick, received, upright(sources[...]))
    for a in range(carry_v.shape[0]):
        carry_v[a : a + 1, :] = import_row(pick, a, weights[a, 0], weights[a, 1])
    level.wait()
    lowest = level_v[...].astype(f32)
    flux = sea[...].astype(f32) * (carry_v[...] - lowest)
    kept = pltpu.make_async_copy(carry_v, carry, sems.at[1])

    @pl.when(is_ocean())
    def _():
        carry_v[...] = flux * (1.0 / PASSES)
        kept.start()
        message[...] = jnp.zeros(message.shape, bf16)

    @pl.when(jnp.logical_not(is_ocean()))
    def _():
        kept.start()
        mix = jnp.concatenate([mixing[0], mixing[1]], axis=1)
        bottom = (lowest + flux).astype(bf16).astype(f32)
        per = WIDTH // tile
        for c in range(x_ref.shape[1] // WIDTH):
            cols = slice(c * WIDTH, (c + 1) * WIDTH)
            flag = flag_ref[:, cols]
            x = with_bottom(x_ref[:, cols], flat_rows(bottom, c * per, per))
            for _ in range(PHYS - 1):
                x = substep(x, flag, mix)
            deep = x * flag
            both = jnp.concatenate([x - deep, deep], axis=0)
            mixed = jnp.dot(mix[0:16], both, preferred_element_type=f32)
            last = 0.5 * x[0:16].astype(f32) + jnp.tanh(mixed)
            for r in range(per):
                low_f[c * per + r : c * per + r + 1, :] = last[0:1, r * tile : (r + 1) * tile]
        row = iota((message.shape[0], 1), 0)
        target = (row * 10923) >> 16
        m = row - MESSAGE * target
        wanted = spread(lists_ref[...], target - 1 + (m >> 1), m & 1)
        hot = one_hot(iota((message.shape[0], low_f.shape[0]), 1) == wanted)
        tiles = low_f[...].astype(bf16)
        message[...] = jnp.dot(hot, tiles, preferred_element_type=f32).astype(bf16)

    kept.wait()


def second_kernel(
    carry, x_ref, sea, flag_ref, mixing,
    out, to_a, to_b,
    carry_v, x_v, sea_v, flag_v, mixing_v, sems,
):
    rows = carry_v.shape[0]

    @pl.when(is_ocean())
    def _():
        copies = fetch(sems, (carry, carry_v), (x_ref, out))
        copies[0].wait()
        even = is_even("gx")
        top, bottom = carry_v[0:HALO], carry_v[rows - HALO : rows]
        to_a[...] = jnp.where(even, bottom, top)
        to_b[...] = jnp.where(even, top, bottom)
        copies[1].wait()

    @pl.when(jnp.logical_not(is_ocean()))
    def _():
        pairs = ((carry, carry_v), (sea, sea_v), (mixing, mixing_v), (flag_ref, flag_v), (x_ref, x_v))
        for copy in fetch(sems, *pairs):
            copy.wait()
        mix = jnp.concatenate([mixing_v[0], mixing_v[1]], axis=1)
        sea_f = sea_v[...].astype(f32)
        imported = carry_v[...]
        per = WIDTH // carry_v.shape[1]
        for c in range(x_v.shape[1] // WIDTH):
            cols = slice(c * WIDTH, (c + 1) * WIDTH)
            flag = flag_v[:, cols]
            x = x_v[:, cols]
            wet = flat_rows(sea_f, c * per, per)
            brought = flat_rows(imported, c * per, per)
            for _ in range(2):
                low = x[0:16].astype(f32)[0:1]
                x = with_bottom(x, (low + wet * (brought - low)).astype(bf16).astype(f32))
                for _ in range(PHYS):
                    x = substep(x, flag, mix)
            out[:, cols] = x


def third_kernel(
    received, sources, weights, sea, surface, diffusion, forcing_a, forcing_b,
    profile, forcing, still_a, still_b,
    wide, to_a, to_b,
    pick, imported, level_v, forcing_v, above_v, below_v, sems,
):
    @pl.when(is_ocean())
    def _():
        rows, tile = surface.shape
        even = is_even("gx")
        odd = jnp.logical_not(even)

        @pl.when(even)
        def _():
            fetch(sems, (still_a, below_v), (still_b, above_v))

        @pl.when(odd)
        def _():
            fetch(sems, (still_b, below_v), (still_a, above_v))

        level = pltpu.make_async_copy(profile.at[0, 0], level_v, sems.at[2])
        held = pltpu.make_async_copy(forcing, forcing_v, sems.at[3])
        level.start()
        held.start()

        def places(rows_of, first, count, offset):
            q = upright(rows_of, first, count)
            return (q >> 1) * MESSAGE + (q & 1) + offset

        chosen_rows(pick.at[0:rows], received, places(sources[...], 0, rows, 2))
        for a in range(rows):
            imported[a : a + 1, :] = import_row(pick, a, weights[a, 0], weights[a, 1])
        for n, buffer in enumerate((below_v, above_v)):
            pltpu.make_async_copy(still_a, buffer, sems.at[n]).wait()
        level.wait()
        held.wait()
        part = slice(4 * HALO, 4 * HALO + 2)
        below = places(below_v[part, 0:rows].astype(jnp.int32), 0, HALO, 4)
        above = places(above_v[part, 0:rows].astype(jnp.int32), rows - HALO, HALO, 0)
        total = rows + 2 * HALO
        chosen_rows(pick.at[rows:total], received, jnp.concatenate([below, above], axis=0))
        imported[rows:total] = jnp.zeros((2 * HALO, tile), f32)
        for still, first in ((below_v, rows), (above_v, total - NEAR)):
            for n in range(NEAR):
                base = PLANES * HALO + 2 * n * tile
                blocks = [still[base + k * tile : base + (k + 1) * tile, :].astype(bf16) for k in range(2)]
                a = first + n
                imported[a : a + 1, :] = import_row(pick, a, blocks[0], blocks[1])

        def plane(own, p):
            part = slice(p * HALO, (p + 1) * HALO)
            return jnp.concatenate([own, below_v[part], above_v[part]], axis=0)

        sea_all = plane(sea[...].astype(f32), 2)
        lowest = plane(level_v[...].astype(f32), 3)
        beyond = (jnp.where(even, forcing_a[...], forcing_b[...]), jnp.where(even, forcing_b[...], forcing_a[...]))
        planes = [
            jnp.concatenate([forcing_v[...], *beyond], axis=0),
            sea_all * (imported[...] - lowest) * (1.0 / PASSES),
            plane(surface[...], 0),
            plane(diffusion[...], 1),
            sea_all,
        ]
        group = iota((total, tile), 1) >> 3
        right = left = planes[0]
        for p, values in enumerate(planes):
            wide[p] = values
            if p:
                right = jnp.where(group == tile // HALO - 1 - p, pltpu.roll(values, tile - HALO * p, 1), right)
                left = jnp.where(group == p, pltpu.roll(values, HALO * p, 1), left)
        even = is_even("gy")
        to_a[...] = jnp.where(even, right, left)
        to_b[...] = jnp.where(even, left, right)


def fourth_kernel(wide, from_a, from_b, surface, out, sems):
    @pl.when(jnp.logical_not(is_ocean()))
    def _():
        fetch(sems, (surface, out))[0].wait()

    @pl.when(is_ocean())
    def _():
        rows, tile = out.shape
        total = wide.shape[1]
        group = iota((total, tile), 1) >> 3
        even = is_even("gy")
        from_right = jnp.where(even, from_a[...], from_b[...])
        from_left = jnp.where(even, from_b[...], from_a[...])
        fields = []
        for p in range(PLANES):
            right, left = from_right, from_left
            if p:
                right = pltpu.roll(right, tile - HALO * p, 1)
                left = pltpu.roll(left, HALO * p, 1)
            beside = jnp.where(group == 0, right, jnp.where(group == tile // HALO - 1, left, 0.0))
            fields.append(jnp.concatenate([wide[p], beside], axis=1))
        forcing_1, forcing_2, height, coefficient, sea = fields
        for forcing in (forcing_1, forcing_2):
            for sweep in range(PASSES):
                around = pltpu.roll(height, total - 1, 0) + pltpu.roll(height, 1, 0)
                around = around + pltpu.roll(height, 2 * tile - 1, 1) + pltpu.roll(height, 1, 1)
                height = sea * (height + coefficient * (around - 4.0 * height) + forcing)
        out[...] = height[0:rows, 0:tile]


def body(
    profile, surface, diffusion, sea_mask, convective, mixing, remap_weights, sources, send_lists
):
    levels, rows, tile = profile.shape[1:]
    cells = rows * tile
    surface_2d = surface.reshape(rows, tile)
    coefficient = diffusion.reshape(rows, tile)
    sea = sea_mask.reshape(rows, tile)
    matrices = mixing.reshape(2, levels, levels)
    weights = remap_weights.reshape(remap_weights.shape[3:])
    wanted = sources.reshape(sources.shape[3:]).T
    lists = send_lists.reshape(send_lists.shape[3:]).T
    slots, senders = lists.shape
    secs = lax.axis_size("sec")
    gx = lax.axis_size("gx")
    gy = lax.axis_size("gy")
    total = rows + 2 * HALO
    grid = (rows, tile)

    def along(axis, count, to_a, to_b):
        base = (secs - 1) * count
        swaps = []
        for start in (0, 1):
            pairs = [(base + i, base + i + 1) for i in range(start, count - 1, 2)]
            swaps.append(pairs + [(t, s) for s, t in pairs])
        return lax.ppermute(to_a, ("sec", axis), swaps[0]), lax.ppermute(to_b, ("sec", axis), swaps[1])

    def semaphores(count):
        return pltpu.SemaphoreType.DMA((count,))

    (chosen,) = call(
        select_kernel,
        "select_tiles",
        [(profile, HBM), (lists, HBM)],
        [((senders * slots, tile), bf16)],
        [VMEM(grid, bf16), VMEM(lists.shape, jnp.int32), semaphores(2)],
    )
    received = lax.all_to_all(chosen.reshape(senders, slots, tile), ("sec", "gx"), 0, 0, tiled=True)

    height = PLANES * HALO + NEAR * 2 * tile
    still_a, still_b = call(
        edges_kernel,
        "edge_rows",
        [(surface_2d, HBM), (coefficient, HBM), (sea, HBM), (profile, HBM), (wanted, HBM), (weights, HBM)],
        [((height, tile), f32)] * 2,
        [
            VMEM(grid, f32),
            VMEM(grid, f32),
            VMEM(grid, jnp.int32),
            VMEM(grid, bf16),
            VMEM(wanted.shape, jnp.int32),
            VMEM((2, NEAR, 2, tile, tile), bf16),
            semaphores(7),
        ],
    )
    still_a, still_b = along("gx", gx, still_a, still_b)

    columns = profile.reshape(levels, cells)
    flag = convective.reshape(1, cells).astype(bf16)
    message, carry = call(
        first_kernel,
        "first_step",
        [
            received.reshape(senders * slots, tile), wanted, weights, sea, (columns, VMEM), flag,
            matrices, lists, (profile, HBM),
        ],
        [((senders * MESSAGE, tile), bf16), (grid, f32, HBM)],
        [VMEM((rows, 2 * tile), f32), VMEM(grid, f32), VMEM(grid, bf16), VMEM(grid, f32), semaphores(2)],
        flops=1 << 34,
    )
    again = lax.all_to_all(
        message.reshape(senders * MESSAGE // 2, 2, tile), ("sec", "gx"), 0, 0, tiled=True
    )
    final, forcing_a, forcing_b = call(
        second_kernel,
        "second_step",
        [(carry, HBM), (columns, HBM), (sea, HBM), (flag, HBM), (matrices, HBM)],
        [((levels, cells), bf16), ((HALO, tile), f32), ((HALO, tile), f32)],
        [
            VMEM(grid, f32),
            VMEM((levels, cells), bf16),
            VMEM(grid, jnp.int32),
            VMEM((1, cells), bf16),
            VMEM(matrices.shape, bf16),
            semaphores(5),
        ],
        flops=1 << 34,
    )
    forcing_a, forcing_b = along("gx", gx, forcing_a, forcing_b)

    wide, to_a, to_b = call(
        third_kernel,
        "second_import",
        [
            again.reshape(senders * MESSAGE, tile), wanted, weights, sea, surface_2d, coefficient,
            forcing_a, forcing_b, (profile, HBM), (carry, HBM), (still_a, HBM), (still_b, HBM),
        ],
        [((PLANES, total, tile), f32), ((total, tile), f32), ((total, tile), f32)],
        [
            VMEM((total, 2 * tile), f32),
            VMEM((total, tile), f32),
            VMEM(grid, bf16),
            VMEM(grid, f32),
            VMEM((height, tile), f32),
            VMEM((height, tile), f32),
            semaphores(4),
        ],
    )
    from_a, from_b = along("gy", gy, to_a, to_b)
    (surface_out,) = call(
        fourth_kernel,
        "passes",
        [wide, from_a, from_b, (surface_2d, HBM)],
        [(grid, f32)],
        [semaphores(1)],
    )
    return (final.reshape(profile.shape), surface_out.reshape(surface.shape))


def solution(mesh):
    return jax.shard_map(
        body,
        mesh=mesh,
        in_specs=(
            P("sec", None, "gx", "gy"),
            P("sec", "gx", "gy"),
            P("sec", "gx", "gy"),
            P("sec", "gx", "gy"),
            P("sec", "gx", "gy"),
            P("sec", None, None, None),
            P("sec", "gx", "gy", None, None, None, None),
            P("sec", "gx", "gy", None, None),
            P("sec", "gx", "gy", None, None),
        ),
        out_specs=(P("sec", None, "gx", "gy"), P("sec", "gx", "gy")),
        check_vma=False,
    )
```

time: 68.3 us -> 61.8 us (0.905)
  the two profiles are of different devices: /device:TPU:31 before, /device:TPU:39 now
where the time goes in v3:
time: 61.8 us; the launch traced here: 61.2 us
  starting transfers between devices  40.8 us (66%)
  Pallas kernels  12 us (19%)
  waiting for transfers between devices  4.54 us (7%)
  local copies, waits for them, and re-layouts  2.95 us (5%)
  between operations  0.95 us (2%)
    all_to_all x1, starting transfers between devices, body(): lax.all_to_all(chosen.reshape(senders, slots, tile), ('sec', 'gx'), 0, 0,...  14.4 us
    pallas_call x6, Pallas kernels, call(): pl.pallas_call(kernel, out_shape=shapes, in_specs=specs, out_specs=[pl.Bl...  12 us
    ppermute x3, starting transfers between devices, along(): lax.ppermute(to_b, ('sec', axis), swaps[1])  11.1 us
    ppermute x3, starting transfers between devices, along(): lax.ppermute(to_a, ('sec', axis), swaps[0])  8.5 us
    all_to_all x1, starting transfers between devices, body(): lax.all_to_all(message.reshape(senders * MESSAGE // 2, 2, tile), ('sec',...  6.86 us
    ppermute x3, waiting for transfers between devices, along(): lax.ppermute(to_b, ('sec', axis), swaps[1])  4.53 us
    unnamed x25, local copies, waits for them, and re-layouts  2.95 us
  transfers between devices with their start and end apart: 8, of which 2 were waited for; matrix products, arithmetic and copies ran while one was open for 5% of the time, Pallas kernels for 10%

profile of v3, /device:TPU:39, one launch (start us, length us, event | category | flops | bytes accessed | tf_op | source)
XLA Modules:
  0.0 61.2 jit_solution(798832899181233565)
XLA Ops:
  0.6 1.7 %select_tiles.1 = bf16[128,128]{1,0:T(8,128)(2,1)} custom-call(bf16[1,128,32,128]{3,2,1,0:T(8,128)(2,1)} %profile.7, s32[2,64]{1,0:T(2,128)} %bitcast.51), custom_call_target="tpu_custom_call" | custom-call | bytes 1048576 | tf_op jit(solution)/shard_map/select_tiles/pallas_call | solution.py:35
  2.4 14.4 %all-to-all-start = ((bf16[64,2,128]{2,1,0:T(2,128)(2,1)}), bf16[64,2,128]{2,1,0:T(2,128)(2,1)S(1)}, u32[]{:S(2)}, u32[]{:S(2)}) async-start(bf16[64,2,128]{2,1,0:T(2,128)(2,1)} %bitcast.2), calls=%async_computation | async-start | bytes 65536 | tf_op jit(solution)/shard_map/all_to_all | solution.py:394
  16.7 0.0 copy-start
  16.8 0.0 copy-start.3
  16.8 0.0 copy-start.7
  16.8 0.0 copy-start.8
  16.8 0.0 copy-start.9
  16.8 2.2 %edge_rows.1 = (f32[808,128]{1,0:T(8,128)}, f32[808,128]{1,0:T(8,128)}) custom-call(f32[32,128]{1,0:T(8,128)} %bitcast.36, f32[32,128]{1,0:T(8,128)} %bitcast.43, s32[32,128]{1,0:T(8,128)} %bitcast.39, bf16[1,128,32,128]{3,2,1,0:T(8,128)(2,1)} %profile.7, s32[2,32]{1,0:T(2,128)} %bitcast.48, bf16[32,2,128,128]{3,2,1,0:T(8,128)(2,1)} %bitcast.29), custom_call_target="tpu_custom_call" | custom-call | bytes 1048576 | tf_op jit(solution)/shard_map/edge_rows/pallas_call | solution.py:35
  19.1 3.1 %collective-permute-start.2 = (f32[808,128]{1,0:T(8,128)}, f32[808,128]{1,0:T(8,128)}, u32[]{:S(2)}, u32[]{:S(2)}) collective-permute-start(f32[808,128]{1,0:T(8,128)} %get-tuple-element.17), channel_id=1, source_target_pairs={{384,392},{400,408},{416,424},{432,440},{448,456},{464,472},{480,4... | collective-permute-start | bytes 1241096 | tf_op jit(solution)/shard_map/ppermute | solution.py:382
  22.2 4.6 %collective-permute-start.3 = (f32[808,128]{1,0:T(8,128)}, f32[808,128]{1,0:T(8,128)}, u32[]{:S(2)}, u32[]{:S(2)}) collective-permute-start(f32[808,128]{1,0:T(8,128)} %get-tuple-element.18), channel_id=1, source_target_pairs={{392,400},{408,416},{424,432},{440,448},{456,464},{472,480},{488,4... | collective-permute-start | bytes 1241096 | tf_op jit(solution)/shard_map/ppermute | solution.py:382
  26.8 1.7 %copy.16 = bf16[16,8,32,128]{3,1,2,0:T(8,128)(2,1)S(1)} copy(bf16[16,8,32,128]{3,2,1,0:T(8,128)(2,1)} %bitcast.55) | data formatting | bytes 2097152
  28.4 0.0 copy-start.1
  28.5 0.0 all-to-all-done
  28.6 2.8 %first_step.1 = (bf16[384,128]{1,0:T(8,128)(2,1)}, f32[32,128]{1,0:T(8,128)}) custom-call(bf16[128,128]{1,0:T(8,128)(2,1)S(1)} %bitcast.45, s32[2,32]{1,0:T(2,128)S(1)} %bitcast.49, bf16[32,2,128,128]{3,2,1,0:T(8,128)(2,1)S(1)} %bitcast.30, s32[32,128]{1,0:T(8,128)S(1)} %bitcast.41, bf16[128,4096]{1,0:T(8,128)(2,1)S(1)} %bitcast.33, ...), custom_call_target="tpu_custom_call" | custom-call | flops 17179869184 | bytes 1048576 | tf_op jit(solution)/shard_map/first_step/pallas_call | solution.py:35
  31.3 6.9 %all-to-all-start.1 = ((bf16[192,2,128]{2,1,0:T(2,128)(2,1)}), bf16[192,2,128]{2,1,0:T(2,128)(2,1)S(1)}, u32[]{:S(2)}, u32[]{:S(2)}) async-start(bf16[192,2,128]{2,1,0:T(2,128)(2,1)} %bitcast.9), calls=%async_computation.1 | async-start | bytes 196608 | tf_op jit(solution)/shard_map/all_to_all | solution.py:427
  38.2 0.0 copy-start.2
  38.2 0.0 copy-start.4
  38.2 0.0 copy-start.5
  38.2 1.3 %second_step.1 = (bf16[128,4096]{1,0:T(8,128)(2,1)S(1)}, f32[8,128]{1,0:T(8,128)S(1)}, f32[8,128]{1,0:T(8,128)S(1)}) custom-call(f32[32,128]{1,0:T(8,128)} %get-tuple-element.12.carry.forcing, bf16[128,4096]{1,0:T(8,128)(2,1)} %bitcast.34, s32[32,128]{1,0:T(8,128)} %bitcast.40, bf16[1,4096]{1,0:T(2,128)(2,1)} %bitcast.47, bf16[2,128,128]{2,1,0:T(8,128)(2,1)} %bitcast.53), custom_call_target="tpu_custom_call" | custom-call | flops 17179869184 | bytes 1048576 | tf_op jit(solution)/shard_map/second_step/pallas_call | solution.py:35
  39.5 3.1 %collective-permute-start = (f32[8,128]{1,0:T(8,128)S(1)}, f32[8,128]{1,0:T(8,128)S(1)}, u32[]{:S(2)}, u32[]{:S(2)}) collective-permute-start(f32[8,128]{1,0:T(8,128)S(1)} %get-tuple-element.15), channel_id=1, source_target_pairs={{384,392},{400,408},{416,424},{432,440},{448,456},{464,472},{480,4... | collective-permute-start | bytes 12296 | tf_op jit(solution)/shard_map/ppermute | solution.py:382
  42.6 4.6 %collective-permute-start.1 = (f32[8,128]{1,0:T(8,128)S(1)}, f32[8,128]{1,0:T(8,128)S(1)}, u32[]{:S(2)}, u32[]{:S(2)}) collective-permute-start(f32[8,128]{1,0:T(8,128)S(1)} %get-tuple-element.16), channel_id=1, source_target_pairs={{392,400},{408,416},{424,432},{440,448},{456,464},{472,480},{488,4... | collective-permute-start | bytes 12296 | tf_op jit(solution)/shard_map/ppermute | solution.py:382
  47.2 1.9 %collective-permute-done.1.forcing_b = f32[8,128]{1,0:T(8,128)S(1)} collective-permute-done((f32[8,128]{1,0:T(8,128)S(1)}, f32[8,128]{1,0:T(8,128)S(1)}, u32[]{:S(2)}, u32[]{:S(2)}) %collective-permute-start.1) | collective-permute-done | bytes 4128 | tf_op jit(solution)/shard_map/ppermute | solution.py:382
  49.1 0.0 all-to-all-done.1
  49.1 0.0 collective-permute-done.2.still_a
  49.1 0.0 collective-permute-done.3.still_b
  49.2 2.6 %second_import.1 = (f32[5,48,128]{2,1,0:T(8,128)S(1)}, f32[48,128]{1,0:T(8,128)S(1)}, f32[48,128]{1,0:T(8,128)S(1)}) custom-call(bf16[384,128]{1,0:T(8,128)(2,1)S(1)} %bitcast.35, s32[2,32]{1,0:T(2,128)S(1)} %bitcast.50, bf16[32,2,128,128]{3,2,1,0:T(8,128)(2,1)S(1)} %bitcast.31, s32[32,128]{1,0:T(8,128)S(1)} %bitcast.42, f32[32,128]{1,0:T(8,128)S(1)} %bitcast.38, ...), custom_call_target="tpu_custom_call" | custom-call | bytes 1048576 | tf_op jit(solution)/shard_map/second_import/pallas_call | solution.py:35
  51.8 2.3 %collective-permute-start.4 = (f32[48,128]{1,0:T(8,128)S(1)}, f32[48,128]{1,0:T(8,128)S(1)}, u32[]{:S(2)}, u32[]{:S(2)}) collective-permute-start(f32[48,128]{1,0:T(8,128)S(1)} %get-tuple-element.20), channel_id=1, source_target_pairs={{384,385},{386,387},{388,389},{390,391},{385,384},{387,386},{389,3... | collective-permute-start | bytes 73736 | tf_op jit(solution)/shard_map/ppermute | solution.py:382
  54.1 1.9 %collective-permute-start.5 = (f32[48,128]{1,0:T(8,128)S(1)}, f32[48,128]{1,0:T(8,128)S(1)}, u32[]{:S(2)}, u32[]{:S(2)}) collective-permute-start(f32[48,128]{1,0:T(8,128)S(1)} %get-tuple-element.21), channel_id=1, source_target_pairs={{385,386},{387,388},{389,390},{386,385},{388,387},{390,389},{393,3... | collective-permute-start | bytes 73736 | tf_op jit(solution)/shard_map/ppermute | solution.py:382
  56.0 1.2 %copy.13 = bf16[16,8,32,128]{3,2,1,0:T(8,128)(2,1)} copy(bf16[16,8,32,128]{3,1,2,0:T(8,128)(2,1)S(1)} %bitcast.32) | data formatting | bytes 2097152
  57.2 0.0 collective-permute-done.4.from_a
  57.2 2.7 %collective-permute-done.5.from_b = f32[48,128]{1,0:T(8,128)S(1)} collective-permute-done((f32[48,128]{1,0:T(8,128)S(1)}, f32[48,128]{1,0:T(8,128)S(1)}, u32[]{:S(2)}, u32[]{:S(2)}) %collective-permute-start.5) | collective-permute-done | bytes 24608 | tf_op jit(solution)/shard_map/ppermute | solution.py:382
  59.8 1.4 %passes.1 = f32[32,128]{1,0:T(8,128)} custom-call(f32[5,48,128]{2,1,0:T(8,128)S(1)} %get-tuple-element.19.wide, f32[48,128]{1,0:T(8,128)S(1)} %collective-permute-done.4.from_a, f32[48,128]{1,0:T(8,128)S(1)} %collective-permute-done.5.from_b, f32[32,128]{1,0:T(8,128)} %bitcast.37), custom_call_target="tpu_custom_call" | custom-call | bytes 1048576 | tf_op jit(solution)/shard_map/passes/pallas_call | solution.py:35
  (16 shorter events, 0.0 us)
Async XLA Ops:
  0.6 26.1 %copy-start.10 = (s32[1,32,128]{2,1,0:T(8,128)S(1)}, s32[1,32,128]{2,1,0:T(8,128)}, u32[]{:S(2)}) copy-start(s32[1,32,128]{2,1,0:T(8,128)} %param.13) | copy-start | bytes 49156
  2.4 26.1 %all-to-all-start = ((bf16[64,2,128]{2,1,0:T(2,128)(2,1)}), bf16[64,2,128]{2,1,0:T(2,128)(2,1)S(1)}, u32[]{:S(2)}, u32[]{:S(2)}) async-start(bf16[64,2,128]{2,1,0:T(2,128)(2,1)} %bitcast.2), calls=%async_computation | async-start | bytes 65536 | tf_op jit(solution)/shard_map/all_to_all | solution.py:394
  16.7 11.8 %copy-start = (bf16[1,1,1,32,2,128,128]{6,5,4,3,2,1,0:T(8,128)(2,1)S(1)}, bf16[1,1,1,32,2,128,128]{6,5,4,3,2,1,0:T(8,128)(2,1)}, u32[]{:S(2)}) copy-start(bf16[1,1,1,32,2,128,128]{6,5,4,3,2,1,0:T(8,128)(2,1)} %param.15) | copy-start | bytes 6291460
  16.8 11.8 %copy-start.3 = (s32[1,32,128]{2,1,0:T(8,128)S(1)}, s32[1,32,128]{2,1,0:T(8,128)}, u32[]{:S(2)}) copy-start(s32[1,32,128]{2,1,0:T(8,128)} %param.12) | copy-start | bytes 49156
  16.8 11.8 %copy-start.7 = (s32[1,1,1,32,2]{3,4,2,1,0:T(2,128)S(1)}, s32[1,1,1,32,2]{3,4,2,1,0:T(2,128)}, u32[]{:S(2)}) copy-start(s32[1,1,1,32,2]{3,4,2,1,0:T(2,128)} %param.16) | copy-start | bytes 772
  16.8 11.8 %copy-start.8 = (s32[1,1,1,64,2]{3,4,2,1,0:T(2,128)S(1)}, s32[1,1,1,64,2]{3,4,2,1,0:T(2,128)}, u32[]{:S(2)}) copy-start(s32[1,1,1,64,2]{3,4,2,1,0:T(2,128)} %param.17) | copy-start | bytes 1540
  16.8 11.7 %copy-start.9 = (bf16[1,2,128,128]{3,2,1,0:T(8,128)(2,1)S(1)}, bf16[1,2,128,128]{3,2,1,0:T(8,128)(2,1)}, u32[]{:S(2)}) copy-start(bf16[1,2,128,128]{3,2,1,0:T(8,128)(2,1)} %param.14) | copy-start | bytes 196612
  19.1 30.1 %collective-permute-start.2 = (f32[808,128]{1,0:T(8,128)}, f32[808,128]{1,0:T(8,128)}, u32[]{:S(2)}, u32[]{:S(2)}) collective-permute-start(f32[808,128]{1,0:T(8,128)} %get-tuple-element.17), channel_id=1, source_target_pairs={{384,392},{400,408},{416,424},{432,440},{448,456},{464,472},{480,4... | collective-permute-start | bytes 1241096 | tf_op jit(solution)/shard_map/ppermute | solution.py:382
  22.2 27.0 %collective-permute-start.3 = (f32[808,128]{1,0:T(8,128)}, f32[808,128]{1,0:T(8,128)}, u32[]{:S(2)}, u32[]{:S(2)}) collective-permute-start(f32[808,128]{1,0:T(8,128)} %get-tuple-element.18), channel_id=1, source_target_pairs={{392,400},{408,416},{424,432},{440,448},{456,464},{472,480},{488,4... | collective-permute-start | bytes 1241096 | tf_op jit(solution)/shard_map/ppermute | solution.py:382
  28.4 2.9 %copy-start.1 = (bf16[16,8,32,128]{3,1,2,0:T(8,128)(2,1)}, bf16[16,8,32,128]{3,1,2,0:T(8,128)(2,1)S(1)}, u32[]{:S(2)}) copy-start(bf16[16,8,32,128]{3,1,2,0:T(8,128)(2,1)S(1)} %copy.16) | copy-start | bytes 3145732
  28.5 2.8 %copy-start.6 = (bf16[1,1,32,128]{3,1,2,0:T(2,128)(2,1)}, bf16[1,1,32,128]{3,1,2,0:T(2,128)(2,1)S(1)}, u32[]{:S(2)}) copy-start(bf16[1,1,32,128]{3,1,2,0:T(2,128)(2,1)S(1)} %copy.17) | copy-start | bytes 24580
  31.3 17.8 %all-to-all-start.1 = ((bf16[192,2,128]{2,1,0:T(2,128)(2,1)}), bf16[192,2,128]{2,1,0:T(2,128)(2,1)S(1)}, u32[]{:S(2)}, u32[]{:S(2)}) async-start(bf16[192,2,128]{2,1,0:T(2,128)(2,1)} %bitcast.9), calls=%async_computation.1 | async-start | bytes 196608 | tf_op jit(solution)/shard_map/all_to_all | solution.py:427
  38.2 10.9 %copy-start.2 = (f32[1,32,128]{2,1,0:T(8,128)S(1)}, f32[1,32,128]{2,1,0:T(8,128)}, u32[]{:S(2)}) copy-start(f32[1,32,128]{2,1,0:T(8,128)} %param.10) | copy-start | bytes 49156
  38.2 10.9 %copy-start.4 = (s32[1,32,128]{2,1,0:T(8,128)S(1)}, s32[1,32,128]{2,1,0:T(8,128)}, u32[]{:S(2)}) copy-start(s32[1,32,128]{2,1,0:T(8,128)} %param.12) | copy-start | bytes 49156
  38.2 10.9 %copy-start.5 = (f32[1,32,128]{2,1,0:T(8,128)S(1)}, f32[1,32,128]{2,1,0:T(8,128)}, u32[]{:S(2)}) copy-start(f32[1,32,128]{2,1,0:T(8,128)} %param.11) | copy-start | bytes 49156
  39.5 7.7 %collective-permute-start = (f32[8,128]{1,0:T(8,128)S(1)}, f32[8,128]{1,0:T(8,128)S(1)}, u32[]{:S(2)}, u32[]{:S(2)}) collective-permute-start(f32[8,128]{1,0:T(8,128)S(1)} %get-tuple-element.15), channel_id=1, source_target_pairs={{384,392},{400,408},{416,424},{432,440},{448,456},{464,472},{480,4... | collective-permute-start | bytes 12296 | tf_op jit(solution)/shard_map/ppermute | solution.py:382
  42.6 6.5 %collective-permute-start.1 = (f32[8,128]{1,0:T(8,128)S(1)}, f32[8,128]{1,0:T(8,128)S(1)}, u32[]{:S(2)}, u32[]{:S(2)}) collective-permute-start(f32[8,128]{1,0:T(8,128)S(1)} %get-tuple-element.16), channel_id=1, source_target_pairs={{392,400},{408,416},{424,432},{440,448},{456,464},{472,480},{488,4... | collective-permute-start | bytes 12296 | tf_op jit(solution)/shard_map/ppermute | solution.py:382
  51.8 5.4 %collective-permute-start.4 = (f32[48,128]{1,0:T(8,128)S(1)}, f32[48,128]{1,0:T(8,128)S(1)}, u32[]{:S(2)}, u32[]{:S(2)}) collective-permute-start(f32[48,128]{1,0:T(8,128)S(1)} %get-tuple-element.20), channel_id=1, source_target_pairs={{384,385},{386,387},{388,389},{390,391},{385,384},{387,386},{389,3... | collective-permute-start | bytes 73736 | tf_op jit(solution)/shard_map/ppermute | solution.py:382
  54.1 5.8 %collective-permute-start.5 = (f32[48,128]{1,0:T(8,128)S(1)}, f32[48,128]{1,0:T(8,128)S(1)}, u32[]{:S(2)}, u32[]{:S(2)}) collective-permute-start(f32[48,128]{1,0:T(8,128)S(1)} %get-tuple-element.21), channel_id=1, source_target_pairs={{385,386},{387,388},{389,390},{386,385},{388,387},{390,389},{393,3... | collective-permute-start | bytes 73736 | tf_op jit(solution)/shard_map/ppermute | solution.py:382

commit v4 on v3

v4 whole, which is shorter than its diff:
```python
import functools

import jax
import jax.numpy as jnp
from jax import lax
from jax.experimental import pallas as pl
from jax.experimental.pallas import tpu as pltpu
from jax.sharding import PartitionSpec as P

PHYS = 4
PASSES = 4
HALO = 8
NEAR = 3
PLANES = 5
WIDTH = 2048
MESSAGE = 8
bf16 = jnp.bfloat16
f32 = jnp.float32
HBM = pltpu.HBM
VMEM = pltpu.VMEM
VMEM_LIMIT = 16 * 1024 * 1024


def call(kernel, name, operands, outs, scratch=(), flops=0, aliases=None):
    values, specs = [], []
    for operand in operands:
        value, place = operand if isinstance(operand, tuple) else (operand, None)
        if place is not None:
            value = pltpu.with_memory_space_constraint(value, place)
        values.append(value)
        specs.append(pl.BlockSpec(memory_space=HBM if place is HBM else VMEM))
    shapes = [
        out[2](out[0], out[1]) if len(out) > 2 else jax.ShapeDtypeStruct(out[0], out[1]) for out in outs
    ]
    return pl.pallas_call(
        kernel,
        out_shape=shapes,
        in_specs=specs,
        out_specs=[pl.BlockSpec(memory_space=out[2] if len(out) > 2 else VMEM) for out in outs],
        scratch_shapes=list(scratch),
        input_output_aliases=aliases or {},
        name=name,
        cost_estimate=pl.CostEstimate(flops=flops, bytes_accessed=1 << 20, transcendentals=0),
        compiler_params=pltpu.CompilerParams(vmem_limit_bytes=VMEM_LIMIT),
    )(*values)


def fetch(sems, *pairs):
    copies = [pltpu.make_async_copy(source, target, sems.at[n]) for n, (source, target) in enumerate(pairs)]
    for copy in copies:
        copy.start()
    return copies


def is_ocean():
    return lax.axis_index("sec") == lax.axis_size("sec") - 1


def is_even(axis):
    return lax.rem(lax.axis_index(axis), 2) == 0


def iota(shape, dim):
    return lax.broadcasted_iota(jnp.int32, shape, dim)


def one_hot(flags):
    return jnp.where(flags, 1.0, 0.0).astype(bf16)


def spread(rows, column, odd):
    hot = one_hot(iota((column.shape[0], rows.shape[1]), 1) == column)
    values = rows.astype(f32).astype(bf16)
    both = lax.dot_general(hot, values, (((1,), (1,)), ((), ())), preferred_element_type=f32)
    return jnp.where(odd == 1, both[:, 1:2], both[:, 0:1]).astype(jnp.int32)


def upright(rows, first=0, count=None):
    count = rows.shape[1] if count is None else count
    unit = one_hot(iota((count, rows.shape[1]), 0) + first == iota((count, rows.shape[1]), 1))
    values = rows.astype(f32).astype(bf16)
    turned = lax.dot_general(unit, values, (((1,), (1,)), ((), ())), preferred_element_type=f32)
    return turned.astype(jnp.int32)


def select_kernel(profile, lists_ref, out_ref, lowest, tiles_v, lists_v, sems):
    copies = fetch(sems, (lists_ref, lists_v), (profile.at[0, 0], tiles_v))
    row = iota((out_ref.shape[0], 1), 0)
    copies[0].wait()
    tile = spread(lists_v[...], row >> 1, row & 1)
    hot = one_hot(iota((out_ref.shape[0], tiles_v.shape[0]), 1) == tile)
    copies[1].wait()
    tiles = tiles_v[...]
    out_ref[...] = jnp.dot(hot, tiles, preferred_element_type=f32).astype(bf16)
    lowest[...] = tiles.astype(f32)


def parts(values):
    high = values.astype(bf16).astype(f32)
    rest = values - high
    middle = rest.astype(bf16).astype(f32)
    return [high, middle, rest - middle]


def edges_kernel(
    surface, diffusion, sea, profile, sources, weights, lists, to_a, to_b, hot, hot_message,
    surface_v, diffusion_v, sea_v, level_v, sources_v, lists_v, edge_v, hot_v, sems,
):
    rows, size = surface_v.shape
    count = 2 * NEAR
    last = is_even("gx")
    near = jnp.where(last, 2 * rows - count, 0)
    pairs = (
        (weights.at[pl.ds(near, count)], edge_v.at[0, 0:count]),
        (weights.at[pl.ds(2 * rows - count - near, count)], edge_v.at[1, 0:count]),
        (surface, surface_v),
        (diffusion, diffusion_v),
        (sea, sea_v),
        (profile.at[0, 0], level_v),
        (sources, sources_v),
        (lists, lists_v),
    )
    copies = [pltpu.make_async_copy(source, target, sems.at[n]) for n, (source, target) in enumerate(pairs)]
    copies[-2].start()
    copies[-1].start()

    @pl.when(is_ocean())
    def _():
        for copy in copies[:-2]:
            copy.start()

    row = iota((hot_v.shape[0], 1), 0)
    target, m = row >> 3, row & 7
    own = lax.axis_index("sec") * lax.axis_size("gx") + lax.axis_index("gx")
    of_edge = jnp.where(target == own + 1, rows - HALO + m, jnp.where(target == own - 1, m, -1))
    copies[-2].wait()
    copies[-1].wait()
    of_tiles = spread(lists_v[...], target - 1 + (m >> 1), m & 1)
    wanted = jnp.where(is_ocean(), of_edge, of_tiles)
    hot_v[...] = one_hot(iota(hot_v.shape, 1) == wanted)
    sent = pltpu.make_async_copy(hot_v, hot_message, sems.at[len(copies)])
    sent.start()
    q = upright(sources_v[...])
    place = iota((rows, hot.shape[1]), 1)
    hot[...] = jnp.concatenate([one_hot(q[:, k : k + 1] == place) for k in (0, 1)], axis=0)

    @pl.when(is_ocean())
    def _():
        for copy in copies[2:-2]:
            copy.wait()
        held = jnp.concatenate([sources_v[...].astype(f32), jnp.zeros((2, size - rows), f32)], axis=1)
        fields = (
            *parts(surface_v[...]),
            *parts(diffusion_v[...]),
            sea_v[...].astype(f32),
            level_v[...].astype(f32),
        )
        for n in (0, 1):
            tail = last if n == 0 else jnp.logical_not(last)
            pieces = [jnp.where(tail, v[rows - HALO : rows], v[0:HALO]) for v in fields] + [held]
            used = sum(piece.shape[0] for piece in pieces)
            pieces.append(jnp.zeros((size - used, size), f32))
            edge_v[n, count] = jnp.concatenate(pieces, axis=0).astype(bf16)
        copies[0].wait()
        copies[1].wait()
        for copy in fetch(sems, (edge_v.at[0], to_a), (edge_v.at[1], to_b)):
            copy.wait()

    sent.wait()


def pass_kernel(edge, *refs):
    pass


def import_row(pick_ref, a, first, second):
    row = pick_ref[a : a + 1, :].astype(bf16)
    block = jnp.concatenate([first, second], axis=1)
    return lax.dot_general(row, block, (((1,), (1,)), ((), ())), preferred_element_type=f32)


def substep(x, flag, mix):
    deep = x * flag
    both = jnp.concatenate([x - deep, deep], axis=0)
    mixed = jnp.dot(mix, both, preferred_element_type=f32)
    return (0.5 * x.astype(f32) + jnp.tanh(mixed)).astype(bf16)


def with_bottom(x, bottom):
    top = x[0:16].astype(f32)
    top = jnp.where(iota(top.shape, 0) == 0, bottom, top).astype(bf16)
    return jnp.concatenate([top, x[16:]], axis=0)


def flat_rows(grid, first, count):
    return jnp.concatenate([grid[first + r : first + r + 1] for r in range(count)], axis=1)


def first_kernel(
    received, hot, weights, lowest_ref, sea, x_ref, flag_ref, mixing, hot_message,
    message, carry, pick, low_f, carry_v, hot_v, sems,
):
    rows, tile = carry_v.shape
    pltpu.make_async_copy(hot_message, hot_v, sems.at[1]).start()
    picked = jnp.dot(hot[...], received[...], preferred_element_type=f32)
    pick[:, 0:tile] = picked[0:rows]
    pick[:, tile : 2 * tile] = picked[rows : 2 * rows]
    for a in range(rows):
        carry_v[a : a + 1, :] = import_row(pick, a, weights[2 * a], weights[2 * a + 1])
    lowest = lowest_ref[...]
    flux = sea[...].astype(f32) * (carry_v[...] - lowest)
    kept = pltpu.make_async_copy(carry_v, carry, sems.at[0])

    def send(rows_of):
        pltpu.make_async_copy(hot_message, hot_v, sems.at[1]).wait()
        made = jnp.dot(hot_v[...], rows_of.astype(bf16), preferred_element_type=f32)
        message[...] = made.astype(bf16)

    @pl.when(is_ocean())
    def _():
        forcing = flux * (1.0 / PASSES)
        carry_v[...] = forcing
        kept.start()
        send(forcing)

    @pl.when(jnp.logical_not(is_ocean()))
    def _():
        kept.start()
        mix = jnp.concatenate([mixing[0], mixing[1]], axis=1)
        bottom = (lowest + flux).astype(bf16).astype(f32)
        per = WIDTH // tile
        for c in range(x_ref.shape[1] // WIDTH):
            cols = slice(c * WIDTH, (c + 1) * WIDTH)
            flag = flag_ref[:, cols]
            x = with_bottom(x_ref[:, cols], flat_rows(bottom, c * per, per))
            for _ in range(PHYS - 1):
                x = substep(x, flag, mix)
            deep = x * flag
            both = jnp.concatenate([x - deep, deep], axis=0)
            mixed = jnp.dot(mix[0:16], both, preferred_element_type=f32)
            last = 0.5 * x[0:16].astype(f32) + jnp.tanh(mixed)
            for r in range(per):
                low_f[c * per + r : c * per + r + 1, :] = last[0:1, r * tile : (r + 1) * tile]
        send(low_f[...])

    kept.wait()


def second_kernel(
    carry, x_ref, flag_ref, mixing, sea, out, made, carry_v, x_v, flag_v, mixing_v, sea_v, sems
):
    made[...] = jnp.zeros(made.shape, f32)

    @pl.when(is_ocean())
    def _():
        fetch(sems, (x_ref, x_v))[0].wait()
        fetch(sems, (x_v, out))[0].wait()

    @pl.when(jnp.logical_not(is_ocean()))
    def _():
        pairs = ((carry, carry_v), (sea, sea_v), (mixing, mixing_v), (flag_ref, flag_v), (x_ref, x_v))
        for copy in fetch(sems, *pairs):
            copy.wait()
        mix = jnp.concatenate([mixing_v[0], mixing_v[1]], axis=1)
        sea_f = sea_v[...].astype(f32)
        imported = carry_v[...]
        per = WIDTH // carry_v.shape[1]
        for c in range(x_v.shape[1] // WIDTH):
            cols = slice(c * WIDTH, (c + 1) * WIDTH)
            flag = flag_v[:, cols]
            x = x_v[:, cols]
            wet = flat_rows(sea_f, c * per, per)
            brought = flat_rows(imported, c * per, per)
            for _ in range(2):
                low = x[0:16].astype(f32)[0:1]
                x = with_bottom(x, (low + wet * (brought - low)).astype(bf16).astype(f32))
                for _ in range(PHYS):
                    x = substep(x, flag, mix)
            x_v[:, cols] = x
        fetch(sems, (x_v, out))[0].wait()


def ready_kernel(
    surface, diffusion, sea, profile, sources, carry, still_a, still_b, made,
    hot, planes,
    surface_v, diffusion_v, sea_v, level_v, sources_v, carry_v, sems,
):
    @pl.when(is_ocean())
    def _():
        rows, tile = surface_v.shape
        total = rows + 2 * HALO
        even = is_even("gx")

        copies = fetch(
            sems,
            (surface, surface_v),
            (diffusion, diffusion_v),
            (sea, sea_v),
            (profile.at[0, 0], level_v),
            (sources, sources_v),
            (carry, carry_v),
        )
        for copy in copies:
            copy.wait()
        edges = [still[2 * NEAR].astype(f32) for still in (still_a, still_b)]
        below = jnp.where(even, edges[0], edges[1])
        above = jnp.where(even, edges[1], edges[0])

        def whole_of(values, at, pieces):
            held = [below[at : at + HALO], above[at : at + HALO]]
            for n in range(1, pieces):
                part = slice(at + n * HALO, at + (n + 1) * HALO)
                held = [held[0] + below[part], held[1] + above[part]]
            return jnp.concatenate([values, *held], axis=0)

        planes[0] = whole_of(surface_v[...], 0, 3)
        planes[1] = whole_of(diffusion_v[...], 3 * HALO, 3)
        planes[2] = whole_of(sea_v[...].astype(f32), 6 * HALO, 1)
        planes[3] = whole_of(level_v[...].astype(f32), 7 * HALO, 1)
        planes[4, 0:rows] = carry_v[...]
        planes[4, rows:total] = jnp.zeros((2 * HALO, tile), f32)

        at = slice(8 * HALO, 8 * HALO + 2)
        q = jnp.concatenate(
            [
                upright(sources_v[...]),
                upright(below[at, 0:rows].astype(jnp.int32), 0, HALO),
                upright(above[at, 0:rows].astype(jnp.int32), rows - HALO, HALO),
            ],
            axis=0,
        )
        row = iota((total, 1), 0)
        offset = jnp.where(row < rows, 2, jnp.where(row < rows + HALO, 4, 0))
        place = iota((total, hot.shape[1]), 1)
        q = (q >> 1) * MESSAGE + (q & 1) + offset
        own = lax.axis_index("sec") * lax.axis_size("gx") + lax.axis_index("gx")
        row = iota((2 * HALO, 1), 0)
        beyond = jnp.where(row < HALO, (own + 1) * MESSAGE, (own - 1) * MESSAGE - HALO) + row
        place_b = iota((2 * HALO, hot.shape[1]), 1)
        hot[...] = jnp.concatenate(
            [one_hot(q[:, 0:1] == place), one_hot(q[:, 1:2] == place), one_hot(beyond == place_b)], axis=0
        )


def third_kernel(
    received, weights, hot, planes, still_a, still_b, wide, to_a, to_b, pick, imported
):
    @pl.when(is_ocean())
    def _():
        total, tile = imported.shape
        rows = total - 2 * HALO
        picked = jnp.dot(hot[...], received[...], preferred_element_type=f32)
        pick[:, 0:tile] = picked[0:total]
        pick[:, tile : 2 * tile] = picked[total : 2 * total]
        imported[rows:total] = jnp.zeros((2 * HALO, tile), f32)
        for a in range(rows):
            imported[a : a + 1, :] = import_row(pick, a, weights[2 * a], weights[2 * a + 1])
        from_next = is_even("gx")
        for n in range(NEAR):
            for a, first in ((rows + n, from_next), (total - NEAR + n, jnp.logical_not(from_next))):
                blocks = [jnp.where(first, still_a[2 * n + k], still_b[2 * n + k]) for k in range(2)]
                imported[a : a + 1, :] = import_row(pick, a, blocks[0], blocks[1])
        fields = [
            jnp.concatenate([planes[4, 0:rows], picked[2 * total :]], axis=0),
            planes[2] * (imported[...] - planes[3]) * (1.0 / PASSES),
            planes[0],
            planes[1],
            planes[2],
        ]
        group = iota((total, tile), 1) >> 3
        right = left = fields[0]
        for p, values in enumerate(fields):
            wide[p] = values
            if p:
                right = jnp.where(group == tile // HALO - 1 - p, pltpu.roll(values, tile - HALO * p, 1), right)
                left = jnp.where(group == p, pltpu.roll(values, HALO * p, 1), left)
        even = is_even("gy")
        to_a[...] = jnp.where(even, right, left)
        to_b[...] = jnp.where(even, left, right)


def fourth_kernel(wide, from_a, from_b, surface, out, sems):
    @pl.when(jnp.logical_not(is_ocean()))
    def _():
        fetch(sems, (surface, out))[0].wait()

    @pl.when(is_ocean())
    def _():
        rows, tile = out.shape
        total = wide.shape[1]
        group = iota((total, tile), 1) >> 3
        even = is_even("gy")
        from_right = jnp.where(even, from_a[...], from_b[...])
        from_left = jnp.where(even, from_b[...], from_a[...])
        fields = []
        for p in range(PLANES):
            right, left = from_right, from_left
            if p:
                right = pltpu.roll(right, tile - HALO * p, 1)
                left = pltpu.roll(left, HALO * p, 1)
            beside = jnp.where(group == 0, right, jnp.where(group == tile // HALO - 1, left, 0.0))
            fields.append(jnp.concatenate([wide[p], beside], axis=1))
        forcing_1, forcing_2, height, coefficient, sea = fields
        for forcing in (forcing_1, forcing_2):
            for sweep in range(PASSES):
                around = pltpu.roll(height, total - 1, 0) + pltpu.roll(height, 1, 0)
                around = around + pltpu.roll(height, 2 * tile - 1, 1) + pltpu.roll(height, 1, 1)
                height = sea * (height + coefficient * (around - 4.0 * height) + forcing)
        out[...] = height[0:rows, 0:tile]


def body(
    profile, surface, diffusion, sea_mask, convective, mixing, remap_weights, sources, send_lists
):
    levels, rows, tile = profile.shape[1:]
    cells = rows * tile
    surface_2d = surface.reshape(rows, tile)
    coefficient = diffusion.reshape(rows, tile)
    sea = sea_mask.reshape(rows, tile)
    matrices = mixing.reshape(2, levels, levels)
    weights = remap_weights.reshape(2 * rows, tile, tile)
    wanted = sources.reshape(sources.shape[3:]).T
    lists = send_lists.reshape(send_lists.shape[3:]).T
    slots, senders = lists.shape
    secs = lax.axis_size("sec")
    gx = lax.axis_size("gx")
    gy = lax.axis_size("gy")
    total = rows + 2 * HALO
    grid = (rows, tile)

    base = {"gx": (secs - 1) * gx, "gy": (secs - 1) * gy}
    counts = {"gx": gx, "gy": gy}

    def swap(axis, start, values):
        first = base[axis]
        pairs = [(first + i, first + i + 1) for i in range(start, counts[axis] - 1, 2)]
        return lax.ppermute(values, ("sec", axis), pairs + [(t, s) for s, t in pairs])

    def semaphores(count):
        return pltpu.SemaphoreType.DMA((count,))

    chosen, lowest = call(
        select_kernel,
        "select_tiles",
        [(profile, HBM), (lists, HBM)],
        [((senders * slots, tile), bf16), (grid, f32)],
        [VMEM(grid, bf16), VMEM(lists.shape, jnp.int32), semaphores(2)],
    )
    received = lax.all_to_all(chosen.reshape(senders, slots, tile), ("sec", "gx"), 0, 0, tiled=True)

    edge = ((2 * NEAR + 1, tile, tile), bf16, HBM)
    edge_operands = [(v, HBM) for v in (surface_2d, coefficient, sea, profile, wanted, weights)]
    edge_scratch = [
        VMEM(grid, f32),
        VMEM(grid, f32),
        VMEM(grid, jnp.int32),
        VMEM(grid, bf16),
        VMEM(wanted.shape, jnp.int32),
    ]
    edge_a, edge_b, hot_first, hot_message = call(
        edges_kernel,
        "edge_rows",
        [*edge_operands, (lists, HBM)],
        [edge, edge, ((2 * rows, senders * slots), bf16), ((senders * MESSAGE, rows), bf16, HBM)],
        [
            *edge_scratch,
            VMEM(lists.shape, jnp.int32),
            VMEM((2, *edge[0]), bf16),
            VMEM((senders * MESSAGE, rows), bf16),
            semaphores(9),
        ],
    )
    still_a = swap("gx", 0, edge_a)

    columns = profile.reshape(levels, cells)
    flag = convective.reshape(1, cells).astype(bf16)
    message, carry = call(
        first_kernel,
        "first_step",
        [
            received.reshape(senders * slots, tile), hot_first, weights, lowest, sea, (columns, VMEM),
            flag, matrices, (hot_message, HBM),
        ],
        [((senders * MESSAGE, tile), bf16), (grid, f32, HBM)],
        [
            VMEM((rows, 2 * tile), f32),
            VMEM(grid, f32),
            VMEM(grid, f32),
            VMEM((senders * MESSAGE, rows), bf16),
            semaphores(2),
        ],
        flops=1 << 34,
    )
    again = lax.all_to_all(
        message.reshape(senders * MESSAGE // 2, 2, tile), ("sec", "gx"), 0, 0, tiled=True
    )
    (edge_b,) = call(pass_kernel, "pass_edge", [(edge_b, HBM), (carry, HBM), still_a], [edge], aliases={0: 0})
    still_b = swap("gx", 1, edge_b)
    final, made = call(
        second_kernel,
        "second_step",
        [(carry, HBM), (columns, HBM), (flag, HBM), (matrices, HBM), (sea, HBM)],
        [((levels, cells), bf16, HBM), ((8, tile), f32)],
        [
            VMEM(grid, f32),
            VMEM((levels, cells), bf16),
            VMEM((1, cells), bf16),
            VMEM(matrices.shape, bf16),
            VMEM(grid, jnp.int32),
            semaphores(5),
        ],
        flops=1 << 34,
    )
    picks = 2 * total + 2 * HALO
    hot, planes = call(
        ready_kernel,
        "ready_import",
        [*edge_operands[:5], (carry, HBM), still_a, still_b, made],
        [((picks, senders * MESSAGE), bf16), ((PLANES, total, tile), f32)],
        [*edge_scratch, VMEM(grid, f32), semaphores(6)],
    )
    wide, to_a, to_b = call(
        third_kernel,
        "second_import",
        [again.reshape(senders * MESSAGE, tile), weights, hot, planes, still_a, still_b],
        [((PLANES, total, tile), f32), ((total, tile), f32), ((total, tile), f32)],
        [
            VMEM((total, 2 * tile), f32),
            VMEM((total, tile), f32),
        ],
    )
    from_a, from_b = swap("gy", 0, to_a), swap("gy", 1, to_b)
    (surface_out,) = call(
        fourth_kernel,
        "passes",
        [wide, from_a, from_b, (surface_2d, HBM)],
        [(grid, f32)],
        [semaphores(1)],
    )
    return (final.reshape(profile.shape), surface_out.reshape(surface.shape))


def solution(mesh):
    return jax.shard_map(
        body,
        mesh=mesh,
        in_specs=(
            P("sec", None, "gx", "gy"),
            P("sec", "gx", "gy"),
            P("sec", "gx", "gy"),
            P("sec", "gx", "gy"),
            P("sec", "gx", "gy"),
            P("sec", None, None, None),
            P("sec", "gx", "gy", None, None, None, None),
            P("sec", "gx", "gy", None, None),
            P("sec", "gx", "gy", None, None),
        ),
        out_specs=(P("sec", None, "gx", "gy"), P("sec", "gx", "gy")),
        check_vma=False,
    )
```

time: 61.8 us -> 56.6 us (0.916)
  starting transfers between devices: 40.8 us -> 35.2 us
  waiting for transfers between devices: 4.54 us -> 5.53 us
    ppermute x6 -> x4, starting transfers between devices: 19.6 us -> 11.9 us  [swap(): lax.ppermute(values, ('sec', axis), pairs + [(t, s) for s, t in pairs])]
    all_to_all x1, starting transfers between devices: 6.86 us -> 8.88 us  [body(): lax.all_to_all(message.reshape(senders * MESSAGE // 2, 2, tile), ('sec',...]
    ppermute x6 -> x4, waiting for transfers between devices: 4.54 us -> 5.13 us  [swap(): lax.ppermute(values, ('sec', axis), pairs + [(t, s) for s, t in pairs])]
    pallas_call x6 -> x8, Pallas kernels: 12 us -> 11.6 us  [call(): pl.pallas_call(kernel, out_shape=shapes, in_specs=specs, out_specs=[pl.Bl...]
    unnamed x25 -> x17, local copies, waits for them, and re-layouts: 2.95 us -> 2.92 us
  transfers between devices with their start and end apart: 8 -> 6, of which waited for: 2 -> 3; matrix products, arithmetic and copies ran while one was open for 5% -> 5% of each run, Pallas kernels for 10% -> 13%
where the time goes in v4:
time: 56.6 us; the launch traced here: 56 us
  starting transfers between devices  35.2 us (62%)
  Pallas kernels  11.6 us (20%)
  waiting for transfers between devices  5.53 us (10%)
  local copies, waits for them, and re-layouts  2.92 us (5%)
  between operations  0.85 us (2%)
    all_to_all x1, starting transfers between devices, body(): lax.all_to_all(chosen.reshape(senders, slots, tile), ('sec', 'gx'), 0, 0,...  14.4 us
    ppermute x4, starting transfers between devices, swap(): lax.ppermute(values, ('sec', axis), pairs + [(t, s) for s, t in pairs])  11.9 us
    pallas_call x8, Pallas kernels, call(): pl.pallas_call(kernel, out_shape=shapes, in_specs=specs, out_specs=[pl.Bl...  11.6 us
    all_to_all x1, starting transfers between devices, body(): lax.all_to_all(message.reshape(senders * MESSAGE // 2, 2, tile), ('sec',...  8.88 us
    ppermute x4, waiting for transfers between devices, swap(): lax.ppermute(values, ('sec', axis), pairs + [(t, s) for s, t in pairs])  5.13 us
    unnamed x17, local copies, waits for them, and re-layouts  2.92 us
  transfers between devices with their start and end apart: 6, of which 3 were waited for; matrix products, arithmetic and copies ran while one was open for 5% of the time, Pallas kernels for 13%

profile of v4, /device:TPU:39, one launch (start us, length us, event | category | flops | bytes accessed | tf_op | source)
XLA Modules:
  0.0 56.0 jit_solution(1740213438183053786)
XLA Ops:
  0.6 0.0 copy-start.6
  0.6 1.7 %select_tiles.1 = (bf16[128,128]{1,0:T(8,128)(2,1)}, f32[32,128]{1,0:T(8,128)S(1)}) custom-call(bf16[1,128,32,128]{3,2,1,0:T(8,128)(2,1)} %profile.5, s32[2,64]{1,0:T(2,128)} %bitcast.53), custom_call_target="tpu_custom_call" | custom-call | bytes 1048576 | tf_op jit(solution)/shard_map/select_tiles/pallas_call | solution.py:35
  2.4 14.4 %all-to-all-start = ((bf16[64,2,128]{2,1,0:T(2,128)(2,1)}), bf16[64,2,128]{2,1,0:T(2,128)(2,1)S(1)}, u32[]{:S(2)}, u32[]{:S(2)}) async-start(bf16[64,2,128]{2,1,0:T(2,128)(2,1)} %bitcast.2), calls=%async_computation | async-start | bytes 65536 | tf_op jit(solution)/shard_map/all_to_all | solution.py:449
  16.7 0.0 copy-start
  16.7 0.0 copy-start.2
  16.8 0.0 copy-start.4
  16.8 2.1 %edge_rows.1 = (bf16[7,128,128]{2,1,0:T(8,128)(2,1)}, bf16[7,128,128]{2,1,0:T(8,128)(2,1)}, bf16[64,128]{1,0:T(8,128)(2,1)S(1)}, bf16[512,32]{1,0:T(8,128)(2,1)}) custom-call(f32[32,128]{1,0:T(8,128)} %bitcast.47, f32[32,128]{1,0:T(8,128)} %bitcast.50, s32[32,128]{1,0:T(8,128)} %bitcast.35, bf16[1,128,32,128]{3,2,1,0:T(8,128)(2,1)} %profile.5, ...), custom_call_target="tpu_custom_call" | custom-call | bytes 1048576 | tf_op jit(solution)/shard_map/edge_rows/pallas_call | solution.py:35
  18.9 3.1 %collective-permute-start = (bf16[7,128,128]{2,1,0:T(8,128)(2,1)}, bf16[7,128,128]{2,1,0:T(8,128)(2,1)S(1)}, u32[]{:S(2)}, u32[]{:S(2)}) collective-permute-start(bf16[7,128,128]{2,1,0:T(8,128)(2,1)} %get-tuple-element.24), channel_id=1, source_target_pairs={{384,392},{400,408},{416,424},{432,440},{448,456},{464,472},{480,4... | collective-permute-start | bytes 688136 | tf_op jit(solution)/shard_map/ppermute | solution.py:437
  22.0 0.0 copy-done.6
  22.0 0.0 copy-start.3
  22.0 1.7 %copy.17 = bf16[16,8,32,128]{3,1,2,0:T(8,128)(2,1)S(1)} copy(bf16[16,8,32,128]{3,2,1,0:T(8,128)(2,1)} %bitcast.44) | data formatting | bytes 2097152
  23.7 0.0 copy-start.1
  23.7 0.4 all-to-all-done
  24.1 0.0 copy-done
  24.1 0.0 copy-done.2
  24.1 0.0 copy-done.4
  24.1 2.1 %first_step.1 = (bf16[512,128]{1,0:T(8,128)(2,1)}, f32[32,128]{1,0:T(8,128)}) custom-call(bf16[128,128]{1,0:T(8,128)(2,1)S(1)} %bitcast.39, bf16[64,128]{1,0:T(8,128)(2,1)S(1)} %get-tuple-element.18.hot, bf16[64,128,128]{2,1,0:T(8,128)(2,1)S(1)} %bitcast.30, f32[32,128]{1,0:T(8,128)S(1)} %get-tuple-element.19.lowest_ref, s32[32,128]{1,0:T(8,128)S(1)} %bitcast.38, ...), custom_call_target="tpu_custom_call" | custom-call | flops 17179869184 | bytes 1048576 | tf_op jit(solution)/shard_map/first_step/pallas_call | solution.py:35
  26.2 0.0 copy-done.3
  26.2 8.9 %all-to-all-start.1 = ((bf16[256,2,128]{2,1,0:T(2,128)(2,1)}), bf16[256,2,128]{2,1,0:T(2,128)(2,1)S(1)}, u32[]{:S(2)}, u32[]{:S(2)}) async-start(bf16[256,2,128]{2,1,0:T(2,128)(2,1)} %bitcast.12), calls=%async_computation.1 | async-start | bytes 262144 | tf_op jit(solution)/shard_map/all_to_all | solution.py:494
  35.1 0.0 collective-permute-done.refs_1_.still_a
  35.1 4.6 %collective-permute-start.1 = (bf16[7,128,128]{2,1,0:T(8,128)(2,1)}, bf16[7,128,128]{2,1,0:T(8,128)(2,1)S(1)}, u32[]{:S(2)}, u32[]{:S(2)}) collective-permute-start(bf16[7,128,128]{2,1,0:T(8,128)(2,1)} %pass_edge.1), channel_id=1, source_target_pairs={{392,400},{408,416},{424,432},{440,448},{456,464},{472,480},{488,4... | collective-permute-start | bytes 688136 | tf_op jit(solution)/shard_map/ppermute | solution.py:437
  39.7 2.3 %second_step.1 = (bf16[128,4096]{1,0:T(8,128)(2,1)}, f32[8,128]{1,0:T(8,128)S(1)}) custom-call(f32[32,128]{1,0:T(8,128)} %get-tuple-element.21.carry.refs_0_, bf16[128,4096]{1,0:T(8,128)(2,1)} %bitcast.33, bf16[1,4096]{1,0:T(2,128)(2,1)} %bitcast.41, bf16[2,128,128]{2,1,0:T(8,128)(2,1)} %bitcast.42, s32[32,128]{1,0:T(8,128)} %bitcast.36), custom_call_target="tpu_custom_call" | custom-call | flops 17179869184 | bytes 1048576 | tf_op jit(solution)/shard_map/second_step/pallas_call | solution.py:35
  42.0 2.5 %collective-permute-done.1.still_b = bf16[7,128,128]{2,1,0:T(8,128)(2,1)S(1)} collective-permute-done((bf16[7,128,128]{2,1,0:T(8,128)(2,1)}, bf16[7,128,128]{2,1,0:T(8,128)(2,1)S(1)}, u32[]{:S(2)}, u32[]{:S(2)}) %collective-permute-start.1) | collective-permute-done | bytes 229408 | tf_op jit(solution)/shard_map/ppermute | solution.py:437
  44.5 1.1 %ready_import.1 = (bf16[112,512]{1,0:T(8,128)(2,1)S(1)}, f32[5,48,128]{2,1,0:T(8,128)S(1)}) custom-call(f32[32,128]{1,0:T(8,128)} %bitcast.48, f32[32,128]{1,0:T(8,128)} %bitcast.51, s32[32,128]{1,0:T(8,128)} %bitcast.37, bf16[1,128,32,128]{3,2,1,0:T(8,128)(2,1)} %profile.5, s32[2,32]{1,0:T(2,128)} %bitcast.56, f32[32,128]{1,0:T(8,128)} %get-tuple-element.21.carry.refs_0_, ...), custom_call_target="tpu_custom_call" | custom-call | bytes 1048576 | tf_op jit(solution)/shard_map/ready_import/pallas_call | solution.py:35
  45.6 0.0 all-to-all-done.1
  45.6 1.0 %second_import.1 = (f32[5,48,128]{2,1,0:T(8,128)S(1)}, f32[48,128]{1,0:T(8,128)S(1)}, f32[48,128]{1,0:T(8,128)S(1)}) custom-call(bf16[512,128]{1,0:T(8,128)(2,1)S(1)} %bitcast.34, bf16[64,128,128]{2,1,0:T(8,128)(2,1)S(1)} %bitcast.31, bf16[112,512]{1,0:T(8,128)(2,1)S(1)} %get-tuple-element.27.hot, f32[5,48,128]{2,1,0:T(8,128)S(1)} %get-tuple-element.28.planes, ...), custom_call_target="tpu_custom_call" | custom-call | bytes 1048576 | tf_op jit(solution)/shard_map/second_import/pallas_call | solution.py:35
  46.6 2.3 %collective-permute-start.2 = (f32[48,128]{1,0:T(8,128)S(1)}, f32[48,128]{1,0:T(8,128)S(1)}, u32[]{:S(2)}, u32[]{:S(2)}) collective-permute-start(f32[48,128]{1,0:T(8,128)S(1)} %get-tuple-element.30), channel_id=1, source_target_pairs={{384,385},{386,387},{388,389},{390,391},{385,384},{387,386},{389,3... | collective-permute-start | bytes 73736 | tf_op jit(solution)/shard_map/ppermute | solution.py:437
  48.9 1.9 %collective-permute-start.3 = (f32[48,128]{1,0:T(8,128)S(1)}, f32[48,128]{1,0:T(8,128)S(1)}, u32[]{:S(2)}, u32[]{:S(2)}) collective-permute-start(f32[48,128]{1,0:T(8,128)S(1)} %get-tuple-element.31), channel_id=1, source_target_pairs={{385,386},{387,388},{389,390},{386,385},{388,387},{390,389},{393,3... | collective-permute-start | bytes 73736 | tf_op jit(solution)/shard_map/ppermute | solution.py:437
  50.8 1.2 %copy.14 = bf16[16,8,32,128]{3,2,1,0:T(8,128)(2,1)} copy(bf16[16,8,32,128]{3,1,2,0:T(8,128)(2,1)S(1)} %bitcast.45) | data formatting | bytes 2097152
  52.0 0.0 collective-permute-done.2.from_a
  52.0 2.6 %collective-permute-done.3.from_b = f32[48,128]{1,0:T(8,128)S(1)} collective-permute-done((f32[48,128]{1,0:T(8,128)S(1)}, f32[48,128]{1,0:T(8,128)S(1)}, u32[]{:S(2)}, u32[]{:S(2)}) %collective-permute-start.3) | collective-permute-done | bytes 24608 | tf_op jit(solution)/shard_map/ppermute | solution.py:437
  54.7 1.4 %passes.1 = f32[32,128]{1,0:T(8,128)} custom-call(f32[5,48,128]{2,1,0:T(8,128)S(1)} %get-tuple-element.29.wide, f32[48,128]{1,0:T(8,128)S(1)} %collective-permute-done.2.from_a, f32[48,128]{1,0:T(8,128)S(1)} %collective-permute-done.3.from_b, f32[32,128]{1,0:T(8,128)} %bitcast.49), custom_call_target="tpu_custom_call" | custom-call | bytes 1048576 | tf_op jit(solution)/shard_map/passes/pallas_call | solution.py:35
  (6 shorter events, 0.0 us)
Async XLA Ops:
  0.6 21.4 %copy-start.6 = (s32[1,32,128]{2,1,0:T(8,128)S(1)}, s32[1,32,128]{2,1,0:T(8,128)}, u32[]{:S(2)}) copy-start(s32[1,32,128]{2,1,0:T(8,128)} %param.13) | copy-start | bytes 49156
  2.4 21.8 %all-to-all-start = ((bf16[64,2,128]{2,1,0:T(2,128)(2,1)}), bf16[64,2,128]{2,1,0:T(2,128)(2,1)S(1)}, u32[]{:S(2)}, u32[]{:S(2)}) async-start(bf16[64,2,128]{2,1,0:T(2,128)(2,1)} %bitcast.2), calls=%async_computation | async-start | bytes 65536 | tf_op jit(solution)/shard_map/all_to_all | solution.py:449
  16.7 7.4 %copy-start = (bf16[1,1,1,32,2,128,128]{6,5,4,3,2,1,0:T(8,128)(2,1)S(1)}, bf16[1,1,1,32,2,128,128]{6,5,4,3,2,1,0:T(8,128)(2,1)}, u32[]{:S(2)}) copy-start(bf16[1,1,1,32,2,128,128]{6,5,4,3,2,1,0:T(8,128)(2,1)} %param.15) | copy-start | bytes 6291460
  16.7 7.4 %copy-start.2 = (s32[1,32,128]{2,1,0:T(8,128)S(1)}, s32[1,32,128]{2,1,0:T(8,128)}, u32[]{:S(2)}) copy-start(s32[1,32,128]{2,1,0:T(8,128)} %param.12) | copy-start | bytes 49156
  16.8 7.4 %copy-start.4 = (bf16[1,2,128,128]{3,2,1,0:T(8,128)(2,1)S(1)}, bf16[1,2,128,128]{3,2,1,0:T(8,128)(2,1)}, u32[]{:S(2)}) copy-start(bf16[1,2,128,128]{3,2,1,0:T(8,128)(2,1)} %param.14) | copy-start | bytes 196612
  18.9 16.2 %collective-permute-start = (bf16[7,128,128]{2,1,0:T(8,128)(2,1)}, bf16[7,128,128]{2,1,0:T(8,128)(2,1)S(1)}, u32[]{:S(2)}, u32[]{:S(2)}) collective-permute-start(bf16[7,128,128]{2,1,0:T(8,128)(2,1)} %get-tuple-element.24), channel_id=1, source_target_pairs={{384,392},{400,408},{416,424},{432,440},{448,456},{464,472},{480,4... | collective-permute-start | bytes 688136 | tf_op jit(solution)/shard_map/ppermute | solution.py:437
  22.0 4.2 %copy-start.3 = (bf16[1,1,32,128]{3,1,2,0:T(2,128)(2,1)}, bf16[1,1,32,128]{3,1,2,0:T(2,128)(2,1)S(1)}, u32[]{:S(2)}) copy-start(bf16[1,1,32,128]{3,1,2,0:T(2,128)(2,1)S(1)} %copy.18) | copy-start | bytes 24580
  23.7 2.5 %copy-start.1 = (bf16[16,8,32,128]{3,1,2,0:T(8,128)(2,1)}, bf16[16,8,32,128]{3,1,2,0:T(8,128)(2,1)S(1)}, u32[]{:S(2)}) copy-start(bf16[16,8,32,128]{3,1,2,0:T(8,128)(2,1)S(1)} %copy.17) | copy-start | bytes 3145732
  26.2 19.3 %all-to-all-start.1 = ((bf16[256,2,128]{2,1,0:T(2,128)(2,1)}), bf16[256,2,128]{2,1,0:T(2,128)(2,1)S(1)}, u32[]{:S(2)}, u32[]{:S(2)}) async-start(bf16[256,2,128]{2,1,0:T(2,128)(2,1)} %bitcast.12), calls=%async_computation.1 | async-start | bytes 262144 | tf_op jit(solution)/shard_map/all_to_all | solution.py:494
  35.1 9.4 %collective-permute-start.1 = (bf16[7,128,128]{2,1,0:T(8,128)(2,1)}, bf16[7,128,128]{2,1,0:T(8,128)(2,1)S(1)}, u32[]{:S(2)}, u32[]{:S(2)}) collective-permute-start(bf16[7,128,128]{2,1,0:T(8,128)(2,1)} %pass_edge.1), channel_id=1, source_target_pairs={{392,400},{408,416},{424,432},{440,448},{456,464},{472,480},{488,4... | collective-permute-start | bytes 688136 | tf_op jit(solution)/shard_map/ppermute | solution.py:437
  45.6 5.2 %copy-start.5 = (bf16[128,4096]{1,0:T(8,128)(2,1)S(1)}, bf16[128,4096]{1,0:T(8,128)(2,1)}, u32[]{:S(2)}) copy-start(bf16[128,4096]{1,0:T(8,128)(2,1)} %get-tuple-element.22) | copy-start | bytes 3145732
  46.6 5.5 %collective-permute-start.2 = (f32[48,128]{1,0:T(8,128)S(1)}, f32[48,128]{1,0:T(8,128)S(1)}, u32[]{:S(2)}, u32[]{:S(2)}) collective-permute-start(f32[48,128]{1,0:T(8,128)S(1)} %get-tuple-element.30), channel_id=1, source_target_pairs={{384,385},{386,387},{388,389},{390,391},{385,384},{387,386},{389,3... | collective-permute-start | bytes 73736 | tf_op jit(solution)/shard_map/ppermute | solution.py:437
  48.9 5.8 %collective-permute-start.3 = (f32[48,128]{1,0:T(8,128)S(1)}, f32[48,128]{1,0:T(8,128)S(1)}, u32[]{:S(2)}, u32[]{:S(2)}) collective-permute-start(f32[48,128]{1,0:T(8,128)S(1)} %get-tuple-element.31), channel_id=1, source_target_pairs={{385,386},{387,388},{389,390},{386,385},{388,387},{390,389},{393,3... | collective-permute-start | bytes 73736 | tf_op jit(solution)/shard_map/ppermute | solution.py:437

commit v5 on v4

--- a/solution.py
+++ b/solution.py
@@ -13,6 +13,7 @@
 NEAR = 3
 PLANES = 5
 WIDTH = 2048
+PIECES = 8
 MESSAGE = 8
 bf16 = jnp.bfloat16
 f32 = jnp.float32
@@ -52,6 +53,11 @@
     return copies
 
 
+def pieces(source, target):
+    size = source.shape[0] // PIECES
+    return [(source.at[n * size : (n + 1) * size], target.at[n * size : (n + 1) * size]) for n in range(PIECES)]
+
+
 def is_ocean():
     return lax.axis_index("sec") == lax.axis_size("sec") - 1
 
@@ -130,7 +136,7 @@
             copy.start()
 
     row = iota((hot_v.shape[0], 1), 0)
-    target, m = row >> 3, row & 7
+    target, m = (row >> 3) + lists_v.shape[1] - lax.axis_size("gx"), row & 7
     own = lax.axis_index("sec") * lax.axis_size("gx") + lax.axis_index("gx")
     of_edge = jnp.where(target == own + 1, rows - HALO + m, jnp.where(target == own - 1, m, -1))
     copies[-2].wait()
@@ -198,7 +204,7 @@
 
 def first_kernel(
     received, hot, weights, lowest_ref, sea, x_ref, flag_ref, mixing, hot_message,
-    message, carry, pick, low_f, carry_v, hot_v, sems,
+    message, carry, pick, low_f, carry_v, hot_v, message_v, sems,
 ):
     rows, tile = carry_v.shape
     pltpu.make_async_copy(hot_message, hot_v, sems.at[1]).start()
@@ -214,7 +220,10 @@
     def send(rows_of):
         pltpu.make_async_copy(hot_message, hot_v, sems.at[1]).wait()
         made = jnp.dot(hot_v[...], rows_of.astype(bf16), preferred_element_type=f32)
-        message[...] = made.astype(bf16)
+        message_v[...] = made.astype(bf16)
+        total, count = message.shape[0], message_v.shape[0]
+        (copy,) = fetch(sems.at[2:3], (message_v, message.at[total - count : total]))
+        copy.wait()
 
     @pl.when(is_ocean())
     def _():
@@ -247,19 +256,37 @@
 
 
 def second_kernel(
-    carry, x_ref, flag_ref, mixing, sea, out, made, carry_v, x_v, flag_v, mixing_v, sea_v, sems
+    carry, x_ref, flag_ref, mixing, sea, surface, diffusion, profile, sources,
+    out, mine, index,
+    carry_v, x_v, flag_v, mixing_v, sea_v, level_v, sources_v, sems, x_sems,
 ):
-    made[...] = jnp.zeros(made.shape, f32)
-
-    @pl.when(is_ocean())
-    def _():
-        fetch(sems, (x_ref, x_v))[0].wait()
-        fetch(sems, (x_v, out))[0].wait()
+    @pl.when(is_ocean())
+    def _():
+        held = fetch(x_sems, *pieces(x_ref, x_v))
+        copies = fetch(
+            sems,
+            (surface, mine.at[0]),
+            (diffusion, mine.at[1]),
+            (carry, mine.at[4]),
+            (sea, sea_v),
+            (profile.at[0, 0], level_v),
+            (sources, sources_v),
+        )
+        for copy in copies:
+            copy.wait()
+        mine[2] = sea_v[...].astype(f32)
+        mine[3] = level_v[...].astype(f32)
+        q = upright(sources_v[...])
+        index[...] = (q >> 1) * MESSAGE + (q & 1) + 2
+        for copy in held:
+            copy.wait()
+        for copy in fetch(x_sems, *pieces(x_v, out)):
+            copy.wait()
 
     @pl.when(jnp.logical_not(is_ocean()))
     def _():
-        pairs = ((carry, carry_v), (sea, sea_v), (mixing, mixing_v), (flag_ref, flag_v), (x_ref, x_v))
-        for copy in fetch(sems, *pairs):
+        pairs = ((carry, carry_v), (sea, sea_v), (mixing, mixing_v), (flag_ref, flag_v))
+        for copy in fetch(sems, *pairs) + fetch(x_sems, *pieces(x_ref, x_v)):
             copy.wait()
         mix = jnp.concatenate([mixing_v[0], mixing_v[1]], axis=1)
         sea_f = sea_v[...].astype(f32)
@@ -277,31 +304,16 @@
                 for _ in range(PHYS):
                     x = substep(x, flag, mix)
             x_v[:, cols] = x
-        fetch(sems, (x_v, out))[0].wait()
-
-
-def ready_kernel(
-    surface, diffusion, sea, profile, sources, carry, still_a, still_b, made,
-    hot, planes,
-    surface_v, diffusion_v, sea_v, level_v, sources_v, carry_v, sems,
-):
-    @pl.when(is_ocean())
-    def _():
-        rows, tile = surface_v.shape
+        for copy in fetch(x_sems, *pieces(x_v, out)):
+            copy.wait()
+
+
+def ready_kernel(mine, own_index, still_a, still_b, hot, planes):
+    @pl.when(is_ocean())
+    def _():
+        rows, tile = mine.shape[1:]
         total = rows + 2 * HALO
         even = is_even("gx")
-
-        copies = fetch(
-            sems,
-            (surface, surface_v),
-            (diffusion, diffusion_v),
-            (sea, sea_v),
-            (profile.at[0, 0], level_v),
-            (sources, sources_v),
-            (carry, carry_v),
-        )
-        for copy in copies:
-            copy.wait()
         edges = [still[2 * NEAR].astype(f32) for still in (still_a, still_b)]
         below = jnp.where(even, edges[0], edges[1])
         above = jnp.where(even, edges[1], edges[0])
@@ -313,26 +325,20 @@
                 held = [held[0] + below[part], held[1] + above[part]]
             return jnp.concatenate([values, *held], axis=0)
 
-        planes[0] = whole_of(surface_v[...], 0, 3)
-        planes[1] = whole_of(diffusion_v[...], 3 * HALO, 3)
-        planes[2] = whole_of(sea_v[...].astype(f32), 6 * HALO, 1)
-        planes[3] = whole_of(level_v[...].astype(f32), 7 * HALO, 1)
-        planes[4, 0:rows] = carry_v[...]
+        planes[0] = whole_of(mine[0], 0, 3)
+        planes[1] = whole_of(mine[1], 3 * HALO, 3)
+        planes[2] = whole_of(mine[2], 6 * HALO, 1)
+        planes[3] = whole_of(mine[3], 7 * HALO, 1)
+        planes[4, 0:rows] = mine[4]
         planes[4, rows:total] = jnp.zeros((2 * HALO, tile), f32)
 
         at = slice(8 * HALO, 8 * HALO + 2)
-        q = jnp.concatenate(
-            [
-                upright(sources_v[...]),
-                upright(below[at, 0:rows].astype(jnp.int32), 0, HALO),
-                upright(above[at, 0:rows].astype(jnp.int32), rows - HALO, HALO),
-            ],
-            axis=0,
-        )
-        row = iota((total, 1), 0)
-        offset = jnp.where(row < rows, 2, jnp.where(row < rows + HALO, 4, 0))
+        held = [own_index[...]]
+        for edge, first, offset in ((below, 0, 4), (above, rows - HALO, 0)):
+            q = upright(edge[at, 0:rows].astype(jnp.int32), first, HALO)
+            held.append((q >> 1) * MESSAGE + (q & 1) + offset)
+        q = jnp.concatenate(held, axis=0)
         place = iota((total, hot.shape[1]), 1)
-        q = (q >> 1) * MESSAGE + (q & 1) + offset
         own = lax.axis_index("sec") * lax.axis_size("gx") + lax.axis_index("gx")
         row = iota((2 * HALO, 1), 0)
         beyond = jnp.where(row < HALO, (own + 1) * MESSAGE, (own - 1) * MESSAGE - HALO) + row
@@ -461,12 +467,12 @@
         edges_kernel,
         "edge_rows",
         [*edge_operands, (lists, HBM)],
-        [edge, edge, ((2 * rows, senders * slots), bf16), ((senders * MESSAGE, rows), bf16, HBM)],
+        [edge, edge, ((2 * rows, senders * slots), bf16), ((gx * MESSAGE, rows), bf16, HBM)],
         [
             *edge_scratch,
             VMEM(lists.shape, jnp.int32),
             VMEM((2, *edge[0]), bf16),
-            VMEM((senders * MESSAGE, rows), bf16),
+            VMEM((gx * MESSAGE, rows), bf16),
             semaphores(9),
         ],
     )
@@ -481,13 +487,14 @@
             received.reshape(senders * slots, tile), hot_first, weights, lowest, sea, (columns, VMEM),
             flag, matrices, (hot_message, HBM),
         ],
-        [((senders * MESSAGE, tile), bf16), (grid, f32, HBM)],
+        [((senders * MESSAGE, tile), bf16, HBM), (grid, f32, HBM)],
         [
             VMEM((rows, 2 * tile), f32),
             VMEM(grid, f32),
             VMEM(grid, f32),
-            VMEM((senders * MESSAGE, rows), bf16),
-            semaphores(2),
+            VMEM((gx * MESSAGE, rows), bf16),
+            VMEM((gx * MESSAGE, tile), bf16),
+            semaphores(3),
         ],
         flops=1 << 34,
     )
@@ -496,28 +503,32 @@
     )
     (edge_b,) = call(pass_kernel, "pass_edge", [(edge_b, HBM), (carry, HBM), still_a], [edge], aliases={0: 0})
     still_b = swap("gx", 1, edge_b)
-    final, made = call(
+    final, mine, index = call(
         second_kernel,
         "second_step",
-        [(carry, HBM), (columns, HBM), (flag, HBM), (matrices, HBM), (sea, HBM)],
-        [((levels, cells), bf16, HBM), ((8, tile), f32)],
+        [
+            (v, HBM)
+            for v in (carry, columns, flag, matrices, sea, surface_2d, coefficient, profile, wanted)
+        ],
+        [((levels, cells), bf16, HBM), ((PLANES, *grid), f32), ((rows, 2), jnp.int32)],
         [
             VMEM(grid, f32),
             VMEM((levels, cells), bf16),
             VMEM((1, cells), bf16),
             VMEM(matrices.shape, bf16),
             VMEM(grid, jnp.int32),
-            semaphores(5),
+            VMEM(grid, bf16),
+            VMEM(wanted.shape, jnp.int32),
+            semaphores(6),
+            semaphores(PIECES),
         ],
         flops=1 << 34,
     )
-    picks = 2 * total + 2 * HALO
     hot, planes = call(
         ready_kernel,
         "ready_import",
-        [*edge_operands[:5], (carry, HBM), still_a, still_b, made],
-        [((picks, senders * MESSAGE), bf16), ((PLANES, total, tile), f32)],
-        [*edge_scratch, VMEM(grid, f32), semaphores(6)],
+        [mine, index, still_a, still_b],
+        [((2 * total + 2 * HALO, senders * MESSAGE), bf16), ((PLANES, total, tile), f32)],
     )
     wide, to_a, to_b = call(
         third_kernel,

time: 56.6 us -> 55.3 us (0.977)
  Pallas kernels: 11.6 us -> 10.4 us
    pallas_call x8, Pallas kernels: 11.6 us -> 10.4 us  [call(): pl.pallas_call(kernel, out_shape=shapes, in_specs=specs, out_specs=[pl.Bl...]
  transfers between devices with their start and end apart: 6 -> 6, of which waited for: 3 -> 3; matrix products, arithmetic and copies ran while one was open for 5% -> 5% of each run, Pallas kernels for 13% -> 12%
where the time goes in v5:
time: 55.3 us; the launch traced here: 54.8 us
  starting transfers between devices  35.3 us (64%)
  Pallas kernels  10.4 us (19%)
  waiting for transfers between devices  5.35 us (10%)
  local copies, waits for them, and re-layouts  2.93 us (5%)
  between operations  0.84 us (2%)
    all_to_all x1, starting transfers between devices, body(): lax.all_to_all(chosen.reshape(senders, slots, tile), ('sec', 'gx'), 0, 0,...  14.4 us
    ppermute x4, starting transfers between devices, swap(): lax.ppermute(values, ('sec', axis), pairs + [(t, s) for s, t in pairs])  11.9 us
    pallas_call x8, Pallas kernels, call(): pl.pallas_call(kernel, out_shape=shapes, in_specs=specs, out_specs=[pl.Bl...  10.4 us
    all_to_all x1, starting transfers between devices, body(): lax.all_to_all(message.reshape(senders * MESSAGE // 2, 2, tile), ('sec',...  9.02 us
    ppermute x4, waiting for transfers between devices, swap(): lax.ppermute(values, ('sec', axis), pairs + [(t, s) for s, t in pairs])  4.93 us
    unnamed x17, local copies, waits for them, and re-layouts  2.93 us
  transfers between devices with their start and end apart: 6, of which 3 were waited for; matrix products, arithmetic and copies ran while one was open for 5% of the time, Pallas kernels for 12%

profile of v5, /device:TPU:39, one launch (start us, length us, event | category | flops | bytes accessed | tf_op | source)
XLA Modules:
  0.0 54.8 jit_solution(16776067171602178008)
XLA Ops:
  0.6 0.0 copy-start.6
  0.6 1.7 %select_tiles.1 = (bf16[128,128]{1,0:T(8,128)(2,1)}, f32[32,128]{1,0:T(8,128)S(1)}) custom-call(bf16[1,128,32,128]{3,2,1,0:T(8,128)(2,1)} %profile.5, s32[2,64]{1,0:T(2,128)} %bitcast.53), custom_call_target="tpu_custom_call" | custom-call | bytes 1048576 | tf_op jit(solution)/shard_map/select_tiles/pallas_call | solution.py:36
  2.4 14.4 %all-to-all-start = ((bf16[64,2,128]{2,1,0:T(2,128)(2,1)}), bf16[64,2,128]{2,1,0:T(2,128)(2,1)S(1)}, u32[]{:S(2)}, u32[]{:S(2)}) async-start(bf16[64,2,128]{2,1,0:T(2,128)(2,1)} %bitcast.2), calls=%async_computation | async-start | bytes 65536 | tf_op jit(solution)/shard_map/all_to_all | solution.py:455
  16.7 0.0 copy-start
  16.8 0.0 copy-start.2
  16.8 0.0 copy-start.4
  16.8 2.1 %edge_rows.1 = (bf16[7,128,128]{2,1,0:T(8,128)(2,1)}, bf16[7,128,128]{2,1,0:T(8,128)(2,1)}, bf16[64,128]{1,0:T(8,128)(2,1)S(1)}, bf16[128,32]{1,0:T(8,128)(2,1)}) custom-call(f32[32,128]{1,0:T(8,128)} %bitcast.47, f32[32,128]{1,0:T(8,128)} %bitcast.50, s32[32,128]{1,0:T(8,128)} %bitcast.36, bf16[1,128,32,128]{3,2,1,0:T(8,128)(2,1)} %profile.5, ...), custom_call_target="tpu_custom_call" | custom-call | bytes 1048576 | tf_op jit(solution)/shard_map/edge_rows/pallas_call | solution.py:36
  18.9 3.1 %collective-permute-start = (bf16[7,128,128]{2,1,0:T(8,128)(2,1)}, bf16[7,128,128]{2,1,0:T(8,128)(2,1)S(1)}, u32[]{:S(2)}, u32[]{:S(2)}) collective-permute-start(bf16[7,128,128]{2,1,0:T(8,128)(2,1)} %get-tuple-element.27), channel_id=1, source_target_pairs={{384,392},{400,408},{416,424},{432,440},{448,456},{464,472},{480,4... | collective-permute-start | bytes 688136 | tf_op jit(solution)/shard_map/ppermute | solution.py:443
  22.0 0.0 copy-done.6
  22.0 0.0 copy-start.3
  22.0 1.7 %copy.17 = bf16[16,8,32,128]{3,1,2,0:T(8,128)(2,1)S(1)} copy(bf16[16,8,32,128]{3,2,1,0:T(8,128)(2,1)} %bitcast.43) | data formatting | bytes 2097152
  23.7 0.0 copy-start.1
  23.7 0.4 all-to-all-done
  24.1 0.0 copy-done
  24.1 0.0 copy-done.2
  24.1 1.6 %first_step.1 = (bf16[512,128]{1,0:T(8,128)(2,1)}, f32[32,128]{1,0:T(8,128)}) custom-call(bf16[128,128]{1,0:T(8,128)(2,1)S(1)} %bitcast.35, bf16[64,128]{1,0:T(8,128)(2,1)S(1)} %get-tuple-element.19.hot, bf16[64,128,128]{2,1,0:T(8,128)(2,1)S(1)} %bitcast.30, f32[32,128]{1,0:T(8,128)S(1)} %get-tuple-element.20.lowest_ref, s32[32,128]{1,0:T(8,128)S(1)} %bitcast.38, ...), custom_call_target="tpu_custom_call" | custom-call | flops 17179869184 | bytes 1048576 | tf_op jit(solution)/shard_map/first_step/pallas_call | solution.py:36
  25.7 9.0 %all-to-all-start.1 = ((bf16[256,2,128]{2,1,0:T(2,128)(2,1)}), bf16[256,2,128]{2,1,0:T(2,128)(2,1)S(1)}, u32[]{:S(2)}, u32[]{:S(2)}) async-start(bf16[256,2,128]{2,1,0:T(2,128)(2,1)} %bitcast.46), calls=%async_computation.1 | async-start | bytes 262144 | tf_op jit(solution)/shard_map/all_to_all | solution.py:501
  34.8 0.0 collective-permute-done.refs_1_.still_a
  34.8 4.6 %collective-permute-start.1 = (bf16[7,128,128]{2,1,0:T(8,128)(2,1)}, bf16[7,128,128]{2,1,0:T(8,128)(2,1)S(1)}, u32[]{:S(2)}, u32[]{:S(2)}) collective-permute-start(bf16[7,128,128]{2,1,0:T(8,128)(2,1)} %pass_edge.1), channel_id=1, source_target_pairs={{392,400},{408,416},{424,432},{440,448},{456,464},{472,480},{488,4... | collective-permute-start | bytes 688136 | tf_op jit(solution)/shard_map/ppermute | solution.py:443
  39.4 2.5 %second_step.1 = (bf16[128,4096]{1,0:T(8,128)(2,1)}, f32[5,32,128]{2,1,0:T(8,128)S(1)}, s32[32,2]{1,0:T(8,128)S(1)}) custom-call(f32[32,128]{1,0:T(8,128)} %get-tuple-element.22.carry.refs_0_, bf16[128,4096]{1,0:T(8,128)(2,1)} %bitcast.33, bf16[1,4096]{1,0:T(2,128)(2,1)} %bitcast.40, bf16[2,128,128]{2,1,0:T(8,128)(2,1)} %bitcast.41, s32[32,128]{1,0:T(8,128)} %bitcast.37, ...), custom_call_target="tpu_custom_call" | custom-call | flops 17179869184 | bytes 1048576 | tf_op jit(solution)/shard_map/second_step/pallas_call | solution.py:36
  41.8 2.3 %collective-permute-done.1.still_b = bf16[7,128,128]{2,1,0:T(8,128)(2,1)S(1)} collective-permute-done((bf16[7,128,128]{2,1,0:T(8,128)(2,1)}, bf16[7,128,128]{2,1,0:T(8,128)(2,1)S(1)}, u32[]{:S(2)}, u32[]{:S(2)}) %collective-permute-start.1) | collective-permute-done | bytes 229408 | tf_op jit(solution)/shard_map/ppermute | solution.py:443
  44.1 0.2 ready_import.1
  44.3 0.0 all-to-all-done.1
  44.4 0.0 copy-start.5
  44.4 1.0 %second_import.1 = (f32[5,48,128]{2,1,0:T(8,128)S(1)}, f32[48,128]{1,0:T(8,128)S(1)}, f32[48,128]{1,0:T(8,128)S(1)}) custom-call(bf16[512,128]{1,0:T(8,128)(2,1)S(1)} %bitcast.34, bf16[64,128,128]{2,1,0:T(8,128)(2,1)S(1)} %bitcast.31, bf16[112,512]{1,0:T(8,128)(2,1)S(1)} %get-tuple-element.29.hot, f32[5,48,128]{2,1,0:T(8,128)S(1)} %get-tuple-element.30.planes, ...), custom_call_target="tpu_custom_call" | custom-call | bytes 1048576 | tf_op jit(solution)/shard_map/second_import/pallas_call | solution.py:36
  45.3 2.3 %collective-permute-start.2 = (f32[48,128]{1,0:T(8,128)S(1)}, f32[48,128]{1,0:T(8,128)S(1)}, u32[]{:S(2)}, u32[]{:S(2)}) collective-permute-start(f32[48,128]{1,0:T(8,128)S(1)} %get-tuple-element.32), channel_id=1, source_target_pairs={{384,385},{386,387},{388,389},{390,391},{385,384},{387,386},{389,3... | collective-permute-start | bytes 73736 | tf_op jit(solution)/shard_map/ppermute | solution.py:443
  47.7 1.9 %collective-permute-start.3 = (f32[48,128]{1,0:T(8,128)S(1)}, f32[48,128]{1,0:T(8,128)S(1)}, u32[]{:S(2)}, u32[]{:S(2)}) collective-permute-start(f32[48,128]{1,0:T(8,128)S(1)} %get-tuple-element.33), channel_id=1, source_target_pairs={{385,386},{387,388},{389,390},{386,385},{388,387},{390,389},{393,3... | collective-permute-start | bytes 73736 | tf_op jit(solution)/shard_map/ppermute | solution.py:443
  49.6 0.0 copy-done.5
  49.6 1.2 %copy.14 = bf16[16,8,32,128]{3,2,1,0:T(8,128)(2,1)} copy(bf16[16,8,32,128]{3,1,2,0:T(8,128)(2,1)S(1)} %bitcast.44) | data formatting | bytes 2097152
  50.8 0.0 collective-permute-done.2.from_a
  50.8 2.6 %collective-permute-done.3.from_b = f32[48,128]{1,0:T(8,128)S(1)} collective-permute-done((f32[48,128]{1,0:T(8,128)S(1)}, f32[48,128]{1,0:T(8,128)S(1)}, u32[]{:S(2)}, u32[]{:S(2)}) %collective-permute-start.3) | collective-permute-done | bytes 24608 | tf_op jit(solution)/shard_map/ppermute | solution.py:443
  53.4 1.4 %passes.1 = f32[32,128]{1,0:T(8,128)} custom-call(f32[5,48,128]{2,1,0:T(8,128)S(1)} %get-tuple-element.31.wide, f32[48,128]{1,0:T(8,128)S(1)} %collective-permute-done.2.from_a, f32[48,128]{1,0:T(8,128)S(1)} %collective-permute-done.3.from_b, f32[32,128]{1,0:T(8,128)} %bitcast.49), custom_call_target="tpu_custom_call" | custom-call | bytes 1048576 | tf_op jit(solution)/shard_map/passes/pallas_call | solution.py:36
  (6 shorter events, 0.0 us)
Async XLA Ops:
  0.6 21.3 %copy-start.6 = (s32[1,32,128]{2,1,0:T(8,128)S(1)}, s32[1,32,128]{2,1,0:T(8,128)}, u32[]{:S(2)}) copy-start(s32[1,32,128]{2,1,0:T(8,128)} %param.13) | copy-start | bytes 49156
  2.4 21.8 %all-to-all-start = ((bf16[64,2,128]{2,1,0:T(2,128)(2,1)}), bf16[64,2,128]{2,1,0:T(2,128)(2,1)S(1)}, u32[]{:S(2)}, u32[]{:S(2)}) async-start(bf16[64,2,128]{2,1,0:T(2,128)(2,1)} %bitcast.2), calls=%async_computation | async-start | bytes 65536 | tf_op jit(solution)/shard_map/all_to_all | solution.py:455
  16.7 7.4 %copy-start = (bf16[1,1,1,32,2,128,128]{6,5,4,3,2,1,0:T(8,128)(2,1)S(1)}, bf16[1,1,1,32,2,128,128]{6,5,4,3,2,1,0:T(8,128)(2,1)}, u32[]{:S(2)}) copy-start(bf16[1,1,1,32,2,128,128]{6,5,4,3,2,1,0:T(8,128)(2,1)} %param.15) | copy-start | bytes 6291460
  16.8 7.4 %copy-start.2 = (s32[1,32,128]{2,1,0:T(8,128)S(1)}, s32[1,32,128]{2,1,0:T(8,128)}, u32[]{:S(2)}) copy-start(s32[1,32,128]{2,1,0:T(8,128)} %param.12) | copy-start | bytes 49156
  16.8 7.4 %copy-start.4 = (bf16[1,2,128,128]{3,2,1,0:T(8,128)(2,1)S(1)}, bf16[1,2,128,128]{3,2,1,0:T(8,128)(2,1)}, u32[]{:S(2)}) copy-start(bf16[1,2,128,128]{3,2,1,0:T(8,128)(2,1)} %param.14) | copy-start | bytes 196612
  18.9 15.9 %collective-permute-start = (bf16[7,128,128]{2,1,0:T(8,128)(2,1)}, bf16[7,128,128]{2,1,0:T(8,128)(2,1)S(1)}, u32[]{:S(2)}, u32[]{:S(2)}) collective-permute-start(bf16[7,128,128]{2,1,0:T(8,128)(2,1)} %get-tuple-element.27), channel_id=1, source_target_pairs={{384,392},{400,408},{416,424},{432,440},{448,456},{464,472},{480,4... | collective-permute-start | bytes 688136 | tf_op jit(solution)/shard_map/ppermute | solution.py:443
  22.0 3.7 %copy-start.3 = (bf16[1,1,32,128]{3,1,2,0:T(2,128)(2,1)}, bf16[1,1,32,128]{3,1,2,0:T(2,128)(2,1)S(1)}, u32[]{:S(2)}) copy-start(bf16[1,1,32,128]{3,1,2,0:T(2,128)(2,1)S(1)} %copy.18) | copy-start | bytes 24580
  23.7 2.0 %copy-start.1 = (bf16[16,8,32,128]{3,1,2,0:T(8,128)(2,1)}, bf16[16,8,32,128]{3,1,2,0:T(8,128)(2,1)S(1)}, u32[]{:S(2)}) copy-start(bf16[16,8,32,128]{3,1,2,0:T(8,128)(2,1)S(1)} %copy.17) | copy-start | bytes 3145732
  25.7 18.6 %all-to-all-start.1 = ((bf16[256,2,128]{2,1,0:T(2,128)(2,1)}), bf16[256,2,128]{2,1,0:T(2,128)(2,1)S(1)}, u32[]{:S(2)}, u32[]{:S(2)}) async-start(bf16[256,2,128]{2,1,0:T(2,128)(2,1)} %bitcast.46), calls=%async_computation.1 | async-start | bytes 262144 | tf_op jit(solution)/shard_map/all_to_all | solution.py:501
  34.8 9.4 %collective-permute-start.1 = (bf16[7,128,128]{2,1,0:T(8,128)(2,1)}, bf16[7,128,128]{2,1,0:T(8,128)(2,1)S(1)}, u32[]{:S(2)}, u32[]{:S(2)}) collective-permute-start(bf16[7,128,128]{2,1,0:T(8,128)(2,1)} %pass_edge.1), channel_id=1, source_target_pairs={{392,400},{408,416},{424,432},{440,448},{456,464},{472,480},{488,4... | collective-permute-start | bytes 688136 | tf_op jit(solution)/shard_map/ppermute | solution.py:443
  44.4 5.2 %copy-start.5 = (bf16[128,4096]{1,0:T(8,128)(2,1)S(1)}, bf16[128,4096]{1,0:T(8,128)(2,1)}, u32[]{:S(2)}) copy-start(bf16[128,4096]{1,0:T(8,128)(2,1)} %get-tuple-element.23) | copy-start | bytes 3145732
  45.3 5.5 %collective-permute-start.2 = (f32[48,128]{1,0:T(8,128)S(1)}, f32[48,128]{1,0:T(8,128)S(1)}, u32[]{:S(2)}, u32[]{:S(2)}) collective-permute-start(f32[48,128]{1,0:T(8,128)S(1)} %get-tuple-element.32), channel_id=1, source_target_pairs={{384,385},{386,387},{388,389},{390,391},{385,384},{387,386},{389,3... | collective-permute-start | bytes 73736 | tf_op jit(solution)/shard_map/ppermute | solution.py:443
  47.7 5.8 %collective-permute-start.3 = (f32[48,128]{1,0:T(8,128)S(1)}, f32[48,128]{1,0:T(8,128)S(1)}, u32[]{:S(2)}, u32[]{:S(2)}) collective-permute-start(f32[48,128]{1,0:T(8,128)S(1)} %get-tuple-element.33), channel_id=1, source_target_pairs={{385,386},{387,388},{389,390},{386,385},{388,387},{390,389},{393,3... | collective-permute-start | bytes 73736 | tf_op jit(solution)/shard_map/ppermute | solution.py:443

commit v6 on v5

--- a/solution.py
+++ b/solution.py
@@ -66,6 +66,10 @@
     return lax.rem(lax.axis_index(axis), 2) == 0
 
 
+def next_first():
+    return jnp.logical_not(is_even("gx"))
+
+
 def iota(shape, dim):
     return lax.broadcasted_iota(jnp.int32, shape, dim)
 
@@ -114,7 +118,7 @@
 ):
     rows, size = surface_v.shape
     count = 2 * NEAR
-    last = is_even("gx")
+    last = next_first()
     near = jnp.where(last, 2 * rows - count, 0)
     pairs = (
         (weights.at[pl.ds(near, count)], edge_v.at[0, 0:count]),
@@ -179,10 +183,25 @@
     pass
 
 
-def import_row(pick_ref, a, first, second):
-    row = pick_ref[a : a + 1, :].astype(bf16)
-    block = jnp.concatenate([first, second], axis=1)
-    return lax.dot_general(row, block, (((1,), (1,)), ((), ())), preferred_element_type=f32)
+def import_group(pick, first, blocks):
+    rows = pick[first : first + 8, :].astype(bf16)
+    size = pick.shape[1] // 2
+    place = iota((8, size), 0)
+    held = sorted(blocks)
+    made = jnp.zeros((8, size), f32)
+    for at in range(0, len(held), 2):
+        pair = held[at : at + 2]
+        block = jnp.concatenate([jnp.concatenate(blocks[n], axis=1) for n in pair], axis=0)
+        found = lax.dot_general(rows, block, (((1,), (1,)), ((), ())), preferred_element_type=f32)
+        for m, n in enumerate(pair):
+            made = jnp.where(place == n, found[:, m * size : (m + 1) * size], made)
+    return made
+
+
+def import_rows(pick, weights, out, rows):
+    for first in range(0, rows, 8):
+        blocks = {n: (weights[2 * (first + n)], weights[2 * (first + n) + 1]) for n in range(8)}
+        out[first : first + 8] = import_group(pick, first, blocks)
 
 
 def substep(x, flag, mix):
@@ -211,8 +230,7 @@
     picked = jnp.dot(hot[...], received[...], preferred_element_type=f32)
     pick[:, 0:tile] = picked[0:rows]
     pick[:, tile : 2 * tile] = picked[rows : 2 * rows]
-    for a in range(rows):
-        carry_v[a : a + 1, :] = import_row(pick, a, weights[2 * a], weights[2 * a + 1])
+    import_rows(pick, weights, carry_v, rows)
     lowest = lowest_ref[...]
     flux = sea[...].astype(f32) * (carry_v[...] - lowest)
     kept = pltpu.make_async_copy(carry_v, carry, sems.at[0])
@@ -313,7 +331,7 @@
     def _():
         rows, tile = mine.shape[1:]
         total = rows + 2 * HALO
-        even = is_even("gx")
+        even = next_first()
         edges = [still[2 * NEAR].astype(f32) for still in (still_a, still_b)]
         below = jnp.where(even, edges[0], edges[1])
         above = jnp.where(even, edges[1], edges[0])
@@ -358,14 +376,17 @@
         picked = jnp.dot(hot[...], received[...], preferred_element_type=f32)
         pick[:, 0:tile] = picked[0:total]
         pick[:, tile : 2 * tile] = picked[total : 2 * total]
-        imported[rows:total] = jnp.zeros((2 * HALO, tile), f32)
-        for a in range(rows):
-            imported[a : a + 1, :] = import_row(pick, a, weights[2 * a], weights[2 * a + 1])
-        from_next = is_even("gx")
-        for n in range(NEAR):
-            for a, first in ((rows + n, from_next), (total - NEAR + n, jnp.logical_not(from_next))):
-                blocks = [jnp.where(first, still_a[2 * n + k], still_b[2 * n + k]) for k in range(2)]
-                imported[a : a + 1, :] = import_row(pick, a, blocks[0], blocks[1])
+        import_rows(pick, weights, imported, rows)
+        below_first = next_first()
+        for start, last, pair in (
+            (rows, False, (still_a, still_b)),
+            (rows + HALO, True, (still_b, still_a)),
+        ):
+            blocks = {}
+            for n in range(NEAR):
+                block = [jnp.where(below_first, pair[0][2 * n + k], pair[1][2 * n + k]) for k in range(2)]
+                blocks[HALO - NEAR + n if last else n] = block
+            imported[start : start + HALO] = import_group(pick, start, blocks)
         fields = [
             jnp.concatenate([planes[4, 0:rows], picked[2 * total :]], axis=0),
             planes[2] * (imported[...] - planes[3]) * (1.0 / PASSES),
@@ -476,7 +497,7 @@
             semaphores(9),
         ],
     )
-    still_a = swap("gx", 0, edge_a)
+    still_a = swap("gx", 1, edge_a)
 
     columns = profile.reshape(levels, cells)
     flag = convective.reshape(1, cells).astype(bf16)
@@ -502,7 +523,7 @@
         message.reshape(senders * MESSAGE // 2, 2, tile), ("sec", "gx"), 0, 0, tiled=True
     )
     (edge_b,) = call(pass_kernel, "pass_edge", [(edge_b, HBM), (carry, HBM), still_a], [edge], aliases={0: 0})
-    still_b = swap("gx", 1, edge_b)
+    still_b = swap("gx", 0, edge_b)
     final, mine, index = call(
         second_kernel,
         "second_step",

time: 55.3 us -> 54.9 us (level)
  starting transfers between devices: 35.3 us -> 34.1 us
  waiting for transfers between devices: 5.35 us -> 6.13 us
    all_to_all x1, waiting for transfers between devices: 0.01 us -> 1.49 us  [body(): lax.all_to_all(message.reshape(senders * MESSAGE // 2, 2, tile), ('sec',...]
    all_to_all x1, starting transfers between devices: 9.02 us -> 7.85 us  [body(): lax.all_to_all(message.reshape(senders * MESSAGE // 2, 2, tile), ('sec',...]
where the time goes in v6:
time: 54.9 us; the launch traced here: 54.4 us
  starting transfers between devices  34.1 us (62%)
  Pallas kernels  10.3 us (19%)
  waiting for transfers between devices  6.13 us (11%)
  local copies, waits for them, and re-layouts  2.93 us (5%)
  between operations  0.86 us (2%)
    all_to_all x1, starting transfers between devices, body(): lax.all_to_all(chosen.reshape(senders, slots, tile), ('sec', 'gx'), 0, 0,...  14.4 us
    ppermute x4, starting transfers between devices, swap(): lax.ppermute(values, ('sec', axis), pairs + [(t, s) for s, t in pairs])  11.9 us
    pallas_call x8, Pallas kernels, call(): pl.pallas_call(kernel, out_shape=shapes, in_specs=specs, out_specs=[pl.Bl...  10.3 us
    all_to_all x1, starting transfers between devices, body(): lax.all_to_all(message.reshape(senders * MESSAGE // 2, 2, tile), ('sec',...  7.85 us
    ppermute x4, waiting for transfers between devices, swap(): lax.ppermute(values, ('sec', axis), pairs + [(t, s) for s, t in pairs])  4.64 us
    unnamed x17, local copies, waits for them, and re-layouts  2.93 us
    all_to_all x1, waiting for transfers between devices, body(): lax.all_to_all(message.reshape(senders * MESSAGE // 2, 2, tile), ('sec',...  1.49 us
  transfers between devices with their start and end apart: 6, of which 3 were waited for; matrix products, arithmetic and copies ran while one was open for 5% of the time, Pallas kernels for 12%

profile of v6, /device:TPU:39, one launch (start us, length us, event | category | flops | bytes accessed | tf_op | source)
XLA Modules:
  0.0 54.4 jit_solution(12630401639247966953)
XLA Ops:
  0.6 0.0 copy-start.6
  0.6 1.7 %select_tiles.1 = (bf16[128,128]{1,0:T(8,128)(2,1)}, f32[32,128]{1,0:T(8,128)S(1)}) custom-call(bf16[1,128,32,128]{3,2,1,0:T(8,128)(2,1)} %profile.5, s32[2,64]{1,0:T(2,128)} %bitcast.53), custom_call_target="tpu_custom_call" | custom-call | bytes 1048576 | tf_op jit(solution)/shard_map/select_tiles/pallas_call | solution.py:36
  2.4 14.4 %all-to-all-start = ((bf16[64,2,128]{2,1,0:T(2,128)(2,1)}), bf16[64,2,128]{2,1,0:T(2,128)(2,1)S(1)}, u32[]{:S(2)}, u32[]{:S(2)}) async-start(bf16[64,2,128]{2,1,0:T(2,128)(2,1)} %bitcast.2), calls=%async_computation | async-start | bytes 65536 | tf_op jit(solution)/shard_map/all_to_all | solution.py:476
  16.7 0.0 copy-start
  16.8 0.0 copy-start.2
  16.8 0.0 copy-start.4
  16.8 2.1 %edge_rows.1 = (bf16[7,128,128]{2,1,0:T(8,128)(2,1)}, bf16[7,128,128]{2,1,0:T(8,128)(2,1)}, bf16[64,128]{1,0:T(8,128)(2,1)S(1)}, bf16[128,32]{1,0:T(8,128)(2,1)}) custom-call(f32[32,128]{1,0:T(8,128)} %bitcast.47, f32[32,128]{1,0:T(8,128)} %bitcast.50, s32[32,128]{1,0:T(8,128)} %bitcast.36, bf16[1,128,32,128]{3,2,1,0:T(8,128)(2,1)} %profile.5, ...), custom_call_target="tpu_custom_call" | custom-call | bytes 1048576 | tf_op jit(solution)/shard_map/edge_rows/pallas_call | solution.py:36
  18.9 4.6 %collective-permute-start = (bf16[7,128,128]{2,1,0:T(8,128)(2,1)}, bf16[7,128,128]{2,1,0:T(8,128)(2,1)S(1)}, u32[]{:S(2)}, u32[]{:S(2)}) collective-permute-start(bf16[7,128,128]{2,1,0:T(8,128)(2,1)} %get-tuple-element.27), channel_id=1, source_target_pairs={{392,400},{408,416},{424,432},{440,448},{456,464},{472,480},{488,4... | collective-permute-start | bytes 688136 | tf_op jit(solution)/shard_map/ppermute | solution.py:464
  23.5 0.0 copy-done.6
  23.5 0.0 copy-start.3
  23.5 1.7 %copy.17 = bf16[16,8,32,128]{3,1,2,0:T(8,128)(2,1)S(1)} copy(bf16[16,8,32,128]{3,2,1,0:T(8,128)(2,1)} %bitcast.43) | data formatting | bytes 2097152
  25.2 0.0 copy-start.1
  25.2 0.0 all-to-all-done
  25.2 0.0 copy-done
  25.2 0.0 copy-done.2
  25.2 0.0 copy-done.4
  25.2 1.6 %first_step.1 = (bf16[512,128]{1,0:T(8,128)(2,1)}, f32[32,128]{1,0:T(8,128)}) custom-call(bf16[128,128]{1,0:T(8,128)(2,1)S(1)} %bitcast.35, bf16[64,128]{1,0:T(8,128)(2,1)S(1)} %get-tuple-element.19.hot, bf16[64,128,128]{2,1,0:T(8,128)(2,1)S(1)} %bitcast.30, f32[32,128]{1,0:T(8,128)S(1)} %get-tuple-element.20.lowest_ref, s32[32,128]{1,0:T(8,128)S(1)} %bitcast.38, ...), custom_call_target="tpu_custom_call" | custom-call | flops 17179869184 | bytes 1048576 | tf_op jit(solution)/shard_map/first_step/pallas_call | solution.py:36
  26.8 7.9 %all-to-all-start.1 = ((bf16[256,2,128]{2,1,0:T(2,128)(2,1)}), bf16[256,2,128]{2,1,0:T(2,128)(2,1)S(1)}, u32[]{:S(2)}, u32[]{:S(2)}) async-start(bf16[256,2,128]{2,1,0:T(2,128)(2,1)} %bitcast.46), calls=%async_computation.1 | async-start | bytes 262144 | tf_op jit(solution)/shard_map/all_to_all | solution.py:522
  34.7 0.0 collective-permute-done.refs_1_.still_a
  34.7 3.1 %collective-permute-start.1 = (bf16[7,128,128]{2,1,0:T(8,128)(2,1)}, bf16[7,128,128]{2,1,0:T(8,128)(2,1)S(1)}, u32[]{:S(2)}, u32[]{:S(2)}) collective-permute-start(bf16[7,128,128]{2,1,0:T(8,128)(2,1)} %pass_edge.1), channel_id=1, source_target_pairs={{384,392},{400,408},{416,424},{432,440},{448,456},{464,472},{480,4... | collective-permute-start | bytes 688136 | tf_op jit(solution)/shard_map/ppermute | solution.py:464
  37.8 2.5 %second_step.1 = (bf16[128,4096]{1,0:T(8,128)(2,1)}, f32[5,32,128]{2,1,0:T(8,128)S(1)}, s32[32,2]{1,0:T(8,128)S(1)}) custom-call(f32[32,128]{1,0:T(8,128)} %get-tuple-element.22.carry.refs_0_, bf16[128,4096]{1,0:T(8,128)(2,1)} %bitcast.33, bf16[1,4096]{1,0:T(2,128)(2,1)} %bitcast.40, bf16[2,128,128]{2,1,0:T(8,128)(2,1)} %bitcast.41, s32[32,128]{1,0:T(8,128)} %bitcast.37, ...), custom_call_target="tpu_custom_call" | custom-call | flops 17179869184 | bytes 1048576 | tf_op jit(solution)/shard_map/second_step/pallas_call | solution.py:36
  40.3 2.0 %collective-permute-done.1.still_b = bf16[7,128,128]{2,1,0:T(8,128)(2,1)S(1)} collective-permute-done((bf16[7,128,128]{2,1,0:T(8,128)(2,1)}, bf16[7,128,128]{2,1,0:T(8,128)(2,1)S(1)}, u32[]{:S(2)}, u32[]{:S(2)}) %collective-permute-start.1) | collective-permute-done | bytes 229408 | tf_op jit(solution)/shard_map/ppermute | solution.py:464
  42.3 0.2 ready_import.1
  42.5 1.5 %all-to-all-done.1 = bf16[256,2,128]{2,1,0:T(2,128)(2,1)S(1)} async-done(((bf16[256,2,128]{2,1,0:T(2,128)(2,1)}), bf16[256,2,128]{2,1,0:T(2,128)(2,1)S(1)}, u32[]{:S(2)}, u32[]{:S(2)}) %all-to-all-start.1) | async-done | bytes 131104 | tf_op jit(solution)/shard_map/all_to_all | solution.py:522
  44.0 0.9 %second_import.1 = (f32[5,48,128]{2,1,0:T(8,128)S(1)}, f32[48,128]{1,0:T(8,128)S(1)}, f32[48,128]{1,0:T(8,128)S(1)}) custom-call(bf16[512,128]{1,0:T(8,128)(2,1)S(1)} %bitcast.34, bf16[64,128,128]{2,1,0:T(8,128)(2,1)S(1)} %bitcast.31, bf16[112,512]{1,0:T(8,128)(2,1)S(1)} %get-tuple-element.29.hot, f32[5,48,128]{2,1,0:T(8,128)S(1)} %get-tuple-element.30.planes, ...), custom_call_target="tpu_custom_call" | custom-call | bytes 1048576 | tf_op jit(solution)/shard_map/second_import/pallas_call | solution.py:36
  44.9 2.3 %collective-permute-start.2 = (f32[48,128]{1,0:T(8,128)S(1)}, f32[48,128]{1,0:T(8,128)S(1)}, u32[]{:S(2)}, u32[]{:S(2)}) collective-permute-start(f32[48,128]{1,0:T(8,128)S(1)} %get-tuple-element.32), channel_id=1, source_target_pairs={{384,385},{386,387},{388,389},{390,391},{385,384},{387,386},{389,3... | collective-permute-start | bytes 73736 | tf_op jit(solution)/shard_map/ppermute | solution.py:464
  47.2 1.9 %collective-permute-start.3 = (f32[48,128]{1,0:T(8,128)S(1)}, f32[48,128]{1,0:T(8,128)S(1)}, u32[]{:S(2)}, u32[]{:S(2)}) collective-permute-start(f32[48,128]{1,0:T(8,128)S(1)} %get-tuple-element.33), channel_id=1, source_target_pairs={{385,386},{387,388},{389,390},{386,385},{388,387},{390,389},{393,3... | collective-permute-start | bytes 73736 | tf_op jit(solution)/shard_map/ppermute | solution.py:464
  49.2 0.0 copy-done.5
  49.2 1.2 %copy.14 = bf16[16,8,32,128]{3,2,1,0:T(8,128)(2,1)} copy(bf16[16,8,32,128]{3,1,2,0:T(8,128)(2,1)S(1)} %bitcast.44) | data formatting | bytes 2097152
  50.4 0.0 collective-permute-done.2.from_a
  50.4 2.6 %collective-permute-done.3.from_b = f32[48,128]{1,0:T(8,128)S(1)} collective-permute-done((f32[48,128]{1,0:T(8,128)S(1)}, f32[48,128]{1,0:T(8,128)S(1)}, u32[]{:S(2)}, u32[]{:S(2)}) %collective-permute-start.3) | collective-permute-done | bytes 24608 | tf_op jit(solution)/shard_map/ppermute | solution.py:464
  53.0 1.4 %passes.1 = f32[32,128]{1,0:T(8,128)} custom-call(f32[5,48,128]{2,1,0:T(8,128)S(1)} %get-tuple-element.31.wide, f32[48,128]{1,0:T(8,128)S(1)} %collective-permute-done.2.from_a, f32[48,128]{1,0:T(8,128)S(1)} %collective-permute-done.3.from_b, f32[32,128]{1,0:T(8,128)} %bitcast.49), custom_call_target="tpu_custom_call" | custom-call | bytes 1048576 | tf_op jit(solution)/shard_map/passes/pallas_call | solution.py:36
  (6 shorter events, 0.0 us)
Async XLA Ops:
  0.6 22.8 %copy-start.6 = (s32[1,32,128]{2,1,0:T(8,128)S(1)}, s32[1,32,128]{2,1,0:T(8,128)}, u32[]{:S(2)}) copy-start(s32[1,32,128]{2,1,0:T(8,128)} %param.13) | copy-start | bytes 49156
  2.4 22.8 %all-to-all-start = ((bf16[64,2,128]{2,1,0:T(2,128)(2,1)}), bf16[64,2,128]{2,1,0:T(2,128)(2,1)S(1)}, u32[]{:S(2)}, u32[]{:S(2)}) async-start(bf16[64,2,128]{2,1,0:T(2,128)(2,1)} %bitcast.2), calls=%async_computation | async-start | bytes 65536 | tf_op jit(solution)/shard_map/all_to_all | solution.py:476
  16.7 8.5 %copy-start = (bf16[1,1,1,32,2,128,128]{6,5,4,3,2,1,0:T(8,128)(2,1)S(1)}, bf16[1,1,1,32,2,128,128]{6,5,4,3,2,1,0:T(8,128)(2,1)}, u32[]{:S(2)}) copy-start(bf16[1,1,1,32,2,128,128]{6,5,4,3,2,1,0:T(8,128)(2,1)} %param.15) | copy-start | bytes 6291460
  16.8 8.5 %copy-start.2 = (s32[1,32,128]{2,1,0:T(8,128)S(1)}, s32[1,32,128]{2,1,0:T(8,128)}, u32[]{:S(2)}) copy-start(s32[1,32,128]{2,1,0:T(8,128)} %param.12) | copy-start | bytes 49156
  16.8 8.5 %copy-start.4 = (bf16[1,2,128,128]{3,2,1,0:T(8,128)(2,1)S(1)}, bf16[1,2,128,128]{3,2,1,0:T(8,128)(2,1)}, u32[]{:S(2)}) copy-start(bf16[1,2,128,128]{3,2,1,0:T(8,128)(2,1)} %param.14) | copy-start | bytes 196612
  18.9 15.8 %collective-permute-start = (bf16[7,128,128]{2,1,0:T(8,128)(2,1)}, bf16[7,128,128]{2,1,0:T(8,128)(2,1)S(1)}, u32[]{:S(2)}, u32[]{:S(2)}) collective-permute-start(bf16[7,128,128]{2,1,0:T(8,128)(2,1)} %get-tuple-element.27), channel_id=1, source_target_pairs={{392,400},{408,416},{424,432},{440,448},{456,464},{472,480},{488,4... | collective-permute-start | bytes 688136 | tf_op jit(solution)/shard_map/ppermute | solution.py:464
  23.5 3.3 %copy-start.3 = (bf16[1,1,32,128]{3,1,2,0:T(2,128)(2,1)}, bf16[1,1,32,128]{3,1,2,0:T(2,128)(2,1)S(1)}, u32[]{:S(2)}) copy-start(bf16[1,1,32,128]{3,1,2,0:T(2,128)(2,1)S(1)} %copy.18) | copy-start | bytes 24580
  25.2 1.6 %copy-start.1 = (bf16[16,8,32,128]{3,1,2,0:T(8,128)(2,1)}, bf16[16,8,32,128]{3,1,2,0:T(8,128)(2,1)S(1)}, u32[]{:S(2)}) copy-start(bf16[16,8,32,128]{3,1,2,0:T(8,128)(2,1)S(1)} %copy.17) | copy-start | bytes 3145732
  26.8 17.2 %all-to-all-start.1 = ((bf16[256,2,128]{2,1,0:T(2,128)(2,1)}), bf16[256,2,128]{2,1,0:T(2,128)(2,1)S(1)}, u32[]{:S(2)}, u32[]{:S(2)}) async-start(bf16[256,2,128]{2,1,0:T(2,128)(2,1)} %bitcast.46), calls=%async_computation.1 | async-start | bytes 262144 | tf_op jit(solution)/shard_map/all_to_all | solution.py:522
  34.7 7.6 %collective-permute-start.1 = (bf16[7,128,128]{2,1,0:T(8,128)(2,1)}, bf16[7,128,128]{2,1,0:T(8,128)(2,1)S(1)}, u32[]{:S(2)}, u32[]{:S(2)}) collective-permute-start(bf16[7,128,128]{2,1,0:T(8,128)(2,1)} %pass_edge.1), channel_id=1, source_target_pairs={{384,392},{400,408},{416,424},{432,440},{448,456},{464,472},{480,4... | collective-permute-start | bytes 688136 | tf_op jit(solution)/shard_map/ppermute | solution.py:464
  44.0 5.2 %copy-start.5 = (bf16[128,4096]{1,0:T(8,128)(2,1)S(1)}, bf16[128,4096]{1,0:T(8,128)(2,1)}, u32[]{:S(2)}) copy-start(bf16[128,4096]{1,0:T(8,128)(2,1)} %get-tuple-element.23) | copy-start | bytes 3145732
  44.9 5.5 %collective-permute-start.2 = (f32[48,128]{1,0:T(8,128)S(1)}, f32[48,128]{1,0:T(8,128)S(1)}, u32[]{:S(2)}, u32[]{:S(2)}) collective-permute-start(f32[48,128]{1,0:T(8,128)S(1)} %get-tuple-element.32), channel_id=1, source_target_pairs={{384,385},{386,387},{388,389},{390,391},{385,384},{387,386},{389,3... | collective-permute-start | bytes 73736 | tf_op jit(solution)/shard_map/ppermute | solution.py:464
  47.2 5.8 %collective-permute-start.3 = (f32[48,128]{1,0:T(8,128)S(1)}, f32[48,128]{1,0:T(8,128)S(1)}, u32[]{:S(2)}, u32[]{:S(2)}) collective-permute-start(f32[48,128]{1,0:T(8,128)S(1)} %get-tuple-element.33), channel_id=1, source_target_pairs={{385,386},{387,388},{389,390},{386,385},{388,387},{390,389},{393,3... | collective-permute-start | bytes 73736 | tf_op jit(solution)/shard_map/ppermute | solution.py:464

commit v7 on v6

--- a/solution.py
+++ b/solution.py
@@ -198,10 +198,13 @@
     return made
 
 
-def import_rows(pick, weights, out, rows):
-    for first in range(0, rows, 8):
-        blocks = {n: (weights[2 * (first + n)], weights[2 * (first + n) + 1]) for n in range(8)}
-        out[first : first + 8] = import_group(pick, first, blocks)
+def import_rows(pick, weights, out, first, count):
+    made = []
+    for at in range(first, first + count, 8):
+        blocks = {n: (weights[2 * (at + n)], weights[2 * (at + n) + 1]) for n in range(8)}
+        made.append(import_group(pick, at, blocks))
+        out[at : at + 8] = made[-1]
+    return jnp.concatenate(made, axis=0)
 
 
 def substep(x, flag, mix):
@@ -230,9 +233,8 @@
     picked = jnp.dot(hot[...], received[...], preferred_element_type=f32)
     pick[:, 0:tile] = picked[0:rows]
     pick[:, tile : 2 * tile] = picked[rows : 2 * rows]
-    import_rows(pick, weights, carry_v, rows)
     lowest = lowest_ref[...]
-    flux = sea[...].astype(f32) * (carry_v[...] - lowest)
+    sea_f = sea[...].astype(f32)
     kept = pltpu.make_async_copy(carry_v, carry, sems.at[0])
 
     def send(rows_of):
@@ -245,21 +247,23 @@
 
     @pl.when(is_ocean())
     def _():
-        forcing = flux * (1.0 / PASSES)
+        imported = import_rows(pick, weights, carry_v, 0, rows)
+        forcing = sea_f * (imported - lowest) * (1.0 / PASSES)
         carry_v[...] = forcing
         kept.start()
         send(forcing)
 
     @pl.when(jnp.logical_not(is_ocean()))
     def _():
-        kept.start()
         mix = jnp.concatenate([mixing[0], mixing[1]], axis=1)
-        bottom = (lowest + flux).astype(bf16).astype(f32)
         per = WIDTH // tile
         for c in range(x_ref.shape[1] // WIDTH):
             cols = slice(c * WIDTH, (c + 1) * WIDTH)
+            part = slice(c * per, (c + 1) * per)
             flag = flag_ref[:, cols]
-            x = with_bottom(x_ref[:, cols], flat_rows(bottom, c * per, per))
+            flux = sea_f[part] * (import_rows(pick, weights, carry_v, c * per, per) - lowest[part])
+            bottom = (lowest[part] + flux).astype(bf16).astype(f32)
+            x = with_bottom(x_ref[:, cols], flat_rows(bottom, 0, per))
             for _ in range(PHYS - 1):
                 x = substep(x, flag, mix)
             deep = x * flag
@@ -268,6 +272,7 @@
             last = 0.5 * x[0:16].astype(f32) + jnp.tanh(mixed)
             for r in range(per):
                 low_f[c * per + r : c * per + r + 1, :] = last[0:1, r * tile : (r + 1) * tile]
+        kept.start()
         send(low_f[...])
 
     kept.wait()
@@ -376,7 +381,7 @@
         picked = jnp.dot(hot[...], received[...], preferred_element_type=f32)
         pick[:, 0:tile] = picked[0:total]
         pick[:, tile : 2 * tile] = picked[total : 2 * total]
-        import_rows(pick, weights, imported, rows)
+        import_rows(pick, weights, imported, 0, rows)
         below_first = next_first()
         for start, last, pair in (
             (rows, False, (still_a, still_b)),

time: 54.9 us -> 55.2 us (level)
  no operation moved by 1% of the time
where the time goes in v7:
time: 55.2 us; the launch traced here: 54.6 us
  starting transfers between devices  34.4 us (62%)
  Pallas kernels  10.3 us (19%)
  waiting for transfers between devices  6.13 us (11%)
  local copies, waits for them, and re-layouts  2.93 us (5%)
  between operations  0.86 us (2%)
    all_to_all x1, starting transfers between devices, body(): lax.all_to_all(chosen.reshape(senders, slots, tile), ('sec', 'gx'), 0, 0,...  14.4 us
    ppermute x4, starting transfers between devices, swap(): lax.ppermute(values, ('sec', axis), pairs + [(t, s) for s, t in pairs])  11.9 us
    pallas_call x8, Pallas kernels, call(): pl.pallas_call(kernel, out_shape=shapes, in_specs=specs, out_specs=[pl.Bl...  10.3 us
    all_to_all x1, starting transfers between devices, body(): lax.all_to_all(message.reshape(senders * MESSAGE // 2, 2, tile), ('sec',...  8.09 us
    ppermute x4, waiting for transfers between devices, swap(): lax.ppermute(values, ('sec', axis), pairs + [(t, s) for s, t in pairs])  4.64 us
    unnamed x17, local copies, waits for them, and re-layouts  2.93 us
    all_to_all x1, waiting for transfers between devices, body(): lax.all_to_all(message.reshape(senders * MESSAGE // 2, 2, tile), ('sec',...  1.49 us
  transfers between devices with their start and end apart: 6, of which 3 were waited for; matrix products, arithmetic and copies ran while one was open for 5% of the time, Pallas kernels for 12%

profile of v7, /device:TPU:39, one launch (start us, length us, event | category | flops | bytes accessed | tf_op | source)
XLA Modules:
  0.0 54.6 jit_solution(9458061967257974890)
XLA Ops:
  0.6 0.0 copy-start.6
  0.6 1.7 %select_tiles.1 = (bf16[128,128]{1,0:T(8,128)(2,1)}, f32[32,128]{1,0:T(8,128)S(1)}) custom-call(bf16[1,128,32,128]{3,2,1,0:T(8,128)(2,1)} %profile.5, s32[2,64]{1,0:T(2,128)} %bitcast.53), custom_call_target="tpu_custom_call" | custom-call | bytes 1048576 | tf_op jit(solution)/shard_map/select_tiles/pallas_call | solution.py:36
  2.4 14.4 %all-to-all-start = ((bf16[64,2,128]{2,1,0:T(2,128)(2,1)}), bf16[64,2,128]{2,1,0:T(2,128)(2,1)S(1)}, u32[]{:S(2)}, u32[]{:S(2)}) async-start(bf16[64,2,128]{2,1,0:T(2,128)(2,1)} %bitcast.2), calls=%async_computation | async-start | bytes 65536 | tf_op jit(solution)/shard_map/all_to_all | solution.py:481
  16.7 0.0 copy-start
  16.8 0.0 copy-start.2
  16.8 0.0 copy-start.4
  16.8 2.1 %edge_rows.1 = (bf16[7,128,128]{2,1,0:T(8,128)(2,1)}, bf16[7,128,128]{2,1,0:T(8,128)(2,1)}, bf16[64,128]{1,0:T(8,128)(2,1)S(1)}, bf16[128,32]{1,0:T(8,128)(2,1)}) custom-call(f32[32,128]{1,0:T(8,128)} %bitcast.47, f32[32,128]{1,0:T(8,128)} %bitcast.50, s32[32,128]{1,0:T(8,128)} %bitcast.36, bf16[1,128,32,128]{3,2,1,0:T(8,128)(2,1)} %profile.5, ...), custom_call_target="tpu_custom_call" | custom-call | bytes 1048576 | tf_op jit(solution)/shard_map/edge_rows/pallas_call | solution.py:36
  18.9 4.6 %collective-permute-start = (bf16[7,128,128]{2,1,0:T(8,128)(2,1)}, bf16[7,128,128]{2,1,0:T(8,128)(2,1)S(1)}, u32[]{:S(2)}, u32[]{:S(2)}) collective-permute-start(bf16[7,128,128]{2,1,0:T(8,128)(2,1)} %get-tuple-element.27), channel_id=1, source_target_pairs={{392,400},{408,416},{424,432},{440,448},{456,464},{472,480},{488,4... | collective-permute-start | bytes 688136 | tf_op jit(solution)/shard_map/ppermute | solution.py:469
  23.5 0.0 copy-done.6
  23.5 0.0 copy-start.3
  23.5 1.7 %copy.17 = bf16[16,8,32,128]{3,1,2,0:T(8,128)(2,1)S(1)} copy(bf16[16,8,32,128]{3,2,1,0:T(8,128)(2,1)} %bitcast.43) | data formatting | bytes 2097152
  25.2 0.0 copy-start.1
  25.2 0.0 all-to-all-done
  25.2 0.0 copy-done
  25.2 0.0 copy-done.2
  25.2 0.0 copy-done.4
  25.2 1.6 %first_step.1 = (bf16[512,128]{1,0:T(8,128)(2,1)}, f32[32,128]{1,0:T(8,128)}) custom-call(bf16[128,128]{1,0:T(8,128)(2,1)S(1)} %bitcast.35, bf16[64,128]{1,0:T(8,128)(2,1)S(1)} %get-tuple-element.19.hot, bf16[64,128,128]{2,1,0:T(8,128)(2,1)S(1)} %bitcast.30, f32[32,128]{1,0:T(8,128)S(1)} %get-tuple-element.20.lowest_ref, s32[32,128]{1,0:T(8,128)S(1)} %bitcast.38, ...), custom_call_target="tpu_custom_call" | custom-call | flops 17179869184 | bytes 1048576 | tf_op jit(solution)/shard_map/first_step/pallas_call | solution.py:36
  26.8 0.0 copy-done.3
  26.8 8.1 %all-to-all-start.1 = ((bf16[256,2,128]{2,1,0:T(2,128)(2,1)}), bf16[256,2,128]{2,1,0:T(2,128)(2,1)S(1)}, u32[]{:S(2)}, u32[]{:S(2)}) async-start(bf16[256,2,128]{2,1,0:T(2,128)(2,1)} %bitcast.46), calls=%async_computation.1 | async-start | bytes 262144 | tf_op jit(solution)/shard_map/all_to_all | solution.py:527
  34.9 0.0 collective-permute-done.refs_1_.still_a
  35.0 3.1 %collective-permute-start.1 = (bf16[7,128,128]{2,1,0:T(8,128)(2,1)}, bf16[7,128,128]{2,1,0:T(8,128)(2,1)S(1)}, u32[]{:S(2)}, u32[]{:S(2)}) collective-permute-start(bf16[7,128,128]{2,1,0:T(8,128)(2,1)} %pass_edge.1), channel_id=1, source_target_pairs={{384,392},{400,408},{416,424},{432,440},{448,456},{464,472},{480,4... | collective-permute-start | bytes 688136 | tf_op jit(solution)/shard_map/ppermute | solution.py:469
  38.1 2.5 %second_step.1 = (bf16[128,4096]{1,0:T(8,128)(2,1)}, f32[5,32,128]{2,1,0:T(8,128)S(1)}, s32[32,2]{1,0:T(8,128)S(1)}) custom-call(f32[32,128]{1,0:T(8,128)} %get-tuple-element.22.carry.refs_0_, bf16[128,4096]{1,0:T(8,128)(2,1)} %bitcast.33, bf16[1,4096]{1,0:T(2,128)(2,1)} %bitcast.40, bf16[2,128,128]{2,1,0:T(8,128)(2,1)} %bitcast.41, s32[32,128]{1,0:T(8,128)} %bitcast.37, ...), custom_call_target="tpu_custom_call" | custom-call | flops 17179869184 | bytes 1048576 | tf_op jit(solution)/shard_map/second_step/pallas_call | solution.py:36
  40.5 2.0 %collective-permute-done.1.still_b = bf16[7,128,128]{2,1,0:T(8,128)(2,1)S(1)} collective-permute-done((bf16[7,128,128]{2,1,0:T(8,128)(2,1)}, bf16[7,128,128]{2,1,0:T(8,128)(2,1)S(1)}, u32[]{:S(2)}, u32[]{:S(2)}) %collective-permute-start.1) | collective-permute-done | bytes 229408 | tf_op jit(solution)/shard_map/ppermute | solution.py:469
  42.5 0.2 ready_import.1
  42.7 1.5 %all-to-all-done.1 = bf16[256,2,128]{2,1,0:T(2,128)(2,1)S(1)} async-done(((bf16[256,2,128]{2,1,0:T(2,128)(2,1)}), bf16[256,2,128]{2,1,0:T(2,128)(2,1)S(1)}, u32[]{:S(2)}, u32[]{:S(2)}) %all-to-all-start.1) | async-done | bytes 131104 | tf_op jit(solution)/shard_map/all_to_all | solution.py:527
  44.2 0.9 %second_import.1 = (f32[5,48,128]{2,1,0:T(8,128)S(1)}, f32[48,128]{1,0:T(8,128)S(1)}, f32[48,128]{1,0:T(8,128)S(1)}) custom-call(bf16[512,128]{1,0:T(8,128)(2,1)S(1)} %bitcast.34, bf16[64,128,128]{2,1,0:T(8,128)(2,1)S(1)} %bitcast.31, bf16[112,512]{1,0:T(8,128)(2,1)S(1)} %get-tuple-element.29.hot, f32[5,48,128]{2,1,0:T(8,128)S(1)} %get-tuple-element.30.planes, ...), custom_call_target="tpu_custom_call" | custom-call | bytes 1048576 | tf_op jit(solution)/shard_map/second_import/pallas_call | solution.py:36
  45.1 2.3 %collective-permute-start.2 = (f32[48,128]{1,0:T(8,128)S(1)}, f32[48,128]{1,0:T(8,128)S(1)}, u32[]{:S(2)}, u32[]{:S(2)}) collective-permute-start(f32[48,128]{1,0:T(8,128)S(1)} %get-tuple-element.32), channel_id=1, source_target_pairs={{384,385},{386,387},{388,389},{390,391},{385,384},{387,386},{389,3... | collective-permute-start | bytes 73736 | tf_op jit(solution)/shard_map/ppermute | solution.py:469
  47.5 1.9 %collective-permute-start.3 = (f32[48,128]{1,0:T(8,128)S(1)}, f32[48,128]{1,0:T(8,128)S(1)}, u32[]{:S(2)}, u32[]{:S(2)}) collective-permute-start(f32[48,128]{1,0:T(8,128)S(1)} %get-tuple-element.33), channel_id=1, source_target_pairs={{385,386},{387,388},{389,390},{386,385},{388,387},{390,389},{393,3... | collective-permute-start | bytes 73736 | tf_op jit(solution)/shard_map/ppermute | solution.py:469
  49.4 1.2 %copy.14 = bf16[16,8,32,128]{3,2,1,0:T(8,128)(2,1)} copy(bf16[16,8,32,128]{3,1,2,0:T(8,128)(2,1)S(1)} %bitcast.44) | data formatting | bytes 2097152
  50.6 0.0 collective-permute-done.2.from_a
  50.6 2.6 %collective-permute-done.3.from_b = f32[48,128]{1,0:T(8,128)S(1)} collective-permute-done((f32[48,128]{1,0:T(8,128)S(1)}, f32[48,128]{1,0:T(8,128)S(1)}, u32[]{:S(2)}, u32[]{:S(2)}) %collective-permute-start.3) | collective-permute-done | bytes 24608 | tf_op jit(solution)/shard_map/ppermute | solution.py:469
  53.3 1.4 %passes.1 = f32[32,128]{1,0:T(8,128)} custom-call(f32[5,48,128]{2,1,0:T(8,128)S(1)} %get-tuple-element.31.wide, f32[48,128]{1,0:T(8,128)S(1)} %collective-permute-done.2.from_a, f32[48,128]{1,0:T(8,128)S(1)} %collective-permute-done.3.from_b, f32[32,128]{1,0:T(8,128)} %bitcast.49), custom_call_target="tpu_custom_call" | custom-call | bytes 1048576 | tf_op jit(solution)/shard_map/passes/pallas_call | solution.py:36
  (6 shorter events, 0.0 us)
Async XLA Ops:
  0.6 22.8 %copy-start.6 = (s32[1,32,128]{2,1,0:T(8,128)S(1)}, s32[1,32,128]{2,1,0:T(8,128)}, u32[]{:S(2)}) copy-start(s32[1,32,128]{2,1,0:T(8,128)} %param.13) | copy-start | bytes 49156
  2.4 22.8 %all-to-all-start = ((bf16[64,2,128]{2,1,0:T(2,128)(2,1)}), bf16[64,2,128]{2,1,0:T(2,128)(2,1)S(1)}, u32[]{:S(2)}, u32[]{:S(2)}) async-start(bf16[64,2,128]{2,1,0:T(2,128)(2,1)} %bitcast.2), calls=%async_computation | async-start | bytes 65536 | tf_op jit(solution)/shard_map/all_to_all | solution.py:481
  16.7 8.5 %copy-start = (bf16[1,1,1,32,2,128,128]{6,5,4,3,2,1,0:T(8,128)(2,1)S(1)}, bf16[1,1,1,32,2,128,128]{6,5,4,3,2,1,0:T(8,128)(2,1)}, u32[]{:S(2)}) copy-start(bf16[1,1,1,32,2,128,128]{6,5,4,3,2,1,0:T(8,128)(2,1)} %param.15) | copy-start | bytes 6291460
  16.8 8.5 %copy-start.2 = (s32[1,32,128]{2,1,0:T(8,128)S(1)}, s32[1,32,128]{2,1,0:T(8,128)}, u32[]{:S(2)}) copy-start(s32[1,32,128]{2,1,0:T(8,128)} %param.12) | copy-start | bytes 49156
  16.8 8.5 %copy-start.4 = (bf16[1,2,128,128]{3,2,1,0:T(8,128)(2,1)S(1)}, bf16[1,2,128,128]{3,2,1,0:T(8,128)(2,1)}, u32[]{:S(2)}) copy-start(bf16[1,2,128,128]{3,2,1,0:T(8,128)(2,1)} %param.14) | copy-start | bytes 196612
  18.9 16.1 %collective-permute-start = (bf16[7,128,128]{2,1,0:T(8,128)(2,1)}, bf16[7,128,128]{2,1,0:T(8,128)(2,1)S(1)}, u32[]{:S(2)}, u32[]{:S(2)}) collective-permute-start(bf16[7,128,128]{2,1,0:T(8,128)(2,1)} %get-tuple-element.27), channel_id=1, source_target_pairs={{392,400},{408,416},{424,432},{440,448},{456,464},{472,480},{488,4... | collective-permute-start | bytes 688136 | tf_op jit(solution)/shard_map/ppermute | solution.py:469
  23.5 3.3 %copy-start.3 = (bf16[1,1,32,128]{3,1,2,0:T(2,128)(2,1)}, bf16[1,1,32,128]{3,1,2,0:T(2,128)(2,1)S(1)}, u32[]{:S(2)}) copy-start(bf16[1,1,32,128]{3,1,2,0:T(2,128)(2,1)S(1)} %copy.18) | copy-start | bytes 24580
  25.2 1.6 %copy-start.1 = (bf16[16,8,32,128]{3,1,2,0:T(8,128)(2,1)}, bf16[16,8,32,128]{3,1,2,0:T(8,128)(2,1)S(1)}, u32[]{:S(2)}) copy-start(bf16[16,8,32,128]{3,1,2,0:T(8,128)(2,1)S(1)} %copy.17) | copy-start | bytes 3145732
  26.8 17.4 %all-to-all-start.1 = ((bf16[256,2,128]{2,1,0:T(2,128)(2,1)}), bf16[256,2,128]{2,1,0:T(2,128)(2,1)S(1)}, u32[]{:S(2)}, u32[]{:S(2)}) async-start(bf16[256,2,128]{2,1,0:T(2,128)(2,1)} %bitcast.46), calls=%async_computation.1 | async-start | bytes 262144 | tf_op jit(solution)/shard_map/all_to_all | solution.py:527
  35.0 7.6 %collective-permute-start.1 = (bf16[7,128,128]{2,1,0:T(8,128)(2,1)}, bf16[7,128,128]{2,1,0:T(8,128)(2,1)S(1)}, u32[]{:S(2)}, u32[]{:S(2)}) collective-permute-start(bf16[7,128,128]{2,1,0:T(8,128)(2,1)} %pass_edge.1), channel_id=1, source_target_pairs={{384,392},{400,408},{416,424},{432,440},{448,456},{464,472},{480,4... | collective-permute-start | bytes 688136 | tf_op jit(solution)/shard_map/ppermute | solution.py:469
  44.2 5.2 %copy-start.5 = (bf16[128,4096]{1,0:T(8,128)(2,1)S(1)}, bf16[128,4096]{1,0:T(8,128)(2,1)}, u32[]{:S(2)}) copy-start(bf16[128,4096]{1,0:T(8,128)(2,1)} %get-tuple-element.23) | copy-start | bytes 3145732
  45.1 5.5 %collective-permute-start.2 = (f32[48,128]{1,0:T(8,128)S(1)}, f32[48,128]{1,0:T(8,128)S(1)}, u32[]{:S(2)}, u32[]{:S(2)}) collective-permute-start(f32[48,128]{1,0:T(8,128)S(1)} %get-tuple-element.32), channel_id=1, source_target_pairs={{384,385},{386,387},{388,389},{390,391},{385,384},{387,386},{389,3... | collective-permute-start | bytes 73736 | tf_op jit(solution)/shard_map/ppermute | solution.py:469
  47.5 5.8 %collective-permute-start.3 = (f32[48,128]{1,0:T(8,128)S(1)}, f32[48,128]{1,0:T(8,128)S(1)}, u32[]{:S(2)}, u32[]{:S(2)}) collective-permute-start(f32[48,128]{1,0:T(8,128)S(1)} %get-tuple-element.33), channel_id=1, source_target_pairs={{385,386},{387,388},{389,390},{386,385},{388,387},{390,389},{393,3... | collective-permute-start | bytes 73736 | tf_op jit(solution)/shard_map/ppermute | solution.py:469
